TPU v7x, 32 devices: a whole 2x2x4 slice. The times are simulated.
32 devices in a mesh: dp: 8 (over y, x, core), tensor: 4 (over z).
Axes of the slice: x: 2, y: 2, z: 4, core: 2. Of those that a mesh axis runs over, the one named last changes fastest.
Arguments:
- tokens: bfloat16 [8192, 768], P('dp'), may hold values from -6 to 6
- type_table: float32 [2, 768], replicated, may hold values from -3 to 3
- norm_gain: float32 [2, 2, 768], replicated, may hold values from 0.5 to 1.5
- norm_bias: float32 [2, 2, 768], replicated, may hold values from -1.8 to 1.8
- w_qkv: bfloat16 [2, 768, 3, 768], P(None, None, None, 'tensor'), may hold values from -0.21875 to 0.21875
- w_out: bfloat16 [2, 768, 768], P(None, 'tensor'), may hold values from -0.625 to 0.625
- w_up: bfloat16 [2, 768, 3072], P(None, None, 'tensor'), may hold values from -0.21875 to 0.21875
- w_down: bfloat16 [2, 3072, 768], P(None, 'tensor'), may hold values from -0.109375 to 0.109375
- cotangent: bfloat16 [32, 12, 768], P('dp'), may hold values from -6 to 6
- positions: int32 [32, 12], P('dp'), may hold values from -1 to 39, as said below
Outputs:
- hidden_out: float32 [8192, 768], P('dp')
- grad_tokens: float32 [8192, 768], P('dp')
- grad_type: float32 [2, 768], P(None, 'dp')
- grad_gain: float32 [2, 2, 768], P(None, None, 'dp')
- grad_bias: float32 [2, 2, 768], P(None, None, 'dp')
- grad_qkv: float32 [2, 768, 3, 768], P(None, 'dp', None, 'tensor')
- grad_out: float32 [2, 768, 768], P(None, 'tensor', 'dp')
- grad_up: float32 [2, 768, 3072], P(None, 'dp', 'tensor')
- grad_down: float32 [2, 3072, 768], P(None, 'tensor', 'dp')
Inputs may be any that keep to these rules, and one draw needn't show every extreme that they name: `positions`: each pair has between 1 and 12 masked words in its first slots, at distinct rows below 40; the slots after them hold -1; in every draw some pair has all 12 slots used.
All inputs are finite; a program needn't handle non-finite values.
Results may differ from a plain program's by a relative error of at most 0.03.
Values may be sent and summed in bfloat16 or wider, within the bound.
No kernel may reach another device: no remote copies, remote signals or barrier semaphores. Data moves between devices by JAX's collectives and lax.ppermute only.
A program may use at most 128 MiB of HBM per device.

v0:
```python
import functools

import jax
import jax.numpy as jnp
from jax import lax
from jax.experimental import pallas as pl
from jax.experimental.pallas import tpu as pltpu
from jax.sharding import PartitionSpec as P

HD = 64
WORDS = 40
TOP_ROWS = 48
SLOT_ROWS = 16
EPSILON = 1e-06
ROOT_HALF = 0.7071067811865476
ROOT_TWO_PI = 2.5066282746310002
GROUP = 8
STEP = 32
F32 = jnp.float32
BF16 = jnp.bfloat16
VMEM_BYTES = 48 * 1024 * 1024


def dot(left, right, dims):
    return lax.dot_general(left, right, (dims, ((), ())), preferred_element_type=F32)


def nn(left, right):
    return dot(left, right, ((1,), (0,)))


def nt(left, right):
    return dot(left, right, ((1,), (1,)))


def tn(left, right):
    return dot(left, right, ((0,), (0,)))


def gelu(values):
    return 0.5 * values * (1.0 + lax.erf(values * ROOT_HALF))


def gelu_slope(values):
    return 0.5 * (1.0 + lax.erf(values * ROOT_HALF)) + values * jnp.exp(-0.5 * values * values) / ROOT_TWO_PI


def norm_parts(values):
    average = jnp.mean(values, axis=-1, keepdims=True)
    centred = values - average
    spread = jnp.mean(centred * centred, axis=-1, keepdims=True)
    rate = lax.rsqrt(spread + EPSILON)
    return centred * rate, rate


def norm_rows(source, gain, bias, target):
    for r in range(0, source.shape[0], STEP):
        rows = slice(r, r + STEP)
        target[rows, :] = (norm_parts(source[rows, :])[0] * gain[...] + bias[...]).astype(BF16)


def norm_back_rows(rows, values, gain, incoming, gain_grad, bias_grad):
    unit, rate = norm_parts(values[rows, :])
    e = incoming[rows, :]
    scaled = e * gain[...]
    inner = jnp.mean(scaled * unit, axis=-1, keepdims=True)
    gain_grad[...] += jnp.sum(e * unit, axis=0, keepdims=True)
    bias_grad[...] += jnp.sum(e, axis=0, keepdims=True)
    return rate * (scaled - jnp.mean(scaled, axis=-1, keepdims=True) - unit * inner)


def fetch(spot, own, pieces, scratches, sems):
    count = len(scratches)
    rows = scratches[0].shape[1] // GROUP
    for source, scratch in zip(own, scratches):
        pltpu.make_async_copy(source, scratch.at[0], sems.at[0]).start()
    for k, pair in enumerate(pieces, 1):
        for c, source in enumerate(pair):
            for i in range(GROUP // 2):
                at = pl.multiple_of((spot ^ (2 * i + c)) * rows, rows)
                for m, scratch in enumerate(scratches):
                    pltpu.make_async_copy(
                        source.at[pl.ds((i * count + m) * rows, rows)],
                        scratch.at[k, pl.ds(at, rows)],
                        sems.at[k],
                    ).start()


def arrived(k, scratches, sems):
    for scratch in scratches:
        pltpu.make_async_copy(scratch.at[k], scratch.at[k], sems.at[k]).wait()


def flip(spot, source, target):
    width = source.shape[1]
    rows = width // GROUP
    turned = source.astype(F32).T.astype(BF16)
    for j in range(GROUP):
        s = spot ^ j
        at = pl.multiple_of(((s & 1) * (GROUP // 2) + (s >> 1)) * rows, rows)
        target[pl.ds(at, rows), :] = turned[j * rows : (j + 1) * rows, :]


def put_block(block, keep, send, columns=slice(None)):
    half = block.shape[0] // 2
    rows = half // (GROUP // 2)
    for i in range(GROUP // 2):
        keep[i, 0, :, columns] = block[i * rows : (i + 1) * rows].astype(BF16)
        send[i, 0, :, columns] = block[half + i * rows : half + (i + 1) * rows].astype(BF16)


def any_spec():
    return pl.BlockSpec(memory_space=pl.ANY)


def smem_spec():
    return pl.BlockSpec(memory_space=pltpu.SMEM)


def whole(shape):
    return pl.BlockSpec(shape, lambda k: (0,) * len(shape))


def per_quarter(shape):
    return pl.BlockSpec((1,) + shape, lambda k: (k,) + (0,) * len(shape))


def block_specs(rows, width):
    return [pl.BlockSpec((GROUP // 2, 1, rows, width), lambda k: (0, k, 0, 0))] * 2


def params():
    return pltpu.CompilerParams(vmem_limit_bytes=VMEM_BYTES, dimension_semantics=("arbitrary",))


def cost(flops, moved):
    return pl.CostEstimate(flops=flops, bytes_accessed=moved, transcendentals=0)


def attention_forward_kernel(spot_ref, x, gain, bias, own, *rest):
    n = len(rest) - 5 - 2
    pieces = [(rest[2 * i], rest[2 * i + 1]) for i in range(n // 2)]
    middle, normed, proj, logsum, mixed, block, sems = rest[n:]
    k = pl.program_id(0)
    inner = mixed.shape[-1]
    heads = inner // HD

    @pl.when(k == 0)
    def _():
        fetch(spot_ref[0], [own], pieces, [block], sems)
        norm_rows(x, gain, bias, normed)
        middle[...] = x[...]
        logsum[...] = jnp.zeros_like(logsum)

    arrived(k, [block], sems)
    proj[0] = nn(normed[...], block[k, :, : 3 * inner]).astype(BF16)
    lane = lax.broadcasted_iota(jnp.int32, logsum.shape, 1)
    for h in range(heads):
        own_lanes = slice(h * HD, (h + 1) * HD)
        queries = proj[0, :, own_lanes] * jnp.asarray(HD**-0.5, BF16)
        keys = proj[0, :, inner + h * HD : inner + (h + 1) * HD]
        values = proj[0, :, 2 * inner + h * HD : 2 * inner + (h + 1) * HD]
        scores = nt(queries, keys)
        top = jnp.max(scores, axis=-1, keepdims=True)
        powers = jnp.exp(scores - top)
        total = jnp.sum(powers, axis=-1, keepdims=True)
        logsum[...] = jnp.where(lane == k * heads + h, top + jnp.log(total), logsum[...])
        weights = (powers * (1.0 / total)).astype(BF16)
        mixed[0, :, own_lanes] = nn(weights, values).astype(BF16)
    middle[...] += nt(mixed[0], block[k, :, 3 * inner :]).astype(BF16).astype(F32)


def attention_forward(spot, x, gain, bias, own, pieces):
    length, width = x.shape
    n_t = len(pieces) + 1
    inner = own.shape[1] // 4
    flat = [v for pair in pieces for v in pair]
    out = [
        jax.ShapeDtypeStruct((length, width), F32),
        jax.ShapeDtypeStruct((length, width), BF16),
        jax.ShapeDtypeStruct((n_t, length, 3 * inner), BF16),
        jax.ShapeDtypeStruct((length, 128), F32),
        jax.ShapeDtypeStruct((n_t, length, inner), BF16),
    ]
    return pl.pallas_call(
        attention_forward_kernel,
        grid=(n_t,),
        out_shape=out,
        in_specs=[smem_spec(), whole((length, width)), whole((1, width)), whole((1, width))] + [any_spec()] * (1 + len(flat)),
        out_specs=[
            whole((length, width)),
            whole((length, width)),
            per_quarter((length, 3 * inner)),
            whole((length, 128)),
            per_quarter((length, inner)),
        ],
        scratch_shapes=[pltpu.VMEM((n_t,) + own.shape, BF16), pltpu.SemaphoreType.DMA((n_t,))],
        compiler_params=params(),
        cost_estimate=cost(4_000_000_000, 10_000_000),
        name="attention_forward",
    )(spot, x, gain, bias, own, *flat)


def mlp_forward_kernel(kept_rows, top, spot_ref, x, gain, bias, own_up, own_down, *rest):
    n = len(rest) - 3 - 4
    pieces = [(rest[2 * i], rest[2 * i + 1]) for i in range(n // 2)]
    out, normed, upward, ups, downs, total, sems = rest[n:]
    k = pl.program_id(0)

    @pl.when(k == 0)
    def _():
        fetch(spot_ref[0], [own_up, own_down], pieces, [ups, downs], sems)
        norm_rows(x, gain, bias, normed)
        total[...] = x[...]

    arrived(k, [ups, downs], sems)
    up = nn(normed[...], ups[k])
    upward[0] = up[:kept_rows]
    active = gelu(up).astype(BF16)
    total[...] += nn(active, downs[k]).astype(BF16).astype(F32)

    @pl.when(k == pl.num_programs(0) - 1)
    def _():
        out[...] = total[...].astype(out.dtype)


def mlp_forward(spot, x, gain, bias, own_up, own_down, pieces, kept_rows, top):
    length, width = x.shape
    n_t = len(pieces) + 1
    hidden = own_up.shape[1]
    flat = [v for pair in pieces for v in pair]
    out_type = BF16 if top else F32
    out = [
        jax.ShapeDtypeStruct((length, width), out_type),
        jax.ShapeDtypeStruct((length, width), BF16),
        jax.ShapeDtypeStruct((n_t, kept_rows, hidden), F32),
    ]
    return pl.pallas_call(
        functools.partial(mlp_forward_kernel, kept_rows, top),
        grid=(n_t,),
        out_shape=out,
        in_specs=[smem_spec(), whole((length, width)), whole((1, width)), whole((1, width))] + [any_spec()] * (2 + len(flat)),
        out_specs=[whole((length, width)), whole((length, width)), per_quarter((kept_rows, hidden))],
        scratch_shapes=[
            pltpu.VMEM((n_t,) + own_up.shape, BF16),
            pltpu.VMEM((n_t,) + own_down.shape, BF16),
            pltpu.VMEM((length, width), F32),
            pltpu.SemaphoreType.DMA((n_t,)),
        ],
        compiler_params=params(),
        cost_estimate=cost(4_000_000_000, 10_000_000),
        name="mlp_forward",
    )(spot, x, gain, bias, own_up, own_down, *flat)


def mlp_backward_kernel(blocks, spot_ref, incoming, x, gain, normed, upward, own_up, own_down, *rest):
    outs = 3 + (4 if blocks else 0)
    scr = 6 if blocks else 4
    n = len(rest) - outs - scr
    pieces = [(rest[2 * i], rest[2 * i + 1]) for i in range(n // 2)]
    grad, gain_grad, bias_grad = rest[n : n + 3]
    ups, downs, total, sems = rest[n + outs : n + outs + 4]
    k = pl.program_id(0)

    @pl.when(k == 0)
    def _():
        fetch(spot_ref[0], [own_up, own_down], pieces, [ups, downs], sems)
        total[...] = jnp.zeros_like(total)
        if blocks:
            low_t, normed_t = rest[-2:]
            flip(spot_ref[0], incoming[...], low_t)
            flip(spot_ref[0], normed[...], normed_t)

    arrived(k, [ups, downs], sems)
    up = upward[0]
    grad_active = nt(incoming[...].astype(BF16), downs[k])
    bell = 0.5 * (1.0 + lax.erf(up * ROOT_HALF))
    grad_up = (grad_active * (bell + up * jnp.exp(-0.5 * up * up) * (1.0 / ROOT_TWO_PI))).astype(BF16)
    total[...] += nt(grad_up, ups[k])
    if blocks:
        down_keep, down_send, up_keep, up_send = rest[n + 3 : n + 7]
        put_block(nn(low_t_of(rest)[...], (up * bell).astype(BF16)), down_keep, down_send)
        put_block(nn(rest[-1][...], grad_up), up_keep, up_send)

    @pl.when(k == pl.num_programs(0) - 1)
    def _():
        gain_grad[...] = jnp.zeros_like(gain_grad)
        bias_grad[...] = jnp.zeros_like(bias_grad)
        size = min(STEP, 16) if x.shape[0] % STEP else STEP
        for r in range(0, x.shape[0], size):
            rows = slice(r, r + size)
            grad[rows, :] = incoming[rows, :] + norm_back_rows(rows, x, gain, total, gain_grad, bias_grad)


def low_t_of(rest):
    return rest[-2]


def mlp_backward(spot, incoming, x, gain, normed, upward, own_up, own_down, pieces, blocks):
    length, width = incoming.shape
    n_t = len(pieces) + 1
    hidden = own_up.shape[1]
    flat = [v for pair in pieces for v in pair]
    out = [
        jax.ShapeDtypeStruct((length, width), F32),
        jax.ShapeDtypeStruct((1, width), F32),
        jax.ShapeDtypeStruct((1, width), F32),
    ]
    out_specs = [whole((length, width)), whole((1, width)), whole((1, width))]
    scratch = [
        pltpu.VMEM((n_t,) + own_up.shape, BF16),
        pltpu.VMEM((n_t,) + own_down.shape, BF16),
        pltpu.VMEM((length, width), F32),
        pltpu.SemaphoreType.DMA((n_t,)),
    ]
    if blocks:
        out += [jax.ShapeDtypeStruct((GROUP // 2, n_t, width // GROUP, hidden), BF16)] * 4
        out_specs += block_specs(width // GROUP, hidden) * 2
        scratch += [pltpu.VMEM((width, length), BF16)] * 2
    return pl.pallas_call(
        functools.partial(mlp_backward_kernel, blocks),
        grid=(n_t,),
        out_shape=out,
        in_specs=[
            smem_spec(),
            whole((length, width)),
            whole((length, width)),
            whole((1, width)),
            whole((length, width)),
            per_quarter((length, hidden)),
        ]
        + [any_spec()] * (2 + len(flat)),
        out_specs=out_specs,
        scratch_shapes=scratch,
        compiler_params=params(),
        cost_estimate=cost(6_000_000_000, 20_000_000),
        name="mlp_backward",
    )(spot, incoming, x, gain, normed, upward, own_up, own_down, *flat)


def attention_backward_kernel(spot_ref, incoming, x, gain, normed, proj, logsum, mixed, own, *rest):
    n = len(rest) - 5 - 6
    pieces = [(rest[2 * i], rest[2 * i + 1]) for i in range(n // 2)]
    grad, gain_grad, bias_grad, keep, send, block, total, grad_proj, sems, low_t, normed_t = rest[n:]
    k = pl.program_id(0)
    top = incoming.shape[0]
    inner = mixed.shape[-1]
    heads = inner // HD

    @pl.when(k == 0)
    def _():
        fetch(spot_ref[0], [own], pieces, [block], sems)
        total[...] = jnp.zeros_like(total)
        grad_proj[...] = jnp.zeros_like(grad_proj)
        flip(spot_ref[0], incoming[...], low_t)
        flip(spot_ref[0], normed[...], normed_t)

    arrived(k, [block], sems)
    grad_mixed = nn(incoming[...].astype(BF16), block[k, :, 3 * inner :]).astype(BF16)
    lane = lax.broadcasted_iota(jnp.int32, (top, 128), 1)
    for h in range(heads):
        own_lanes = slice(h * HD, (h + 1) * HD)
        key_lanes = slice(inner + h * HD, inner + (h + 1) * HD)
        value_lanes = slice(2 * inner + h * HD, 2 * inner + (h + 1) * HD)
        queries = proj[0, :top, own_lanes] * jnp.asarray(HD**-0.5, BF16)
        keys = proj[0, :, key_lanes]
        values = proj[0, :, value_lanes]
        head_grad = grad_mixed[:, own_lanes]
        row_sum = jnp.sum(jnp.where(lane == k * heads + h, logsum[:top, :], 0.0), axis=-1, keepdims=True)
        weights = jnp.exp(nt(queries, keys) - row_sum)
        grad_weights = nt(head_grad, values)
        inner_sum = jnp.sum(weights * grad_weights, axis=-1, keepdims=True)
        grad_scores = (weights * (grad_weights - inner_sum)).astype(BF16)
        grad_proj[:top, own_lanes] = (nn(grad_scores, keys) * HD**-0.5).astype(BF16)
        grad_proj[:, key_lanes] = tn(grad_scores, queries).astype(BF16)
        grad_proj[:, value_lanes] = tn(weights.astype(BF16), head_grad).astype(BF16)
    total[...] += nt(grad_proj[...], block[k, :, : 3 * inner])
    put_block(nn(normed_t[...], grad_proj[...]), keep, send, slice(0, 3 * inner))
    put_block(nn(low_t[...], mixed[0, :top, :]), keep, send, slice(3 * inner, 4 * inner))

    @pl.when(k == pl.num_programs(0) - 1)
    def _():
        gain_grad[...] = jnp.zeros_like(gain_grad)
        bias_grad[...] = jnp.zeros_like(bias_grad)
        for r in range(0, x.shape[0], 16):
            rows = slice(r, r + 16)
            back = norm_back_rows(rows, x, gain, total, gain_grad, bias_grad)
            grad[rows, :] = back + incoming[rows, :] if r < top else back


def attention_backward(spot, incoming, x, gain, normed, proj, logsum, mixed, own, pieces):
    length, width = x.shape
    top = incoming.shape[0]
    n_t = len(pieces) + 1
    inner = own.shape[1] // 4
    flat = [v for pair in pieces for v in pair]
    out = [
        jax.ShapeDtypeStruct((length, width), F32),
        jax.ShapeDtypeStruct((1, width), F32),
        jax.ShapeDtypeStruct((1, width), F32),
    ] + [jax.ShapeDtypeStruct((GROUP // 2, n_t, width // GROUP, 4 * inner), BF16)] * 2
    return pl.pallas_call(
        attention_backward_kernel,
        grid=(n_t,),
        out_shape=out,
        in_specs=[
            smem_spec(),
            whole((top, width)),
            whole((length, width)),
            whole((1, width)),
            whole((length, width)),
            per_quarter((length, 3 * inner)),
            whole((length, 128)),
            per_quarter((length, inner)),
        ]
        + [any_spec()] * (1 + len(flat)),
        out_specs=[whole((length, width)), whole((1, width)), whole((1, width))] + block_specs(width // GROUP, 4 * inner),
        scratch_shapes=[
            pltpu.VMEM((n_t,) + own.shape, BF16),
            pltpu.VMEM((length, width), F32),
            pltpu.VMEM((length, 3 * inner), BF16),
            pltpu.SemaphoreType.DMA((n_t,)),
            pltpu.VMEM((width, top), BF16),
            pltpu.VMEM((width, length), BF16),
        ],
        compiler_params=params(),
        cost_estimate=cost(6_000_000_000, 20_000_000),
        name="attention_backward",
    )(spot, incoming, x, gain, normed, proj, logsum, mixed, own, *flat)


def swap(values, bit, size):
    return lax.ppermute(values, "dp", [(i, i ^ bit) for i in range(size)])


def shift(values, size):
    return lax.ppermute(values, "tensor", [(i, (i + 1) % size) for i in range(size)])


def pack_kernel(*refs):
    *sources, target, sems = refs
    at = 0
    copies = []
    for i, source in enumerate(sources):
        rows = source.shape[0]
        copies.append(pltpu.make_async_copy(source, target.at[pl.ds(at, rows)], sems.at[i]))
        at += rows
    for copy in copies:
        copy.start()
    for copy in copies:
        copy.wait()


def pack(sources):
    rows = sum(s.shape[0] for s in sources)
    width = sources[0].shape[1]
    return pl.pallas_call(
        pack_kernel,
        out_shape=jax.ShapeDtypeStruct((rows, width), BF16),
        in_specs=[any_spec()] * len(sources),
        out_specs=any_spec(),
        scratch_shapes=[pltpu.SemaphoreType.DMA((len(sources),))],
        cost_estimate=cost(0, 4 * rows * width),
        name="pack",
    )(*sources)


def gather_blocks(part, n_dp, n_t):
    half = part.shape[0] // 2
    quarters = []
    held = part
    for _ in range(n_t - 1):
        held = shift(held, n_t)
        along_x = swap(held, 2, n_dp)
        along_y = swap(held, 4, n_dp)
        corner_a = swap(along_x[:half], 4, n_dp)
        corner_b = swap(along_y[half:], 2, n_dp)
        plane = pack([held, along_x, along_y, corner_a, corner_b])
        quarters.append((plane, swap(plane, 1, n_dp)))
    return quarters


def reduce_blocks(keep, send, n_dp, n_t):
    half = n_t // 2
    got = swap(send, 1, n_dp)

    def both(i, k=slice(None)):
        return keep[i, k].astype(F32) + got[i, k].astype(F32)

    low, high = slice(0, half), slice(half, None)
    corner_a = swap(both(3, low).astype(BF16), 2, n_dp)
    corner_b = swap(both(3, high).astype(BF16), 4, n_dp)
    x_low = swap(both(1, low).astype(BF16), 2, n_dp)
    x_high = swap((both(1, high) + corner_b.astype(F32)).astype(BF16), 2, n_dp)
    y_low = swap((both(2, low) + corner_a.astype(F32)).astype(BF16), 4, n_dp)
    y_high = swap(both(2, high).astype(BF16), 4, n_dp)

    def mine(k):
        x, y = (x_low, y_low) if k < half else (x_high, y_high)
        return both(0, k) + x[k % half].astype(F32) + y[k % half].astype(F32)

    total = mine(1)
    for k in range(2, n_t):
        total = shift(total.astype(BF16), n_t).astype(F32) + mine(k)
    total = shift(total.astype(BF16), n_t).astype(F32) + mine(0)
    groups = n_dp // GROUP
    me = lax.axis_index("dp")
    rows = total.shape[0]
    bit = n_dp // 2
    while bit >= GROUP:
        rows //= 2
        mine_first = (me // bit) % 2
        kept = lax.dynamic_slice_in_dim(total, mine_first * rows, rows, 0)
        sent = lax.dynamic_slice_in_dim(total, (1 - mine_first) * rows, rows, 0)
        total = kept + swap(sent, bit, n_dp)
        bit //= 2
    if groups > 1:
        total = lax.ppermute(
            total, "dp", [(h * GROUP + s, s * groups + h) for h in range(groups) for s in range(GROUP)]
        )
    return total


def sum_all(values, n_dp, n_t):
    bit = 1
    while bit < n_dp:
        values = values + swap(values, bit, n_dp)
        bit *= 2
    bit = 1
    while bit < n_t:
        values = values + lax.ppermute(values, "tensor", [(i, i ^ bit) for i in range(n_t)])
        bit *= 2
    return values


def gather_rows(values, n_dp, n_t):
    held = [values[None]]
    for _ in range(n_t - 1):
        held.append(shift(held[-1], n_t))
    out = jnp.concatenate(held, 0)
    bit = 2
    while bit < n_dp:
        out = jnp.concatenate([out, swap(out, bit, n_dp)], 0)
        bit *= 2
    return jnp.concatenate([out, swap(out, 1, n_dp)], 0)


def shards(tokens, type_table, norm_gain, norm_bias, w_qkv, w_out, w_up, w_down, cotangent, positions, n_dp, n_t):
    total_rows, width = tokens.shape
    pair_count, slots = positions.shape
    assert pair_count == n_t
    length = total_rows // pair_count
    layers = w_qkv.shape[0]
    top = layers - 1
    inner = w_qkv.shape[3]
    me, quarter = lax.axis_index("dp"), lax.axis_index("tensor")
    rows = width // GROUP
    unit = width // n_dp
    spot = me % GROUP
    spots = jnp.reshape(spot, (1,)).astype(jnp.int32)

    def part_of(block):
        return lax.dynamic_slice_in_dim(block, spot * rows, rows, 0)

    own, attn_pieces, mlp_pieces = [], [], []
    for l in range(layers):
        own.append(jnp.concatenate([w_qkv[l].reshape(width, 3 * inner), w_out[l].T], 1))
        attn_pieces.append(gather_blocks(part_of(own[l]), n_dp, n_t))
        mlp_pieces.append(
            gather_blocks(jnp.concatenate([part_of(w_up[l]), part_of(w_down[l])], 0), n_dp, n_t)
        )

    mine = lax.dynamic_slice_in_dim(tokens, quarter * length, length, 0).astype(F32)
    row_ids = lax.broadcasted_iota(jnp.int32, (length, 1), 0)
    stream = mine + jnp.where(row_ids < WORDS, type_table[0], type_table[1])
    gains = [[norm_gain[l, i][None] for i in range(2)] for l in range(layers)]
    biases = [[norm_bias[l, i][None] for i in range(2)] for l in range(layers)]
    saved = []
    for l in range(layers):
        middle, normed, proj, logsum, mixed = attention_forward(
            spots, stream, gains[l][0], biases[l][0], own[l], attn_pieces[l]
        )
        following, normed_mlp, upward = mlp_forward(
            spots, middle, gains[l][1], biases[l][1], w_up[l], w_down[l], mlp_pieces[l],
            TOP_ROWS if l == top else length, l == top,
        )
        saved.append((stream, normed, proj, logsum, mixed, middle, normed_mlp, upward))
        stream = following

    def whole_pairs(values):
        held = values.astype(BF16)
        out = jnp.zeros((total_rows, width), F32)
        for k in range(n_t):
            out = lax.dynamic_update_slice(out, held.astype(F32), (((quarter - k) % n_t) * length, 0))
            if k < n_t - 1:
                held = shift(held, n_t)
        return out

    hidden_out = whole_pairs(stream)

    place = lax.dynamic_slice_in_dim(positions, quarter, 1, 0)[0]
    cot = lax.dynamic_slice_in_dim(cotangent, quarter, 1, 0)[0]
    onehot = (row_ids[:TOP_ROWS] == place[None, :]).astype(BF16)
    incoming = nn(onehot, cot)

    top_normed = saved[top][6][:TOP_ROWS]
    slot_rows = tn(onehot, top_normed).astype(BF16)
    slot_cot = jnp.where(place[:, None] >= 0, cot, 0)
    spare = jnp.zeros((SLOT_ROWS - slots, width), BF16)
    all_rows = gather_rows(jnp.concatenate([slot_cot, spare, slot_rows, spare], 0), n_dp, n_t)
    all_cot = all_rows[:, :SLOT_ROWS].reshape(-1, width)
    all_normed = all_rows[:, SLOT_ROWS:].reshape(-1, width)
    slot_up = nn(all_normed, w_up[top])
    slot_grad = (nt(all_cot, w_down[top]) * gelu_slope(slot_up)).astype(BF16)
    grad_up_top = tn(lax.dynamic_slice_in_dim(all_normed, me * unit, unit, 1), slot_grad)
    grad_down_top = tn(
        gelu(slot_up).astype(BF16), lax.dynamic_slice_in_dim(all_cot, me * unit, unit, 1)
    )

    sums = {}
    gain_grads = [[None, None] for _ in range(layers)]
    bias_grads = [[None, None] for _ in range(layers)]
    for l in range(top, -1, -1):
        stream_l, normed, proj, logsum, mixed, middle, normed_mlp, upward = saved[l]
        part = slice(0, incoming.shape[0])
        incoming, gain_grads[l][1], bias_grads[l][1], *blocks = mlp_backward(
            spots, incoming, middle[part], gains[l][1], normed_mlp[part], upward,
            w_up[l], w_down[l], mlp_pieces[l], l < top,
        )
        if l < top:
            sums["down", l] = reduce_blocks(blocks[0], blocks[1], n_dp, n_t)
            sums["up", l] = reduce_blocks(blocks[2], blocks[3], n_dp, n_t)
        incoming, gain_grads[l][0], bias_grads[l][0], keep, send = attention_backward(
            spots, incoming, stream_l, gains[l][0], normed, proj, logsum, mixed, own[l], attn_pieces[l]
        )
        sums["attn", l] = reduce_blocks(keep, send, n_dp, n_t)

    grad_tokens = whole_pairs(incoming)
    type_grad = jnp.stack([jnp.sum(incoming[:WORDS], 0), jnp.sum(incoming[WORDS:], 0)])
    rows_all = jnp.concatenate(
        [type_grad] + [g for pair in gain_grads for g in pair] + [b for pair in bias_grads for b in pair], 0
    )
    rows_all = sum_all(rows_all, n_dp, n_t)
    rows_mine = lax.dynamic_slice_in_dim(rows_all, me * unit, unit, 1)
    grad_gain = rows_mine[2 : 2 + 2 * layers].reshape(layers, 2, unit)
    grad_bias = rows_mine[2 + 2 * layers :].reshape(layers, 2, unit)
    grad_qkv = jnp.stack([sums["attn", l][:, : 3 * inner].reshape(unit, 3, inner) for l in range(layers)])
    grad_out = jnp.stack([sums["attn", l][:, 3 * inner :].T for l in range(layers)])
    grad_up = jnp.stack([grad_up_top if l == top else sums["up", l] for l in range(layers)])
    grad_down = jnp.stack([grad_down_top if l == top else sums["down", l].T for l in range(layers)])
    return hidden_out, grad_tokens, rows_mine[:2], grad_gain, grad_bias, grad_qkv, grad_out, grad_up, grad_down


def solution(mesh):
    n_dp, n_t = mesh.shape["dp"], mesh.shape["tensor"]
    placed = (
        P("dp", None),
        P(),
        P(),
        P(),
        P(None, None, None, "tensor"),
        P(None, "tensor", None),
        P(None, None, "tensor"),
        P(None, "tensor", None),
        P("dp", None, None),
        P("dp", None),
    )

    def run(*args):
        return shards(*args, n_dp, n_t)

    return jax.shard_map(
        run,
        mesh=mesh,
        in_specs=placed,
        out_specs=(
            P("dp", None),
            P("dp", None),
            P(None, "dp"),
            P(None, None, "dp"),
            P(None, None, "dp"),
            P(None, "dp", None, "tensor"),
            P(None, "tensor", "dp"),
            P(None, "dp", "tensor"),
            P(None, "tensor", "dp"),
        ),
        check_vma=False,
    )
```

profile of v0, /device:TPU:0, one launch (start us, length us, event | category | flops | bytes accessed | tf_op | source)
XLA Modules:
  0.0 793.0 jit_solution(5279523111022525684)
XLA Ops:
  0.7 3.7 fusion.89
  8.2 3.0 collective-permute-start.54
  33.4 2.9 collective-permute-done.36.refs_0_
  50.3 5.9 collective-permute-done.40.refs_4_
  62.6 4.2 collective-permute-done.10.refs_4_
  69.0 3.0 collective-permute-done.45.refs_3_
  78.5 7.7 collective-permute-done.13.refs_1_
  92.5 3.2 collective-permute-start.30
  106.2 4.6 collective-permute-done.21.refs_3_
  118.7 19.0 %pack.12.rest_0_ = bf16[384,768]{1,0:T(8,128)(2,1)} custom-call(bf16[96,768]{1,0:T(8,128)(2,1)} %collective-permute-done.refs_0_, bf16[96,768]{1,0:T(8,128)(2,1)} %copy-done.46, bf16[96,768]{1,0:T(8,128)(2,1)} %copy-done.47, bf16[48,768]{1,0:T(8,128)(2,1)} %collective-permute-done.3.refs_3_, bf16[48,768]{1,0:T(8,128)(2,1)} %copy-done.76), custom_call_target="tpu_custom_call" | custom-call | bytes 1179648 | tf_op jit(solution)/shard_map/pack/pallas_call | solution.py:457
  137.7 19.0 %pack.18.rest_0_ = bf16[384,768]{1,0:T(8,128)(2,1)} custom-call(bf16[96,768]{1,0:T(8,128)(2,1)} %copy-done.62, bf16[96,768]{1,0:T(8,128)(2,1)} %copy-done.48, bf16[96,768]{1,0:T(8,128)(2,1)} %copy-done.50, bf16[48,768]{1,0:T(8,128)(2,1)} %copy-done.78, bf16[48,768]{1,0:T(8,128)(2,1)} %copy-done.80), custom_call_target="tpu_custom_call" | custom-call | bytes 1179648 | tf_op jit(solution)/shard_map/pack/pallas_call | solution.py:457
  170.3 36.9 %pack.15.rest_0_ = bf16[768,768]{1,0:T(8,128)(2,1)} custom-call(bf16[192,768]{1,0:T(8,128)(2,1)} %collective-permute-done.18.refs_0_, bf16[192,768]{1,0:T(8,128)(2,1)} %copy-done.37, bf16[192,768]{1,0:T(8,128)(2,1)} %copy-done.38, bf16[96,768]{1,0:T(8,128)(2,1)} %copy-done.65, bf16[96,768]{1,0:T(8,128)(2,1)} %copy-done.66), custom_call_target="tpu_custom_call" | custom-call | bytes 2359296 | tf_op jit(solution)/shard_map/pack/pallas_call | solution.py:457
  209.6 36.9 %pack.16.rest_2_ = bf16[768,768]{1,0:T(8,128)(2,1)} custom-call(bf16[192,768]{1,0:T(8,128)(2,1)} %collective-permute-done.24.refs_0_, bf16[192,768]{1,0:T(8,128)(2,1)} %copy-done.39, bf16[192,768]{1,0:T(8,128)(2,1)} %collective-permute-done.26.refs_2_, bf16[96,768]{1,0:T(8,128)(2,1)} %copy-done.69, bf16[96,768]{1,0:T(8,128)(2,1)} %collective-permute-done.28.refs_4_), custom_call_target="tpu_custom_call" | custom-call | bytes 2359296 | tf_op jit(solution)/shard_map/pack/pallas_call | solution.py:457
  246.5 36.9 %pack.17.rest_4_ = bf16[768,768]{1,0:T(8,128)(2,1)} custom-call(bf16[192,768]{1,0:T(8,128)(2,1)} %collective-permute-done.30.refs_0_, bf16[192,768]{1,0:T(8,128)(2,1)} %collective-permute-done.31.refs_1_, bf16[192,768]{1,0:T(8,128)(2,1)} %collective-permute-done.32.refs_2_, bf16[96,768]{1,0:T(8,128)(2,1)} %collective-permute-done.33.refs_3_, ...), custom_call_target="tpu_custom_call" | custom-call | bytes 2359296 | tf_op jit(solution)/shard_map/pack/pallas_call | solution.py:457
  291.3 2.6 pad_maximum_fusion.own
  293.9 19.0 %pack.13.rest_2_ = bf16[384,768]{1,0:T(8,128)(2,1)} custom-call(bf16[96,768]{1,0:T(8,128)(2,1)} %copy-done.60, bf16[96,768]{1,0:T(8,128)(2,1)} %copy-done.45, bf16[96,768]{1,0:T(8,128)(2,1)} %copy-done.44, bf16[48,768]{1,0:T(8,128)(2,1)} %copy-done.75, bf16[48,768]{1,0:T(8,128)(2,1)} %copy-done.74), custom_call_target="tpu_custom_call" | custom-call | bytes 1179648 | tf_op jit(solution)/shard_map/pack/pallas_call | solution.py:457
  312.9 19.0 %pack.14.rest_4_ = bf16[384,768]{1,0:T(8,128)(2,1)} custom-call(bf16[96,768]{1,0:T(8,128)(2,1)} %copy-done.61, bf16[96,768]{1,0:T(8,128)(2,1)} %copy-done.49, bf16[96,768]{1,0:T(8,128)(2,1)} %copy-done.51, bf16[48,768]{1,0:T(8,128)(2,1)} %copy-done.77, bf16[48,768]{1,0:T(8,128)(2,1)} %copy-done.79), custom_call_target="tpu_custom_call" | custom-call | bytes 1179648 | tf_op jit(solution)/shard_map/pack/pallas_call | solution.py:457
  333.9 36.9 %pack.21.rest_0_ = bf16[768,768]{1,0:T(8,128)(2,1)} custom-call(bf16[192,768]{1,0:T(8,128)(2,1)} %collective-permute-done.54.refs_0_, bf16[192,768]{1,0:T(8,128)(2,1)} %copy-done.34, bf16[192,768]{1,0:T(8,128)(2,1)} %copy-done.35, bf16[96,768]{1,0:T(8,128)(2,1)} %copy-done.63, bf16[96,768]{1,0:T(8,128)(2,1)} %copy-done.64), custom_call_target="tpu_custom_call" | custom-call | bytes 2359296 | tf_op jit(solution)/shard_map/pack/pallas_call | solution.py:457
  370.8 36.9 %pack.22.rest_2_ = bf16[768,768]{1,0:T(8,128)(2,1)} custom-call(bf16[192,768]{1,0:T(8,128)(2,1)} %collective-permute-done.60.refs_0_, bf16[192,768]{1,0:T(8,128)(2,1)} %copy-done.36, bf16[192,768]{1,0:T(8,128)(2,1)} %collective-permute-done.62.refs_2_, bf16[96,768]{1,0:T(8,128)(2,1)} %copy-done.67, bf16[96,768]{1,0:T(8,128)(2,1)} %copy-done.68), custom_call_target="tpu_custom_call" | custom-call | bytes 2359296 | tf_op jit(solution)/shard_map/pack/pallas_call | solution.py:457
  407.7 36.9 %pack.23.rest_4_ = bf16[768,768]{1,0:T(8,128)(2,1)} custom-call(bf16[192,768]{1,0:T(8,128)(2,1)} %copy-done.52, bf16[192,768]{1,0:T(8,128)(2,1)} %collective-permute-done.67.refs_1_, bf16[192,768]{1,0:T(8,128)(2,1)} %collective-permute-done.68.refs_2_, bf16[96,768]{1,0:T(8,128)(2,1)} %collective-permute-done.69.refs_3_, ...), custom_call_target="tpu_custom_call" | custom-call | bytes 2359296 | tf_op jit(solution)/shard_map/pack/pallas_call | solution.py:457
  447.8 19.0 %pack.19.rest_2_ = bf16[384,768]{1,0:T(8,128)(2,1)} custom-call(bf16[96,768]{1,0:T(8,128)(2,1)} %copy-done.58, bf16[96,768]{1,0:T(8,128)(2,1)} %copy-done.40, bf16[96,768]{1,0:T(8,128)(2,1)} %copy-done.41, bf16[48,768]{1,0:T(8,128)(2,1)} %copy-done.70, bf16[48,768]{1,0:T(8,128)(2,1)} %copy-done.71), custom_call_target="tpu_custom_call" | custom-call | bytes 1179648 | tf_op jit(solution)/shard_map/pack/pallas_call | solution.py:457
  466.9 19.0 %pack.20.rest_4_ = bf16[384,768]{1,0:T(8,128)(2,1)} custom-call(bf16[96,768]{1,0:T(8,128)(2,1)} %copy-done.59, bf16[96,768]{1,0:T(8,128)(2,1)} %copy-done.42, bf16[96,768]{1,0:T(8,128)(2,1)} %copy-done.43, bf16[48,768]{1,0:T(8,128)(2,1)} %copy-done.72, bf16[48,768]{1,0:T(8,128)(2,1)} %copy-done.73), custom_call_target="tpu_custom_call" | custom-call | bytes 1179648 | tf_op jit(solution)/shard_map/pack/pallas_call | solution.py:457
  490.7 9.9 %attention_forward.2 = (f32[256,768]{1,0:T(8,128)S(1)}, bf16[256,768]{1,0:T(8,128)(2,1)S(1)}, bf16[4,256,576]{2,1,0:T(8,128)(2,1)}, f32[256,128]{1,0:T(8,128)S(1)}, bf16[4,256,192]{2,1,0:T(8,128)(2,1)S(1)}) custom-call(s32[1]{0:T(128)} %bitcast.spot_ref, f32[256,768]{1,0:T(8,128)S(1)} %select_add_fusion.x, f32[1,768]{1,0:T(1,128)S(1)} %get-tuple-element.175.gain, ...), custom_call_target="tpu_custom_call" | custom-call | flops 4000000000 | bytes 10000000 | tf_op jit(solution)/shard_map/attention_forward/pallas_call | solution.py:185
  500.7 7.7 mlp_forward.2
  508.5 10.5 %attention_forward.3 = (f32[256,768]{1,0:T(8,128)S(1)}, bf16[256,768]{1,0:T(8,128)(2,1)S(1)}, bf16[4,256,576]{2,1,0:T(8,128)(2,1)}, f32[256,128]{1,0:T(8,128)S(1)}, bf16[4,256,192]{2,1,0:T(8,128)(2,1)S(1)}) custom-call(s32[1]{0:T(128)} %bitcast.spot_ref, f32[256,768]{1,0:T(8,128)S(1)} %get-tuple-element.46.x, f32[1,768]{1,0:T(1,128)S(1)} %get-tuple-element.174.gain, ...), custom_call_target="tpu_custom_call" | custom-call | flops 4000000000 | bytes 10000000 | tf_op jit(solution)/shard_map/attention_forward/pallas_call | solution.py:185
  519.0 6.7 mlp_forward.3
  526.8 6.7 mlp_backward.2
  533.5 16.8 %attention_backward.2 = (f32[256,768]{1,0:T(8,128)S(1)}, f32[1,768]{1,0:T(1,128)S(1)}, f32[1,768]{1,0:T(1,128)S(1)}, bf16[4,4,96,768]{3,2,1,0:T(8,128)(2,1)}, bf16[4,4,96,768]{3,2,1,0:T(8,128)(2,1)}) custom-call(s32[1]{0:T(128)} %bitcast.spot_ref, f32[48,768]{1,0:T(8,128)S(1)} %get-tuple-element.51.incoming, f32[256,768]{1,0:T(8,128)} %copy-done.19, ...), custom_call_target="tpu_custom_call" | custom-call | flops 6000000000 | bytes 20000000 | tf_op jit(solution)/shard_map/attention_backward/pallas_call | solution.py:402
  550.4 12.2 %mlp_backward.3 = (f32[256,768]{1,0:T(8,128)S(1)}, f32[1,768]{1,0:T(1,128)S(1)}, f32[1,768]{1,0:T(1,128)S(1)}, bf16[4,4,96,768]{3,2,1,0:T(8,128)(2,1)}, bf16[4,4...) custom-call(s32[1]{0:T(128)} %bitcast.spot_ref, ...), custom_call_target="tpu_custom_call" | custom-call | flops 6000000000 | bytes 20000000 | tf_op jit(solution)/shard_map/mlp_backward/pallas_call | solution.py:320
  562.7 17.6 %attention_backward.3 = (f32[256,768]{1,0:T(8,128)S(1)}, f32[1,768]{1,0:T(1,128)S(1)}, f32[1,768]{1,0:T(1,128)S(1)}, bf16[4,4,96,768]{3,2,1,0:T(8,128)(2,1)}, bf16[4,4,96,768]{3,2,1,0:T(8,128)(2,1)}) custom-call(s32[1]{0:T(128)} %bitcast.spot_ref, f32[256,768]{1,0:T(8,128)S(1)} %get-tuple-element.59.incoming, f32[256,768]{1,0:T(8,128)} %copy-done.6, ...), custom_call_target="tpu_custom_call" | custom-call | flops 6000000000 | bytes 20000000 | tf_op jit(solution)/shard_map/attention_backward/pallas_call | solution.py:402
  593.3 3.8 collective-permute-done.80
  599.2 2.6 collective-permute-done.81
  604.0 9.9 %collective-permute-done.82 = f32[10,768]{1,0:T(8,128)S(1)} collective-permute-done((f32[10,768]{1,0:T(8,128)S(1)}, f32[10,768]{1,0:T(8,128)S(1)}, u32[]{:S(2)}, u32[]{:S(2)}) %collective-permute-start.82) | collective-permute-done | bytes 30752 | tf_op jit(solution)/shard_map/ppermute | solution.py:531
  615.4 5.3 collective-permute-done.116
  623.1 7.9 collective-permute-done.117
  631.2 3.8 collective-permute-done.76
  635.0 8.4 %collective-permute-done.73 = bf16[256,768]{1,0:T(8,128)(2,1)S(1)} collective-permute-done((bf16[256,768]{1,0:T(8,128)(2,1)S(1)}, bf16[256,768]{1,0:T(8,128)(2,1)S(1)}, u32[]{:S(2)}, u32[]{:S(2)}) %collective-permute-start.73) | collective-permute-done | bytes 393248 | tf_op jit(solution)/shard_map/ppermute | solution.py:437
  645.5 6.3 collective-permute-done.77
  652.8 5.4 collective-permute-done.74
  664.3 4.0 fusion.7
  685.0 7.8 collective-permute-done.105
  696.1 3.0 collective-permute-done.85
  710.2 5.2 collective-permute-done.122
  724.8 3.2 collective-permute-done.86
  731.1 3.2 collective-permute-done.96
  745.7 2.6 collective-permute-done.107
  751.7 4.4 collective-permute-done.87
  773.0 5.8 collective-permute-done.92
  (528 shorter events, 233.5 us)
Async XLA Ops:
  8.2 29.6 %collective-permute-start.54 = (bf16[192,768]{1,0:T(8,128)(2,1)}, bf16[192,768]{1,0:T(8,128)(2,1)}, u32[]{:S(2)}, u32[]{:S(2)}) collective-permute-start(bf16[192,768]{1,0:T(8,128)(2,1)} %pad_maximum_fusion.6), channel_id=1, source_target_pairs={{0,1},{1,2},{2,3},{3,0},{4,5},{5,6},{6,7},{7,4},{8,9},{9,10},{10,1... | collective-permute-start | bytes 884744 | tf_op jit(solution)/shard_map/ppermute | solution.py:437
  13.0 24.8 %collective-permute-start.18 = (bf16[192,768]{1,0:T(8,128)(2,1)}, bf16[192,768]{1,0:T(8,128)(2,1)}, u32[]{:S(2)}, u32[]{:S(2)}) collective-permute-start(bf16[192,768]{1,0:T(8,128)(2,1)} %pad_maximum_fusion.5), channel_id=1, source_target_pairs={{0,1},{1,2},{2,3},{3,0},{4,5},{5,6},{6,7},{7,4},{8,9},{9,10},{10,1... | collective-permute-start | bytes 884744 | tf_op jit(solution)/shard_map/ppermute | solution.py:437
  56.5 18.1 %collective-permute-start.60 = (bf16[192,768]{1,0:T(8,128)(2,1)}, bf16[192,768]{1,0:T(8,128)(2,1)}, u32[]{:S(2)}, u32[]{:S(2)}) collective-permute-start(bf16[192,768]{1,0:T(8,128)(2,1)} %collective-permute-done.54.refs_0_), channel_id=1, source_target_pairs={{0,1},{1,2},{2,3},{3,0},{4,5},{5,6},{6,7},{7,4},{8,9},{9,10},{10,1... | collective-permute-start | bytes 884744 | tf_op jit(solution)/shard_map/ppermute | solution.py:437
  58.2 18.6 %collective-permute-start.55 = (bf16[192,768]{1,0:T(8,128)(2,1)}, bf16[192,768]{1,0:T(8,128)(2,1)S(1)}, u32[]{:S(2)}, u32[]{:S(2)}) collective-permute-start(bf16[192,768]{1,0:T(8,128)(2,1)} %collective-permute-done.54.refs_0_), channel_id=1, source_target_pairs={{0,8},{4,12},{8,0},{12,4},{16,24},{20,28},{24,16},{28,20},{1,9},{5... | collective-permute-start | bytes 884744 | tf_op jit(solution)/shard_map/ppermute | solution.py:433
  58.8 19.6 %collective-permute-start.56 = (bf16[192,768]{1,0:T(8,128)(2,1)}, bf16[192,768]{1,0:T(8,128)(2,1)S(1)}, u32[]{:S(2)}, u32[]{:S(2)}) collective-permute-start(bf16[192,768]{1,0:T(8,128)(2,1)} %collective-permute-done.54.refs_0_), channel_id=1, source_target_pairs={{0,16},{4,20},{8,24},{12,28},{16,0},{20,4},{24,8},{28,12},{1,17},{... | collective-permute-start | bytes 884744 | tf_op jit(solution)/shard_map/ppermute | solution.py:433
  71.9 16.2 %collective-permute-start.24 = (bf16[192,768]{1,0:T(8,128)(2,1)}, bf16[192,768]{1,0:T(8,128)(2,1)}, u32[]{:S(2)}, u32[]{:S(2)}) collective-permute-start(bf16[192,768]{1,0:T(8,128)(2,1)} %collective-permute-done.18.refs_0_), channel_id=1, source_target_pairs={{0,1},{1,2},{2,3},{3,0},{4,5},{5,6},{6,7},{7,4},{8,9},{9,10},{10,1... | collective-permute-start | bytes 884744 | tf_op jit(solution)/shard_map/ppermute | solution.py:437
  74.6 15.9 %collective-permute-start.20 = (bf16[192,768]{1,0:T(8,128)(2,1)}, bf16[192,768]{1,0:T(8,128)(2,1)S(1)}, u32[]{:S(2)}, u32[]{:S(2)}) collective-permute-start(bf16[192,768]{1,0:T(8,128)(2,1)} %collective-permute-done.18.refs_0_), channel_id=1, source_target_pairs={{0,16},{4,20},{8,24},{12,28},{16,0},{20,4},{24,8},{28,12},{1,17},{... | collective-permute-start | bytes 884744 | tf_op jit(solution)/shard_map/ppermute | solution.py:433
  92.5 20.4 %collective-permute-start.30 = (bf16[192,768]{1,0:T(8,128)(2,1)}, bf16[192,768]{1,0:T(8,128)(2,1)}, u32[]{:S(2)}, u32[]{:S(2)}) collective-permute-start(bf16[192,768]{1,0:T(8,128)(2,1)} %collective-permute-done.24.refs_0_), channel_id=1, source_target_pairs={{0,1},{1,2},{2,3},{3,0},{4,5},{5,6},{6,7},{7,4},{8,9},{9,10},{10,1... | collective-permute-start | bytes 884744 | tf_op jit(solution)/shard_map/ppermute | solution.py:437
  112.4 44.4 %collective-permute-start.26 = (bf16[192,768]{1,0:T(8,128)(2,1)}, bf16[192,768]{1,0:T(8,128)(2,1)}, u32[]{:S(2)}, u32[]{:S(2)}) collective-permute-start(bf16[192,768]{1,0:T(8,128)(2,1)} %collective-permute-done.24.refs_0_), channel_id=1, source_target_pairs={{0,16},{4,20},{8,24},{12,28},{16,0},{20,4},{24,8},{28,12},{1,17},{... | collective-permute-start | bytes 884744 | tf_op jit(solution)/shard_map/ppermute | solution.py:433
  112.9 44.0 %collective-permute-start.31 = (bf16[192,768]{1,0:T(8,128)(2,1)}, bf16[192,768]{1,0:T(8,128)(2,1)}, u32[]{:S(2)}, u32[]{:S(2)}) collective-permute-start(bf16[192,768]{1,0:T(8,128)(2,1)} %collective-permute-done.30.refs_0_), channel_id=1, source_target_pairs={{0,8},{4,12},{8,0},{12,4},{16,24},{20,28},{24,16},{28,20},{1,9},{5... | collective-permute-start | bytes 884744 | tf_op jit(solution)/shard_map/ppermute | solution.py:433
  113.6 46.9 %collective-permute-start.62 = (bf16[192,768]{1,0:T(8,128)(2,1)}, bf16[192,768]{1,0:T(8,128)(2,1)}, u32[]{:S(2)}, u32[]{:S(2)}) collective-permute-start(bf16[192,768]{1,0:T(8,128)(2,1)} %collective-permute-done.60.refs_0_), channel_id=1, source_target_pairs={{0,16},{4,20},{8,24},{12,28},{16,0},{20,4},{24,8},{28,12},{1,17},{... | collective-permute-start | bytes 884744 | tf_op jit(solution)/shard_map/ppermute | solution.py:433
  114.8 47.0 %collective-permute-start.32 = (bf16[192,768]{1,0:T(8,128)(2,1)}, bf16[192,768]{1,0:T(8,128)(2,1)}, u32[]{:S(2)}, u32[]{:S(2)}) collective-permute-start(bf16[192,768]{1,0:T(8,128)(2,1)} %collective-permute-done.30.refs_0_), channel_id=1, source_target_pairs={{0,16},{4,20},{8,24},{12,28},{16,0},{20,4},{24,8},{28,12},{1,17},{... | collective-permute-start | bytes 884744 | tf_op jit(solution)/shard_map/ppermute | solution.py:433
  117.8 47.1 %collective-permute-start.27 = (bf16[96,768]{1,0:T(8,128)(2,1)}, bf16[96,768]{1,0:T(8,128)(2,1)S(1)}, u32[]{:S(2)}, u32[]{:S(2)}) collective-permute-start(bf16[96,768]{1,0:T(8,128)(2,1)} %slice.691), channel_id=1, source_target_pairs={{0,16},{4,20},{8,24},{12,28},{16,0},{20,4},{24,8},{28,12},{1,17},{... | collective-permute-start | bytes 442376 | tf_op jit(solution)/shard_map/ppermute | solution.py:433
  156.8 126.6 %collective-permute-start.5 = (bf16[384,768]{1,0:T(8,128)(2,1)}, bf16[384,768]{1,0:T(8,128)(2,1)S(1)}, u32[]{:S(2)}, u32[]{:S(2)}) collective-permute-start(bf16[384,768]{1,0:T(8,128)(2,1)} %pack.12.rest_0_), channel_id=1, source_target_pairs={{0,4},{4,0},{8,12},{12,8},{16,20},{20,16},{24,28},{28,24},{1,5},{5... | collective-permute-start | bytes 1769480 | tf_op jit(solution)/shard_map/ppermute | solution.py:433
  156.9 127.0 %collective-permute-start.41 = (bf16[384,768]{1,0:T(8,128)(2,1)}, bf16[384,768]{1,0:T(8,128)(2,1)}, u32[]{:S(2)}, u32[]{:S(2)}) collective-permute-start(bf16[384,768]{1,0:T(8,128)(2,1)} %pack.18.rest_0_), channel_id=1, source_target_pairs={{0,4},{4,0},{8,12},{12,8},{16,20},{20,16},{24,28},{28,24},{1,5},{5... | collective-permute-start | bytes 1769480 | tf_op jit(solution)/shard_map/ppermute | solution.py:433
  165.5 41.6 %collective-permute-start.34 = (bf16[96,768]{1,0:T(8,128)(2,1)}, bf16[96,768]{1,0:T(8,128)(2,1)}, u32[]{:S(2)}, u32[]{:S(2)}) collective-permute-start(bf16[96,768]{1,0:T(8,128)(2,1)} %slice.694), channel_id=1, source_target_pairs={{0,8},{4,12},{8,0},{12,4},{16,24},{20,28},{24,16},{28,20},{1,9},{5... | collective-permute-start | bytes 442376 | tf_op jit(solution)/shard_map/ppermute | solution.py:433
  166.7 117.9 %collective-permute-start.67 = (bf16[192,768]{1,0:T(8,128)(2,1)}, bf16[192,768]{1,0:T(8,128)(2,1)}, u32[]{:S(2)}, u32[]{:S(2)}) collective-permute-start(bf16[192,768]{1,0:T(8,128)(2,1)} %copy-done.52), channel_id=1, source_target_pairs={{0,8},{4,12},{8,0},{12,4},{16,24},{20,28},{24,16},{28,20},{1,9},{5... | collective-permute-start | bytes 884744 | tf_op jit(solution)/shard_map/ppermute | solution.py:433
  168.0 116.7 %collective-permute-start.68 = (bf16[192,768]{1,0:T(8,128)(2,1)}, bf16[192,768]{1,0:T(8,128)(2,1)}, u32[]{:S(2)}, u32[]{:S(2)}) collective-permute-start(bf16[192,768]{1,0:T(8,128)(2,1)} %copy-done.52), channel_id=1, source_target_pairs={{0,16},{4,20},{8,24},{12,28},{16,0},{20,4},{24,8},{28,12},{1,17},{... | collective-permute-start | bytes 884744 | tf_op jit(solution)/shard_map/ppermute | solution.py:433
  207.2 238.0 %collective-permute-start.23 = (bf16[768,768]{1,0:T(8,128)(2,1)}, bf16[768,768]{1,0:T(8,128)(2,1)}, u32[]{:S(2)}, u32[]{:S(2)}) collective-permute-start(bf16[768,768]{1,0:T(8,128)(2,1)} %pack.15.rest_0_), channel_id=1, source_target_pairs={{0,4},{4,0},{8,12},{12,8},{16,20},{20,16},{24,28},{28,24},{1,5},{5... | collective-permute-start | bytes 3538952 | tf_op jit(solution)/shard_map/ppermute | solution.py:433
  284.6 201.3 %collective-permute-start.29 = (bf16[768,768]{1,0:T(8,128)(2,1)}, bf16[768,768]{1,0:T(8,128)(2,1)}, u32[]{:S(2)}, u32[]{:S(2)}) collective-permute-start(bf16[768,768]{1,0:T(8,128)(2,1)} %pack.16.rest_2_), channel_id=1, source_target_pairs={{0,4},{4,0},{8,12},{12,8},{16,20},{20,16},{24,28},{28,24},{1,5},{5... | collective-permute-start | bytes 3538952 | tf_op jit(solution)/shard_map/ppermute | solution.py:433
  284.6 201.8 %collective-permute-start.35 = (bf16[768,768]{1,0:T(8,128)(2,1)}, bf16[768,768]{1,0:T(8,128)(2,1)}, u32[]{:S(2)}, u32[]{:S(2)}) collective-permute-start(bf16[768,768]{1,0:T(8,128)(2,1)} %pack.17.rest_4_), channel_id=1, source_target_pairs={{0,4},{4,0},{8,12},{12,8},{16,20},{20,16},{24,28},{28,24},{1,5},{5... | collective-permute-start | bytes 3538952 | tf_op jit(solution)/shard_map/ppermute | solution.py:433
  289.9 42.0 %collective-permute-start.69 = (bf16[96,768]{1,0:T(8,128)(2,1)}, bf16[96,768]{1,0:T(8,128)(2,1)}, u32[]{:S(2)}, u32[]{:S(2)}) collective-permute-start(bf16[96,768]{1,0:T(8,128)(2,1)} %slice.705), channel_id=1, source_target_pairs={{0,16},{4,20},{8,24},{12,28},{16,0},{20,4},{24,8},{28,12},{1,17},{... | collective-permute-start | bytes 442376 | tf_op jit(solution)/shard_map/ppermute | solution.py:433
  290.3 41.7 %collective-permute-start.70 = (bf16[96,768]{1,0:T(8,128)(2,1)}, bf16[96,768]{1,0:T(8,128)(2,1)}, u32[]{:S(2)}, u32[]{:S(2)}) collective-permute-start(bf16[96,768]{1,0:T(8,128)(2,1)} %slice.706), channel_id=1, source_target_pairs={{0,8},{4,12},{8,0},{12,4},{16,24},{20,28},{24,16},{28,20},{1,9},{5... | collective-permute-start | bytes 442376 | tf_op jit(solution)/shard_map/ppermute | solution.py:433
  332.0 112.7 %collective-permute-start.11 = (bf16[384,768]{1,0:T(8,128)(2,1)}, bf16[384,768]{1,0:T(8,128)(2,1)}, u32[]{:S(2)}, u32[]{:S(2)}) collective-permute-start(bf16[384,768]{1,0:T(8,128)(2,1)} %pack.13.rest_2_), channel_id=1, source_target_pairs={{0,4},{4,0},{8,12},{12,8},{16,20},{20,16},{24,28},{28,24},{1,5},{5... | collective-permute-start | bytes 1769480 | tf_op jit(solution)/shard_map/ppermute | solution.py:433
  332.0 112.7 %collective-permute-start.17 = (bf16[384,768]{1,0:T(8,128)(2,1)}, bf16[384,768]{1,0:T(8,128)(2,1)}, u32[]{:S(2)}, u32[]{:S(2)}) collective-permute-start(bf16[384,768]{1,0:T(8,128)(2,1)} %pack.14.rest_4_), channel_id=1, source_target_pairs={{0,4},{4,0},{8,12},{12,8},{16,20},{20,16},{24,28},{28,24},{1,5},{5... | collective-permute-start | bytes 1769480 | tf_op jit(solution)/shard_map/ppermute | solution.py:433
  444.6 74.3 %collective-permute-start.59 = (bf16[768,768]{1,0:T(8,128)(2,1)}, bf16[768,768]{1,0:T(8,128)(2,1)}, u32[]{:S(2)}, u32[]{:S(2)}) collective-permute-start(bf16[768,768]{1,0:T(8,128)(2,1)} %pack.21.rest_0_), channel_id=1, source_target_pairs={{0,4},{4,0},{8,12},{12,8},{16,20},{20,16},{24,28},{28,24},{1,5},{5... | collective-permute-start | bytes 3538952 | tf_op jit(solution)/shard_map/ppermute | solution.py:433
  444.8 74.2 %collective-permute-start.65 = (bf16[768,768]{1,0:T(8,128)(2,1)}, bf16[768,768]{1,0:T(8,128)(2,1)}, u32[]{:S(2)}, u32[]{:S(2)}) collective-permute-start(bf16[768,768]{1,0:T(8,128)(2,1)} %pack.22.rest_2_), channel_id=1, source_target_pairs={{0,4},{4,0},{8,12},{12,8},{16,20},{20,16},{24,28},{28,24},{1,5},{5... | collective-permute-start | bytes 3538952 | tf_op jit(solution)/shard_map/ppermute | solution.py:433
  445.2 73.8 %collective-permute-start.71 = (bf16[768,768]{1,0:T(8,128)(2,1)}, bf16[768,768]{1,0:T(8,128)(2,1)}, u32[]{:S(2)}, u32[]{:S(2)}) collective-permute-start(bf16[768,768]{1,0:T(8,128)(2,1)} %pack.23.rest_4_), channel_id=1, source_target_pairs={{0,4},{4,0},{8,12},{12,8},{16,20},{20,16},{24,28},{28,24},{1,5},{5... | collective-permute-start | bytes 3538952 | tf_op jit(solution)/shard_map/ppermute | solution.py:433
  485.9 22.5 %collective-permute-start.47 = (bf16[384,768]{1,0:T(8,128)(2,1)}, bf16[384,768]{1,0:T(8,128)(2,1)S(1)}, u32[]{:S(2)}, u32[]{:S(2)}) collective-permute-start(bf16[384,768]{1,0:T(8,128)(2,1)} %pack.19.rest_2_), channel_id=1, source_target_pairs={{0,4},{4,0},{8,12},{12,8},{16,20},{20,16},{24,28},{28,24},{1,5},{5... | collective-permute-start | bytes 1769480 | tf_op jit(solution)/shard_map/ppermute | solution.py:433
  486.4 22.0 %collective-permute-start.53 = (bf16[384,768]{1,0:T(8,128)(2,1)}, bf16[384,768]{1,0:T(8,128)(2,1)S(1)}, u32[]{:S(2)}, u32[]{:S(2)}) collective-permute-start(bf16[384,768]{1,0:T(8,128)(2,1)} %pack.20.rest_4_), channel_id=1, source_target_pairs={{0,4},{4,0},{8,12},{12,8},{16,20},{20,16},{24,28},{28,24},{1,5},{5... | collective-permute-start | bytes 1769480 | tf_op jit(solution)/shard_map/ppermute | solution.py:433
  580.4 87.9 %collective-permute-start.119 = (bf16[4,4,96,768]{3,2,1,0:T(8,128)(2,1)}, bf16[4,4,96,768]{3,2,1,0:T(8,128)(2,1)}, u32[]{:S(2)}, u32[]{:S(2)}) collective-permute-start(bf16[4,4,96,768]{3,2,1,0:T(8,128)(2,1)} %get-tuple-element.80), channel_id=1, source_target_pairs={{0,4},{4,0},{8,12},{12,8},{16,20},{20,16},{24,28},{28,24},{1,5},{5... | collective-permute-start | bytes 7077896 | tf_op jit(solution)/shard_map/ppermute | solution.py:433
  582.6 89.8 %collective-permute-start.103 = (bf16[4,4,96,768]{3,2,1,0:T(8,128)(2,1)}, bf16[4,4,96,768]{3,2,1,0:T(8,128)(2,1)}, u32[]{:S(2)}, u32[]{:S(2)}) collective-permute-start(bf16[4,4,96,768]{3,2,1,0:T(8,128)(2,1)} %get-tuple-element.78), channel_id=1, source_target_pairs={{0,4},{4,0},{8,12},{12,8},{16,20},{20,16},{24,28},{28,24},{1,5},{5... | collective-permute-start | bytes 7077896 | tf_op jit(solution)/shard_map/ppermute | solution.py:433
  583.2 37.9 %collective-permute-start.72 = (bf16[256,768]{1,0:T(8,128)(2,1)S(1)}, bf16[256,768]{1,0:T(8,128)(2,1)S(1)}, u32[]{:S(2)}, u32[]{:S(2)}) collective-permute-start(bf16[256,768]{1,0:T(8,128)(2,1)S(1)} %get-tuple-element.48), channel_id=1, source_target_pairs={{0,1},{1,2},{2,3},{3,0},{4,5},{5,6},{6,7},{7,4},{8,9},{9,10},{10,1... | collective-permute-start | bytes 1179656 | tf_op jit(solution)/shard_map/ppermute | solution.py:437
  601.8 19.4 %collective-permute-start.75 = (bf16[256,768]{1,0:T(8,128)(2,1)S(1)}, bf16[256,768]{1,0:T(8,128)(2,1)S(1)}, u32[]{:S(2)}, u32[]{:S(2)}) collective-permute-start(bf16[256,768]{1,0:T(8,128)(2,1)S(1)} %get-tuple-element.104), channel_id=1, source_target_pairs={{0,1},{1,2},{2,3},{3,0},{4,5},{5,6},{6,7},{7,4},{8,9},{9,10},{10,1... | collective-permute-start | bytes 1179656 | tf_op jit(solution)/shard_map/ppermute | solution.py:437
  621.1 22.3 %collective-permute-start.73 = (bf16[256,768]{1,0:T(8,128)(2,1)S(1)}, bf16[256,768]{1,0:T(8,128)(2,1)S(1)}, u32[]{:S(2)}, u32[]{:S(2)}) collective-permute-start(bf16[256,768]{1,0:T(8,128)(2,1)S(1)} %collective-permute-done.72), channel_id=1, source_target_pairs={{0,1},{1,2},{2,3},{3,0},{4,5},{5,6},{6,7},{7,4},{8,9},{9,10},{10,1... | collective-permute-start | bytes 1179656 | tf_op jit(solution)/shard_map/ppermute | solution.py:437
  631.1 28.0 %collective-permute-start.118 = (bf16[16,32,768]{2,1,0:T(8,128)(2,1)S(1)}, bf16[16,32,768]{2,1,0:T(8,128)(2,1)S(1)}, u32[]{:S(2)}, u32[]{:S(2)}) collective-permute-start(bf16[16,32,768]{2,1,0:T(8,128)(2,1)S(1)} %get-tuple-element.143), channel_id=1, source_target_pairs={{0,4},{4,0},{8,12},{12,8},{16,20},{20,16},{24,28},{28,24},{1,5},{5... | collective-permute-start | bytes 2359304 | tf_op jit(solution)/shard_map/ppermute | solution.py:433
  635.0 16.9 %collective-permute-start.77 = (bf16[256,768]{1,0:T(8,128)(2,1)S(1)}, bf16[256,768]{1,0:T(8,128)(2,1)S(1)}, u32[]{:S(2)}, u32[]{:S(2)}) collective-permute-start(bf16[256,768]{1,0:T(8,128)(2,1)S(1)} %collective-permute-done.76), channel_id=1, source_target_pairs={{0,1},{1,2},{2,3},{3,0},{4,5},{5,6},{6,7},{7,4},{8,9},{9,10},{10,1... | collective-permute-start | bytes 1179656 | tf_op jit(solution)/shard_map/ppermute | solution.py:437
  651.8 24.0 %collective-permute-start.83 = (bf16[4,4,96,768]{3,2,1,0:T(8,128)(2,1)}, bf16[4,4,96,768]{3,2,1,0:T(8,128)(2,1)}, u32[]{:S(2)}, u32[]{:S(2)}) collective-permute-start(bf16[4,4,96,768]{3,2,1,0:T(8,128)(2,1)} %get-tuple-element.74), channel_id=1, source_target_pairs={{0,4},{4,0},{8,12},{12,8},{16,20},{20,16},{24,28},{28,24},{1,5},{5... | collective-permute-start | bytes 7077896 | tf_op jit(solution)/shard_map/ppermute | solution.py:433
  658.2 19.8 %collective-permute-start.93 = (bf16[4,4,96,768]{3,2,1,0:T(8,128)(2,1)}, bf16[4,4,96,768]{3,2,1,0:T(8,128)(2,1)}, u32[]{:S(2)}, u32[]{:S(2)}) collective-permute-start(bf16[4,4,96,768]{3,2,1,0:T(8,128)(2,1)} %get-tuple-element.76), channel_id=1, source_target_pairs={{0,4},{4,0},{8,12},{12,8},{16,20},{20,16},{24,28},{28,24},{1,5},{5... | collective-permute-start | bytes 7077896 | tf_op jit(solution)/shard_map/ppermute | solution.py:433
  672.3 36.0 %collective-permute-start.120 = (bf16[2,96,768]{2,1,0:T(8,128)(2,1)S(1)}, bf16[2,96,768]{2,1,0:T(8,128)(2,1)S(1)}, u32[]{:S(2)}, u32[]{:S(2)}) collective-permute-start(bf16[2,96,768]{2,1,0:T(8,128)(2,1)S(1)} %get-tuple-element.110), channel_id=1, source_target_pairs={{0,8},{4,12},{8,0},{12,4},{16,24},{20,28},{24,16},{28,20},{1,9},{5... | collective-permute-start | bytes 884744 | tf_op jit(solution)/shard_map/ppermute | solution.py:433
  675.8 17.0 %collective-permute-start.105 = (bf16[2,96,768]{2,1,0:T(8,128)(2,1)S(1)}, bf16[2,96,768]{2,1,0:T(8,128)(2,1)S(1)}, u32[]{:S(2)}, u32[]{:S(2)}) collective-permute-start(bf16[2,96,768]{2,1,0:T(8,128)(2,1)S(1)} %get-tuple-element.115), channel_id=1, source_target_pairs={{0,8},{4,12},{8,0},{12,4},{16,24},{20,28},{24,16},{28,20},{1,9},{5... | collective-permute-start | bytes 884744 | tf_op jit(solution)/shard_map/ppermute | solution.py:433
  680.7 18.4 %collective-permute-start.85 = (bf16[2,96,768]{2,1,0:T(8,128)(2,1)S(1)}, bf16[2,96,768]{2,1,0:T(8,128)(2,1)S(1)}, u32[]{:S(2)}, u32[]{:S(2)}) collective-permute-start(bf16[2,96,768]{2,1,0:T(8,128)(2,1)S(1)} %get-tuple-element.121), channel_id=1, source_target_pairs={{0,8},{4,12},{8,0},{12,4},{16,24},{20,28},{24,16},{28,20},{1,9},{5... | collective-permute-start | bytes 884744 | tf_op jit(solution)/shard_map/ppermute | solution.py:433
  681.9 18.9 %collective-permute-start.88 = (bf16[2,96,768]{2,1,0:T(8,128)(2,1)S(1)}, bf16[2,96,768]{2,1,0:T(8,128)(2,1)S(1)}, u32[]{:S(2)}, u32[]{:S(2)}) collective-permute-start(bf16[2,96,768]{2,1,0:T(8,128)(2,1)S(1)} %get-tuple-element.119), channel_id=1, source_target_pairs={{0,16},{4,20},{8,24},{12,28},{16,0},{20,4},{24,8},{28,12},{1,17},{... | collective-permute-start | bytes 884744 | tf_op jit(solution)/shard_map/ppermute | solution.py:433
  699.1 36.2 %collective-permute-start.126 = (bf16[2,96,768]{2,1,0:T(8,128)(2,1)S(1)}, bf16[2,96,768]{2,1,0:T(8,128)(2,1)S(1)}, u32[]{:S(2)}, u32[]{:S(2)}) collective-permute-start(bf16[2,96,768]{2,1,0:T(8,128)(2,1)S(1)} %get-tuple-element.108), channel_id=1, source_target_pairs={{0,16},{4,20},{8,24},{12,28},{16,0},{20,4},{24,8},{28,12},{1,17},{... | collective-permute-start | bytes 884744 | tf_op jit(solution)/shard_map/ppermute | solution.py:433
  708.4 16.0 %collective-permute-start.84 = (bf16[2,96,768]{2,1,0:T(8,128)(2,1)S(1)}, bf16[2,96,768]{2,1,0:T(8,128)(2,1)S(1)}, u32[]{:S(2)}, u32[]{:S(2)}) collective-permute-start(bf16[2,96,768]{2,1,0:T(8,128)(2,1)S(1)} %get-tuple-element.122), channel_id=1, source_target_pairs={{0,8},{4,12},{8,0},{12,4},{16,24},{20,28},{24,16},{28,20},{1,9},{5... | collective-permute-start | bytes 884744 | tf_op jit(solution)/shard_map/ppermute | solution.py:433
  724.4 18.0 %collective-permute-start.110 = (bf16[2,96,768]{2,1,0:T(8,128)(2,1)S(1)}, bf16[2,96,768]{2,1,0:T(8,128)(2,1)S(1)}, u32[]{:S(2)}, u32[]{:S(2)}) collective-permute-start(bf16[2,96,768]{2,1,0:T(8,128)(2,1)S(1)} %get-tuple-element.114), channel_id=1, source_target_pairs={{0,16},{4,20},{8,24},{12,28},{16,0},{20,4},{24,8},{28,12},{1,17},{... | collective-permute-start | bytes 884744 | tf_op jit(solution)/shard_map/ppermute | solution.py:433
  763.6 20.9 %collective-permute-start.128 = (bf16[96,768]{1,0:T(8,128)(2,1)S(1)}, bf16[96,768]{1,0:T(8,128)(2,1)}, u32[]{:S(2)}, u32[]{:S(2)}) collective-permute-start(bf16[96,768]{1,0:T(8,128)(2,1)S(1)} %fusion.39), channel_id=1, source_target_pairs={{0,1},{1,2},{2,3},{3,0},{4,5},{5,6},{6,7},{7,4},{8,9},{9,10},{10,1... | collective-permute-start | bytes 442376 | tf_op jit(solution)/shard_map/ppermute | solution.py:437
  767.3 23.2 %collective-permute-start.112 = (bf16[96,768]{1,0:T(8,128)(2,1)}, bf16[96,768]{1,0:T(8,128)(2,1)}, u32[]{:S(2)}, u32[]{:S(2)}) collective-permute-start(bf16[96,768]{1,0:T(8,128)(2,1)} %fusion.46), channel_id=1, source_target_pairs={{0,1},{1,2},{2,3},{3,0},{4,5},{5,6},{6,7},{7,4},{8,9},{9,10},{10,1... | collective-permute-start | bytes 442376 | tf_op jit(solution)/shard_map/ppermute | solution.py:437
  (168 other events, 2577.8 us)
where the time goes:
time: 802 us; the launch traced here: 793 us
  Pallas kernels  423 us (53%)
  waiting for transfers between devices  150 us (19%)
  starting transfers between devices  108 us (13%)
  other arithmetic  54.4 us (7%)
  local copies, waits for them, and re-layouts  48.1 us (6%)
    pallas_call x12, Pallas kernels, pack(): pl.pallas_call(pack_kernel, out_shape=jax.ShapeDtypeStruct((rows, width),...  335 us
    ppermute x94, starting transfers between devices, swap(): return lax.ppermute(values, 'dp', [(i, i ^ bit) for i in range(size)])  83.4 us
    ppermute x94, waiting for transfers between devices, swap(): return lax.ppermute(values, 'dp', [(i, i ^ bit) for i in range(size)])  82.4 us
    ppermute x33, waiting for transfers between devices, shift(): lax.ppermute(values, 'tensor', [(i, (i + 1) % size) for i in range(size)])  55.3 us
    pallas_call x2, Pallas kernels, attention_backward(): pl.pallas_call(attention_backward_kernel, grid=(n_t,), out_shape=out, in_...  34.5 us
    ppermute x33, starting transfers between devices, shift(): lax.ppermute(values, 'tensor', [(i, (i + 1) % size) for i in range(size)])  23.9 us
    pallas_call x2, Pallas kernels, attention_forward(): pl.pallas_call(attention_forward_kernel, grid=(n_t,), out_shape=out, in_s...  20.3 us
    pallas_call x2, Pallas kernels, mlp_backward(): pl.pallas_call(functools.partial(mlp_backward_kernel, blocks), grid=(n_t,...  18.9 us
  transfers between devices with their start and end apart: 129, of which 48 were waited for; matrix products, arithmetic and copies ran while one was open for 11% of the time, Pallas kernels for 46%

commit v1 on v0

v1 whole, which is shorter than its diff:
```python
import functools

import jax
import jax.numpy as jnp
from jax import lax
from jax.experimental import pallas as pl
from jax.experimental.pallas import tpu as pltpu
from jax.sharding import PartitionSpec as P

HD = 64
WORDS = 40
TOP_ROWS = 48
SLOT_ROWS = 16
EPSILON = 1e-06
ROOT_HALF = 0.7071067811865476
ROOT_TWO_PI = 2.5066282746310002
GROUP = 8
STEP = 32
F32 = jnp.float32
BF16 = jnp.bfloat16
SMALL_VMEM = 16 * 1024 * 1024
VMEM_BYTES = 60 * 1024 * 1024


def dot(left, right, dims):
    return lax.dot_general(left, right, (dims, ((), ())), preferred_element_type=F32)


def nn(left, right):
    return dot(left, right, ((1,), (0,)))


def nt(left, right):
    return dot(left, right, ((1,), (1,)))


def tn(left, right):
    return dot(left, right, ((0,), (0,)))


def gelu(values):
    return 0.5 * values * (1.0 + lax.erf(values * ROOT_HALF))


def gelu_slope(values):
    return 0.5 * (1.0 + lax.erf(values * ROOT_HALF)) + values * jnp.exp(-0.5 * values * values) / ROOT_TWO_PI


def norm_parts(values):
    average = jnp.mean(values, axis=-1, keepdims=True)
    centred = values - average
    spread = jnp.mean(centred * centred, axis=-1, keepdims=True)
    rate = lax.rsqrt(spread + EPSILON)
    return centred * rate, rate


def norm_rows(source, gain, bias, target):
    for r in range(0, source.shape[0], STEP):
        rows = slice(r, r + STEP)
        target[rows, :] = (norm_parts(source[rows, :])[0] * gain[...] + bias[...]).astype(BF16)


def norm_back_rows(rows, values, gain, incoming, gain_grad, bias_grad):
    unit, rate = norm_parts(values[rows, :])
    e = incoming[rows, :]
    scaled = e * gain[...]
    inner = jnp.mean(scaled * unit, axis=-1, keepdims=True)
    gain_grad[...] += jnp.sum(e * unit, axis=0, keepdims=True)
    bias_grad[...] += jnp.sum(e, axis=0, keepdims=True)
    return rate * (scaled - jnp.mean(scaled, axis=-1, keepdims=True) - unit * inner)


KERNEL_COST = pl.CostEstimate(flops=40_000_000_000, bytes_accessed=1_000_000, transcendentals=0)
SMALL_COST = pl.CostEstimate(flops=1_000_000_000, bytes_accessed=1_000_000, transcendentals=0)


class Pieces:
    def __init__(self, at):
        self.arrays = []
        self.plan = []
        for matrix in at:
            for k, slices in enumerate(matrix, 1):
                for s, (array, lead, row) in enumerate(slices):
                    found = [i for i, v in enumerate(self.arrays) if v is array]
                    if not found:
                        self.arrays.append(array)
                        found = [len(self.arrays) - 1]
                    self.plan.append((len(self.plan) // (len(matrix) * GROUP), k, s, found[0], lead, row))


def fetch(spot, own, plan, sources, scratches, sems, quarters):
    rows = scratches[0].shape[1] // GROUP
    for k in quarters:
        for m, scratch in enumerate(scratches):
            if k == 0:
                pltpu.make_async_copy(own[m], scratch.at[0], sems.at[0]).start()
        for m, at_k, s, which, lead, row in plan:
            if at_k == k:
                source = sources[which] if lead is None else sources[which].at[lead]
                at = pl.multiple_of((spot ^ s) * rows, rows)
                pltpu.make_async_copy(
                    source.at[pl.ds(row, rows)],
                    scratches[m].at[k - quarters[0], pl.ds(at, rows)],
                    sems.at[k - quarters[0]],
                ).start()


def arrived(k, scratches, sems):
    for scratch in scratches:
        pltpu.make_async_copy(scratch.at[k], scratch.at[k], sems.at[k]).wait()


def flip(spot, source, target):
    width = source.shape[1]
    rows = width // GROUP
    turned = source.astype(F32).T.astype(BF16)
    for j in range(GROUP):
        s = spot ^ j
        at = pl.multiple_of(((s & 1) * (GROUP // 2) + (s >> 1)) * rows, rows)
        target[pl.ds(at, rows), :] = turned[j * rows : (j + 1) * rows, :]


def put_block(block, keep, send, part, columns=slice(None)):
    half = block.shape[0] // 2
    rows = half // (GROUP // 2)
    for i in range(GROUP // 2):
        keep[i, 0, part, :, columns] = block[i * rows : (i + 1) * rows].astype(BF16)
        send[i, 0, part, :, columns] = block[half + i * rows : half + (i + 1) * rows].astype(BF16)


def any_spec():
    return pl.BlockSpec(memory_space=pl.ANY)


def smem_spec():
    return pl.BlockSpec(memory_space=pltpu.SMEM)


def whole(shape):
    return pl.BlockSpec(shape, lambda k: (0,) * len(shape))


def per_quarter(shape, first=0):
    return pl.BlockSpec((1,) + shape, lambda k: (first + k,) + (0,) * len(shape))


def block_specs(matrices, rows, width):
    return [pl.BlockSpec((GROUP // 2, 1, matrices, rows, width), lambda k: (0, k, 0, 0, 0))] * 2


def block_shapes(quarters, matrices, rows, width):
    return [jax.ShapeDtypeStruct((GROUP // 2, quarters, matrices, rows, width), BF16)] * 2


def params(limit=VMEM_BYTES):
    return pltpu.CompilerParams(vmem_limit_bytes=limit, dimension_semantics=("arbitrary",))


def cost(flops, moved):
    return pl.CostEstimate(flops=flops, bytes_accessed=moved, transcendentals=0)


def attention_forward_kernel(plan, count, spot_ref, x, gain, bias, own, *rest):
    middle, normed, proj, logsum, mixed, block, sems = rest[count:]
    k = pl.program_id(0)
    inner = mixed.shape[-1]
    heads = inner // HD

    @pl.when(k == 0)
    def _():
        fetch(spot_ref[0], [own], plan, rest[:count], [block], sems, range(block.shape[0]))
        norm_rows(x, gain, bias, normed)
        middle[...] = x[...]
        logsum[...] = jnp.zeros_like(logsum)

    arrived(k, [block], sems)
    proj[0] = nn(normed[...], block[k, :, : 3 * inner]).astype(BF16)
    lane = lax.broadcasted_iota(jnp.int32, logsum.shape, 1)
    for h in range(heads):
        own_lanes = slice(h * HD, (h + 1) * HD)
        queries = proj[0, :, own_lanes] * jnp.asarray(HD**-0.5, BF16)
        keys = proj[0, :, inner + h * HD : inner + (h + 1) * HD]
        values = proj[0, :, 2 * inner + h * HD : 2 * inner + (h + 1) * HD]
        scores = nt(queries, keys)
        top = jnp.max(scores, axis=-1, keepdims=True)
        powers = jnp.exp(scores - top)
        total = jnp.sum(powers, axis=-1, keepdims=True)
        logsum[...] = jnp.where(lane == k * heads + h, top + jnp.log(total), logsum[...])
        weights = (powers * (1.0 / total)).astype(BF16)
        mixed[0, :, own_lanes] = nn(weights, values).astype(BF16)
    middle[...] += nt(mixed[0], block[k, :, 3 * inner :]).astype(BF16).astype(F32)


def attention_forward(spot, x, gain, bias, own, pieces, n_t):
    length, width = x.shape
    inner = own.shape[1] // 4
    count = len(pieces.arrays)
    out = [
        jax.ShapeDtypeStruct((length, width), F32),
        jax.ShapeDtypeStruct((length, width), BF16),
        jax.ShapeDtypeStruct((n_t, length, 3 * inner), BF16),
        jax.ShapeDtypeStruct((length, 128), F32),
        jax.ShapeDtypeStruct((n_t, length, inner), BF16),
    ]
    return pl.pallas_call(
        functools.partial(attention_forward_kernel, pieces.plan, count),
        grid=(n_t,),
        out_shape=out,
        in_specs=[smem_spec(), whole((length, width)), whole((1, width)), whole((1, width))] + [any_spec()] * (1 + count),
        out_specs=[
            whole((length, width)),
            whole((length, width)),
            per_quarter((length, 3 * inner)),
            whole((length, 128)),
            per_quarter((length, inner)),
        ],
        scratch_shapes=[pltpu.VMEM((n_t,) + own.shape, BF16), pltpu.SemaphoreType.DMA((n_t,))],
        compiler_params=params(),
        cost_estimate=KERNEL_COST,
        name="attention_forward",
    )(spot, x, gain, bias, own, *pieces.arrays)


def mlp_forward_kernel(kept_rows, plan, count, spot_ref, x, gain, bias, own_up, own_down, *rest):
    out, normed, upward, ups, downs, total, sems = rest[count:]
    k = pl.program_id(0)

    @pl.when(k == 0)
    def _():
        fetch(spot_ref[0], [own_up, own_down], plan, rest[:count], [ups, downs], sems, range(ups.shape[0]))
        norm_rows(x, gain, bias, normed)
        total[...] = x[...]

    arrived(k, [ups, downs], sems)
    up = nn(normed[...], ups[k])
    upward[0] = up[:kept_rows]
    active = gelu(up).astype(BF16)
    total[...] += nn(active, downs[k]).astype(BF16).astype(F32)

    @pl.when(k == pl.num_programs(0) - 1)
    def _():
        out[...] = total[...].astype(out.dtype)


def mlp_forward(spot, x, gain, bias, own, pieces, n_t, kept_rows, out_type):
    length, width = x.shape
    hidden = own[0].shape[1]
    count = len(pieces.arrays)
    out = [
        jax.ShapeDtypeStruct((length, width), out_type),
        jax.ShapeDtypeStruct((length, width), BF16),
        jax.ShapeDtypeStruct((n_t, kept_rows, hidden), F32),
    ]
    return pl.pallas_call(
        functools.partial(mlp_forward_kernel, kept_rows, pieces.plan, count),
        grid=(n_t,),
        out_shape=out,
        in_specs=[smem_spec(), whole((length, width)), whole((1, width)), whole((1, width))]
        + [any_spec()] * (2 + count),
        out_specs=[whole((length, width)), whole((length, width)), per_quarter((kept_rows, hidden))],
        scratch_shapes=[
            pltpu.VMEM((n_t,) + own[0].shape, BF16),
            pltpu.VMEM((n_t,) + own[1].shape, BF16),
            pltpu.VMEM((length, width), F32),
            pltpu.SemaphoreType.DMA((n_t,)),
        ],
        compiler_params=params(),
        cost_estimate=KERNEL_COST,
        name="mlp_forward",
    )(spot, x, gain, bias, *own, *pieces.arrays)


def mlp_backward_kernel(quarters, last, blocks, plan, count, spot_ref, incoming, x, gain, normed, upward, total_in, *rest):
    own, sources = rest[:2], rest[2 : 2 + count]
    rest = list(rest[2 + count :])
    total = rest.pop(0)
    if last:
        grad, gain_grad, bias_grad = (rest.pop(0) for _ in range(3))
    if blocks:
        keep, send = rest.pop(0), rest.pop(0)
    ups, downs, sems, *flipped = rest
    k = pl.program_id(0)

    @pl.when(k == 0)
    def _():
        fetch(spot_ref[0], own, plan, sources, [ups, downs], sems, quarters)
        total[...] = jnp.zeros_like(total) if quarters[0] == 0 else total_in[...]
        if blocks:
            flip(spot_ref[0], incoming[...], flipped[0])
            flip(spot_ref[0], normed[...], flipped[1])

    arrived(k, [ups, downs], sems)
    up = upward[0]
    grad_active = nt(incoming[...].astype(BF16), downs[k])
    bell = 0.5 * (1.0 + lax.erf(up * ROOT_HALF))
    grad_up = (grad_active * (bell + up * jnp.exp(-0.5 * up * up) * (1.0 / ROOT_TWO_PI))).astype(BF16)
    total[...] += nt(grad_up, ups[k])
    if blocks:
        put_block(nn(flipped[0][...], (up * bell).astype(BF16)), keep, send, 0)
        put_block(nn(flipped[1][...], grad_up), keep, send, 1)

    if last:

        @pl.when(k == pl.num_programs(0) - 1)
        def _():
            gain_grad[...] = jnp.zeros_like(gain_grad)
            bias_grad[...] = jnp.zeros_like(bias_grad)
            for r in range(0, x.shape[0], 16):
                rows = slice(r, r + 16)
                grad[rows, :] = incoming[rows, :] + norm_back_rows(rows, x, gain, total, gain_grad, bias_grad)


def mlp_backward(spot, incoming, x, gain, normed, upward, total, own, pieces, quarters, blocks):
    length, width = incoming.shape
    n_t, hidden = upward.shape[0], upward.shape[2]
    last = quarters[-1] == n_t - 1
    count = len(quarters)
    if total is None:
        total = jnp.zeros((8, 128), F32)
    out = [jax.ShapeDtypeStruct((length, width), F32)]
    out_specs = [whole((length, width))]
    if last:
        out += [jax.ShapeDtypeStruct(v, F32) for v in ((length, width), (1, width), (1, width))]
        out_specs += [whole((length, width)), whole((1, width)), whole((1, width))]
    scratch = [
        pltpu.VMEM((count,) + own[0].shape, BF16),
        pltpu.VMEM((count,) + own[1].shape, BF16),
        pltpu.SemaphoreType.DMA((count,)),
    ]
    if blocks:
        out += block_shapes(count, 2, width // GROUP, hidden)
        out_specs += block_specs(2, width // GROUP, hidden)
        scratch += [pltpu.VMEM((width, length), BF16)] * 2
    return pl.pallas_call(
        functools.partial(mlp_backward_kernel, quarters, last, blocks, pieces.plan, len(pieces.arrays)),
        grid=(count,),
        out_shape=out,
        in_specs=[
            smem_spec(),
            whole((length, width)),
            whole((length, width)),
            whole((1, width)),
            whole((length, width)),
            per_quarter((length, hidden), quarters[0]),
            whole(total.shape),
        ]
        + [any_spec()] * (2 + len(pieces.arrays)),
        out_specs=out_specs,
        scratch_shapes=scratch,
        compiler_params=params(),
        cost_estimate=KERNEL_COST,
        name="mlp_backward",
    )(spot, incoming, x, gain, normed, upward, total, *own, *pieces.arrays)


def attention_backward_kernel(
    quarters, last, plan, count, spot_ref, incoming, x, gain, normed, proj, logsum, mixed, total_in, own, *rest
):
    sources = rest[:count]
    rest = list(rest[count:])
    total = rest.pop(0)
    if last:
        grad, gain_grad, bias_grad = (rest.pop(0) for _ in range(3))
    keep, send, block, grad_proj, sems, low_t, normed_t = rest
    k = pl.program_id(0)
    top = incoming.shape[0]
    inner = mixed.shape[-1]
    heads = inner // HD

    @pl.when(k == 0)
    def _():
        fetch(spot_ref[0], [own], plan, sources, [block], sems, quarters)
        total[...] = jnp.zeros_like(total) if quarters[0] == 0 else total_in[...]
        grad_proj[...] = jnp.zeros_like(grad_proj)
        flip(spot_ref[0], incoming[...], low_t)
        flip(spot_ref[0], normed[...], normed_t)

    arrived(k, [block], sems)
    grad_mixed = nn(incoming[...].astype(BF16), block[k, :, 3 * inner :]).astype(BF16)
    lane = lax.broadcasted_iota(jnp.int32, (top, 128), 1)
    for h in range(heads):
        own_lanes = slice(h * HD, (h + 1) * HD)
        key_lanes = slice(inner + h * HD, inner + (h + 1) * HD)
        value_lanes = slice(2 * inner + h * HD, 2 * inner + (h + 1) * HD)
        queries = proj[0, :top, own_lanes] * jnp.asarray(HD**-0.5, BF16)
        keys = proj[0, :, key_lanes]
        values = proj[0, :, value_lanes]
        head_grad = grad_mixed[:, own_lanes]
        at = lane == (quarters[0] + k) * heads + h
        row_sum = jnp.sum(jnp.where(at, logsum[:top, :], 0.0), axis=-1, keepdims=True)
        weights = jnp.exp(nt(queries, keys) - row_sum)
        grad_weights = nt(head_grad, values)
        inner_sum = jnp.sum(weights * grad_weights, axis=-1, keepdims=True)
        grad_scores = (weights * (grad_weights - inner_sum)).astype(BF16)
        grad_proj[:top, own_lanes] = (nn(grad_scores, keys) * HD**-0.5).astype(BF16)
        grad_proj[:, key_lanes] = tn(grad_scores, queries).astype(BF16)
        grad_proj[:, value_lanes] = tn(weights.astype(BF16), head_grad).astype(BF16)
    total[...] += nt(grad_proj[...], block[k, :, : 3 * inner])
    put_block(nn(normed_t[...], grad_proj[...]), keep, send, 0, slice(0, 3 * inner))
    put_block(nn(low_t[...], mixed[0, :top, :]), keep, send, 0, slice(3 * inner, 4 * inner))

    if last:

        @pl.when(k == pl.num_programs(0) - 1)
        def _():
            gain_grad[...] = jnp.zeros_like(gain_grad)
            bias_grad[...] = jnp.zeros_like(bias_grad)
            for r in range(0, x.shape[0], 16):
                rows = slice(r, r + 16)
                back = norm_back_rows(rows, x, gain, total, gain_grad, bias_grad)
                grad[rows, :] = back + incoming[rows, :] if r < top else back


def attention_backward(spot, incoming, x, gain, normed, proj, logsum, mixed, total, own, pieces, quarters):
    length, width = x.shape
    top = incoming.shape[0]
    n_t = proj.shape[0]
    last = quarters[-1] == n_t - 1
    count = len(quarters)
    inner = own.shape[1] // 4
    if total is None:
        total = jnp.zeros((8, 128), F32)
    out = [jax.ShapeDtypeStruct((length, width), F32)]
    out_specs = [whole((length, width))]
    if last:
        out += [jax.ShapeDtypeStruct(v, F32) for v in ((length, width), (1, width), (1, width))]
        out_specs += [whole((length, width)), whole((1, width)), whole((1, width))]
    out += block_shapes(count, 1, width // GROUP, 4 * inner)
    out_specs += block_specs(1, width // GROUP, 4 * inner)
    return pl.pallas_call(
        functools.partial(attention_backward_kernel, quarters, last, pieces.plan, len(pieces.arrays)),
        grid=(count,),
        out_shape=out,
        in_specs=[
            smem_spec(),
            whole((top, width)),
            whole((length, width)),
            whole((1, width)),
            whole((length, width)),
            per_quarter((length, 3 * inner), quarters[0]),
            whole((length, 128)),
            per_quarter((length, inner), quarters[0]),
            whole(total.shape),
        ]
        + [any_spec()] * (1 + len(pieces.arrays)),
        out_specs=out_specs,
        scratch_shapes=[
            pltpu.VMEM((count,) + own.shape, BF16),
            pltpu.VMEM((length, 3 * inner), BF16),
            pltpu.SemaphoreType.DMA((count,)),
            pltpu.VMEM((width, top), BF16),
            pltpu.VMEM((width, length), BF16),
        ],
        compiler_params=params(),
        cost_estimate=KERNEL_COST,
        name="attention_backward",
    )(spot, incoming, x, gain, normed, proj, logsum, mixed, total, own, *pieces.arrays)


def swap(values, bit, size):
    return lax.ppermute(values, "dp", [(i, i ^ bit) for i in range(size)])


def shift(values, size):
    return lax.ppermute(values, "tensor", [(i, (i + 1) % size) for i in range(size)])


def after(values, *others):
    return lax.optimization_barrier((values, others))[0]


def small_call(kernel, grid, in_specs, out_specs, out_shape, name):
    return pl.pallas_call(
        kernel,
        grid=grid,
        in_specs=in_specs,
        out_specs=out_specs,
        out_shape=out_shape,
        compiler_params=params(SMALL_VMEM),
        cost_estimate=SMALL_COST,
        name=name,
    )


def pack_kernel(*refs):
    count = refs[-1].shape[0]
    sources, targets = refs[:count], refs[count:]
    rows = targets[0].shape[1]
    for k, source in enumerate(sources):
        for m, target in enumerate(targets):
            target[k] = source[m * rows : (m + 1) * rows, :]


def pack(sources, matrices):
    rows, width = sources[0].shape
    shape = (len(sources), rows // matrices, width)
    return small_call(
        pack_kernel,
        (1,),
        [whole((rows, width))] * len(sources),
        [whole(shape)] * matrices,
        [jax.ShapeDtypeStruct(shape, BF16)] * matrices,
        "pack",
    )(*sources)


def hops(part, n_t):
    out = []
    for _ in range(n_t - 1):
        part = shift(part, n_t)
        out.append(part)
    return out


def corner(x_piece, y_piece, n_dp, by_x):
    return swap(y_piece, 2, n_dp) if by_x else swap(x_piece, 4, n_dp)


def with_core(planes, n_dp):
    return [v for plane in planes for v in (plane, swap(plane, 1, n_dp))]


def at_plane(i, shape):
    return pl.BlockSpec((1, 1) + shape, lambda k: (i, k) + (0,) * len(shape))


def corner_kernel(kept, got, out):
    out[...] = (kept[0, 0].astype(F32) + got[0, 0].astype(F32)).astype(BF16)[None]


def sides_kernel(half, kx, gx, ky, gy, ca, cb, x_out, y_out):
    k = pl.program_id(0)
    x = kx[0, 0].astype(F32) + gx[0, 0].astype(F32)
    y = ky[0, 0].astype(F32) + gy[0, 0].astype(F32)
    a, b = ca[0].astype(F32), cb[0].astype(F32)
    x_out[0] = jnp.where(k < half, x, x + b).astype(BF16)
    y_out[0] = jnp.where(k < half, y + a, y).astype(BF16)


def mine_kernel(kept, got, fx, fy, out):
    total = kept[0, 0].astype(F32) + got[0, 0].astype(F32)
    out[0] = (total + fx[0].astype(F32) + fy[0].astype(F32)).astype(out.dtype)


def last_kernel(*refs):
    *parts, out = refs
    total = parts[0][...].astype(F32)
    for part in parts[1:]:
        total = total + part[...].astype(F32)
    out[...] = total


class Reduction:
    def __init__(self, keep, send, quarters, n_dp, n_t):
        self.keep, self.quarters, self.n_dp, self.n_t = keep, quarters, n_dp, n_t
        self.shape = keep.shape[2:]
        self.count = len(quarters)
        self.half = self.count // 2
        self.got = swap(send, 1, n_dp)
        self.stage = 0

    def spec(self, first=0, top=None):
        top = self.count - 1 if top is None else top
        shape = self.shape
        return pl.BlockSpec((1,) + shape, lambda k: (jnp.clip(k - first, 0, top),) + (0,) * len(shape))

    def corners(self, token):
        self.got = after(self.got, token)
        outs = []
        for first, bit in ((0, 2), (self.half, 4)):
            shape = self.shape
            spec = pl.BlockSpec((1, 1) + shape, lambda k, first=first: (3, first + k) + (0,) * len(shape))
            outs.append(
                small_call(
                    corner_kernel,
                    (self.half,),
                    [spec, spec],
                    pl.BlockSpec((1,) + shape, lambda k: (k,) + (0,) * len(shape)),
                    jax.ShapeDtypeStruct((self.half,) + shape, BF16),
                    "corner_sum",
                )(self.keep, self.got)
            )
        self.corner_a, self.corner_b = swap(outs[0], 2, self.n_dp), swap(outs[1], 4, self.n_dp)
        return outs

    def sides(self, token):
        self.corner_a, self.corner_b = after((self.corner_a, self.corner_b), token)
        full = jax.ShapeDtypeStruct((self.count,) + self.shape, BF16)
        x, y = small_call(
            functools.partial(sides_kernel, self.half),
            (self.count,),
            [at_plane(1, self.shape)] * 2
            + [at_plane(2, self.shape)] * 2
            + [self.spec(0, self.half - 1), self.spec(self.half, self.half - 1)],
            [self.spec()] * 2,
            [full, full],
            "side_sum",
        )(self.keep, self.got, self.keep, self.got, self.corner_a, self.corner_b)
        self.from_x, self.from_y = swap(x, 2, self.n_dp), swap(y, 4, self.n_dp)
        return [x, y]

    def quarters_out(self, token):
        self.from_x, self.from_y = after((self.from_x, self.from_y), token)
        self.parts, outs = [], []
        for i, k in enumerate(self.quarters):
            shape = self.shape
            plane = pl.BlockSpec((1, 1) + shape, lambda _, i=i: (0, i) + (0,) * len(shape))
            side = pl.BlockSpec((1,) + shape, lambda _, i=i: (i,) + (0,) * len(shape))
            part = small_call(
                mine_kernel,
                (1,),
                [plane, plane, side, side],
                whole((1,) + shape),
                jax.ShapeDtypeStruct((1,) + shape, F32 if k == 0 else BF16),
                "own_sum",
            )(self.keep, self.got, self.from_x, self.from_y)
            outs.append(part)
            if k:
                part = lax.ppermute(part, "tensor", [(j, (j - k) % self.n_t) for j in range(self.n_t)])
            self.parts.append(part)
        return outs


def finish(parts, n_dp):
    shape = parts[0].shape
    total = small_call(
        last_kernel, (1,), [whole(shape)] * len(parts), whole(shape), jax.ShapeDtypeStruct(shape, F32), "last_sum"
    )(*parts)
    return [spread_rows(total[0, m], n_dp) for m in range(shape[1])]


def spread_rows(total, n_dp):
    groups = n_dp // GROUP
    me = lax.axis_index("dp")
    rows = total.shape[0]
    bit = n_dp // 2
    while bit >= GROUP:
        rows //= 2
        second = (me // bit) % 2
        kept = lax.dynamic_slice_in_dim(total, second * rows, rows, 0)
        sent = lax.dynamic_slice_in_dim(total, (1 - second) * rows, rows, 0)
        total = kept + swap(sent, bit, n_dp)
        bit //= 2
    if groups > 1:
        total = lax.ppermute(
            total, "dp", [(h * GROUP + s, s * groups + h) for h in range(groups) for s in range(GROUP)]
        )
    return total


def sum_all(values, n_dp, n_t):
    bit = 1
    while bit < n_dp:
        values = values + swap(values, bit, n_dp)
        bit *= 2
    bit = 1
    while bit < n_t:
        values = values + lax.ppermute(values, "tensor", [(i, i ^ bit) for i in range(n_t)])
        bit *= 2
    return values


def shards(tokens, type_table, norm_gain, norm_bias, w_qkv, w_out, w_up, w_down, cotangent, positions, n_dp, n_t):
    total_rows, width = tokens.shape
    pair_count, slots = positions.shape
    assert pair_count == n_t
    length = total_rows // pair_count
    layers = w_qkv.shape[0]
    top = layers - 1
    inner = w_qkv.shape[3]
    me, quarter = lax.axis_index("dp"), lax.axis_index("tensor")
    rows = width // GROUP
    unit = width // n_dp
    spot = me % GROUP
    spots = jnp.reshape(spot, (1,)).astype(jnp.int32)

    def part_of(block):
        return lax.dynamic_slice_in_dim(block, spot * rows, rows, 0)

    mine = lax.dynamic_slice_in_dim(tokens, quarter * length, length, 0).astype(F32)
    row_ids = lax.broadcasted_iota(jnp.int32, (length, 1), 0)
    stream = mine + jnp.where(row_ids < WORDS, type_table[0], type_table[1])
    gains = [[norm_gain[l, i][None] for i in range(2)] for l in range(layers)]
    biases = [[norm_bias[l, i][None] for i in range(2)] for l in range(layers)]
    own = [jnp.concatenate([w_qkv[l].reshape(width, 3 * inner), w_out[l].T], 1) for l in range(layers)]

    def attn_part(l):
        left = lax.dynamic_slice(w_qkv, (l, spot * rows, 0, 0), (1, rows, 3, inner)).reshape(rows, 3 * inner)
        right = lax.dynamic_slice(w_out, (l, 0, spot * rows), (1, inner, rows))[0].T
        return jnp.concatenate([left, right], 1)

    def mlp_part(l):
        return jnp.concatenate(
            [lax.dynamic_slice(w, (l, spot * rows, 0), (1, rows, w.shape[2]))[0] for w in (w_up, w_down)], 0
        )

    attn_hops, mlp_hops = [], []
    token = None
    for l in range(layers):
        for part, out in ((attn_part(l), attn_hops), (mlp_part(l), mlp_hops)):
            out.append(hops(part if token is None else after(part, token), n_t))
            token = out[-1][-2]

    def by_hop(held, matrices):
        at = [[] for _ in range(matrices)]
        for k, v in enumerate(held):
            x_piece, y_piece = swap(v, 2, n_dp), swap(v, 4, n_dp)
            slices = with_core([v, x_piece, y_piece, corner(x_piece, y_piece, n_dp, k % 2 == 1)], n_dp)
            for m in range(matrices):
                at[m].append([(piece, None, m * rows) for piece in slices])
        return Pieces(at)

    def at_once(packed, token_of, first):
        sides = [(v, swap(v, 2, n_dp), swap(v, 4, n_dp)) for v in packed]
        token = token_of(after(first, *packed))
        at = []
        for m, (v, x_piece, y_piece) in enumerate(sides):
            x_piece, y_piece = after((x_piece, y_piece), token[0])
            slices = with_core([v, x_piece, y_piece, corner(x_piece, y_piece, n_dp, m % 2 == 1)], n_dp)
            at.append([[(piece, k, 0) for piece in slices] for k in range(n_t - 1)])
        return Pieces(at), token

    attn_pieces, mlp_pieces, saved = [by_hop(attn_hops[0], 1)], [], []
    for l in range(layers):
        pieces, (middle, normed, proj, logsum, mixed) = at_once(
            pack(mlp_hops[l], 2),
            lambda x: attention_forward(spots, x, gains[l][0], biases[l][0], own[l], attn_pieces[l], n_t),
            stream,
        )
        mlp_pieces.append(pieces)

        def feed_forward(x):
            return mlp_forward(
                spots, x, gains[l][1], biases[l][1], (w_up[l], w_down[l]), pieces, n_t,
                TOP_ROWS if l == top else length, BF16 if l == top else F32,
            )

        if l < top:
            pieces, (following, normed_mlp, upward) = at_once(pack(attn_hops[l + 1], 1), feed_forward, middle)
            attn_pieces.append(pieces)
        else:
            following, normed_mlp, upward = feed_forward(middle)
        saved.append((stream, normed, proj, logsum, mixed, middle, normed_mlp, upward))
        stream = following

    def put_pairs(held):
        out = jnp.zeros((total_rows, width), F32)
        for k, v in enumerate(held):
            out = lax.dynamic_update_slice(out, v.astype(F32), (((quarter - k) % n_t) * length, 0))
        return out

    hidden = [stream]

    place = lax.dynamic_slice_in_dim(positions, quarter, 1, 0)[0]
    cot = lax.dynamic_slice_in_dim(cotangent, quarter, 1, 0)[0]
    onehot = (row_ids[:TOP_ROWS] == place[None, :]).astype(BF16)
    incoming = nn(onehot, cot)

    top_normed = saved[top][6][:TOP_ROWS]
    slot_rows = tn(onehot, top_normed).astype(BF16)
    slot_cot = jnp.where(place[:, None] >= 0, cot, 0)
    spare = jnp.zeros((SLOT_ROWS - slots, width), BF16)
    masked = [jnp.concatenate([slot_cot, spare, slot_rows, spare], 0)[None]]

    everything = tuple(range(n_t))
    halves = (everything[: n_t // 2], everything[n_t // 2 :])
    gain_grads = [[None, None] for _ in range(layers)]
    bias_grads = [[None, None] for _ in range(layers)]
    attn_sums, mlp_sums = [None] * layers, [None] * layers
    pending = []

    def advance(token):
        outs = []
        for reduction in pending:
            outs += (reduction.corners, reduction.sides, reduction.quarters_out)[reduction.stage](token)
            reduction.stage += 1
        pending[:] = [r for r in pending if r.stage < 3]
        for held in (hidden, masked):
            if len(held) > 1:
                held[-1] = after(held[-1], token)
                outs.append(held[-1])
            if len(held) < n_t:
                held.append(shift(held[-1], n_t))
        return outs

    ready = advance(incoming)
    for l in range(top, -1, -1):
        stream_l, normed, proj, logsum, mixed, middle, normed_mlp, upward = saved[l]
        part = slice(0, incoming.shape[0])
        total = None
        mlp_sums[l] = []
        for quarters in [everything] if l == top else halves:
            outs = mlp_backward(
                spots, after(incoming, ready), middle[part], gains[l][1], normed_mlp[part], upward, total,
                (w_up[l], w_down[l]), mlp_pieces[l], quarters, l < top,
            )
            total = outs[0]
            ready = advance(total)
            if l < top:
                mlp_sums[l].append(Reduction(outs[-2], outs[-1], quarters, n_dp, n_t))
                pending.append(mlp_sums[l][-1])
        incoming, gain_grads[l][1], bias_grads[l][1] = outs[1:4]
        total = None
        attn_sums[l] = []
        for quarters in [everything] if l == top else halves:
            outs = attention_backward(
                spots, after(incoming, ready), stream_l, gains[l][0], normed, proj, logsum, mixed, total,
                own[l], attn_pieces[l], quarters,
            )
            total = outs[0]
            ready = advance(total)
            attn_sums[l].append(Reduction(outs[-2], outs[-1], quarters, n_dp, n_t))
            pending.append(attn_sums[l][-1])
        incoming, gain_grads[l][0], bias_grads[l][0] = outs[1:4]
    tokens_held = [incoming.astype(BF16)]
    tokens_held += hops(tokens_held[0], n_t)
    while pending:
        ready = advance(ready)

    all_rows = jnp.concatenate(masked, 0)
    bit = 2
    while bit < 2 * n_dp:
        all_rows = jnp.concatenate([all_rows, swap(all_rows, bit if bit < n_dp else 1, n_dp)], 0)
        bit *= 2
    all_cot = all_rows[:, :SLOT_ROWS].reshape(-1, width)
    all_normed = all_rows[:, SLOT_ROWS:].reshape(-1, width)
    slot_up = nn(all_normed, w_up[top])
    slot_grad = (nt(all_cot, w_down[top]) * gelu_slope(slot_up)).astype(BF16)
    grad_up_top = tn(lax.dynamic_slice_in_dim(all_normed, me * unit, unit, 1), slot_grad)
    grad_down_top = tn(
        gelu(slot_up).astype(BF16), lax.dynamic_slice_in_dim(all_cot, me * unit, unit, 1)
    )

    def finished(reductions):
        return finish([p for r in reductions for p in r.parts], n_dp)

    sums = {}
    for l in range(layers):
        (sums["attn", l],) = finished(attn_sums[l])
        if l < top:
            sums["down", l], sums["up", l] = finished(mlp_sums[l])

    hidden_out, grad_tokens = put_pairs(hidden), put_pairs(tokens_held)
    type_grad = jnp.stack([jnp.sum(incoming[:WORDS], 0), jnp.sum(incoming[WORDS:], 0)])
    rows_all = jnp.concatenate(
        [type_grad] + [g for pair in gain_grads for g in pair] + [b for pair in bias_grads for b in pair], 0
    )
    rows_all = sum_all(rows_all, n_dp, n_t)
    rows_mine = lax.dynamic_slice_in_dim(rows_all, me * unit, unit, 1)
    grad_gain = rows_mine[2 : 2 + 2 * layers].reshape(layers, 2, unit)
    grad_bias = rows_mine[2 + 2 * layers :].reshape(layers, 2, unit)
    grad_qkv = jnp.stack([sums["attn", l][:, : 3 * inner].reshape(unit, 3, inner) for l in range(layers)])
    grad_out = jnp.stack([sums["attn", l][:, 3 * inner :].T for l in range(layers)])
    grad_up = jnp.stack([grad_up_top if l == top else sums["up", l] for l in range(layers)])
    grad_down = jnp.stack([grad_down_top if l == top else sums["down", l].T for l in range(layers)])
    return hidden_out, grad_tokens, rows_mine[:2], grad_gain, grad_bias, grad_qkv, grad_out, grad_up, grad_down


def solution(mesh):
    n_dp, n_t = mesh.shape["dp"], mesh.shape["tensor"]
    placed = (
        P("dp", None),
        P(),
        P(),
        P(),
        P(None, None, None, "tensor"),
        P(None, "tensor", None),
        P(None, None, "tensor"),
        P(None, "tensor", None),
        P("dp", None, None),
        P("dp", None),
    )

    def run(*args):
        return shards(*args, n_dp, n_t)

    return jax.shard_map(
        run,
        mesh=mesh,
        in_specs=placed,
        out_specs=(
            P("dp", None),
            P("dp", None),
            P(None, "dp"),
            P(None, None, "dp"),
            P(None, None, "dp"),
            P(None, "dp", None, "tensor"),
            P(None, "tensor", "dp"),
            P(None, "dp", "tensor"),
            P(None, "tensor", "dp"),
        ),
        check_vma=False,
    )
```

time: 802 us -> 445 us (0.55)
  Pallas kernels: 423 us -> 117 us
  other arithmetic: 54.4 us -> 15.3 us
  starting transfers between devices: 108 us -> 83 us
  waiting for transfers between devices: 150 us -> 164 us
    pallas_call x20 -> x43, Pallas kernels: 423 us -> 117 us  [the longest x3 35.2 us: attention_backward(): pl.pallas_call(functools.partial(attention_backward_kernel, quarters, las...]
    ppermute x0 -> x9, waiting for transfers between devices: none -> 30.1 us  [quarters_out(): lax.ppermute(part, 'tensor', [(j, (j - k) % self.n_t) for j in range(self...]
    ppermute x94 -> x87, starting transfers between devices: 83.4 us -> 54.6 us  [swap(): return lax.ppermute(values, 'dp', [(i, i ^ bit) for i in range(size)])]
    convert_element_type x20 -> x0, other arithmetic: 25.8 us -> none  [the longest x8 8.24 us: reduce_blocks(): total = shift(total.astype(BF16), n_t).astype(F32) + mine(k)]
    slice x26 -> x0, local copies, waits for them, and re-layouts: 16.6 us -> none  [the longest x12 6.38 us: gather_blocks(): corner_b = swap(along_y[half:], 2, n_dp)]
    ppermute x0 -> x9, starting transfers between devices: none -> 9.41 us  [quarters_out(): lax.ppermute(part, 'tensor', [(j, (j - k) % self.n_t) for j in range(self...]
    ppermute x33 -> x21, waiting for transfers between devices: 55.3 us -> 47.1 us  [shift(): lax.ppermute(values, 'tensor', [(i, (i + 1) % size) for i in range(size)])]
    ppermute x33 -> x21, starting transfers between devices: 23.9 us -> 16.2 us  [shift(): lax.ppermute(values, 'tensor', [(i, (i + 1) % size) for i in range(size)])]
  transfers between devices with their start and end apart: 129 -> 119, of which waited for: 48 -> 39; matrix products, arithmetic and copies ran while one was open for 11% -> 10% of each run, Pallas kernels for 46% -> 25%
where the time goes in v1:
time: 445 us; the launch traced here: 437 us
  waiting for transfers between devices  164 us (37%)
  Pallas kernels  117 us (26%)
  starting transfers between devices  83 us (19%)
  local copies, waits for them, and re-layouts  47.6 us (11%)
  other arithmetic  15.3 us (3%)
  matrix products  7.12 us (2%)
    ppermute x87, waiting for transfers between devices, swap(): return lax.ppermute(values, 'dp', [(i, i ^ bit) for i in range(size)])  80.5 us
    ppermute x87, starting transfers between devices, swap(): return lax.ppermute(values, 'dp', [(i, i ^ bit) for i in range(size)])  54.6 us
    ppermute x21, waiting for transfers between devices, shift(): lax.ppermute(values, 'tensor', [(i, (i + 1) % size) for i in range(size)])  47.1 us
    pallas_call x3, Pallas kernels, attention_backward(): pl.pallas_call(functools.partial(attention_backward_kernel, quarters, las...  35.2 us
    ppermute x9, waiting for transfers between devices, quarters_out(): lax.ppermute(part, 'tensor', [(j, (j - k) % self.n_t) for j in range(self...  30.1 us
    pallas_call x3, Pallas kernels, mlp_backward(): pl.pallas_call(functools.partial(mlp_backward_kernel, quarters, last, blo...  25.6 us
    unnamed x184, local copies, waits for them, and re-layouts  19.4 us
    pallas_call x2, Pallas kernels, attention_forward(): pl.pallas_call(functools.partial(attention_forward_kernel, pieces.plan, c...  17.8 us
  transfers between devices with their start and end apart: 119, of which 39 were waited for; matrix products, arithmetic and copies ran while one was open for 10% of the time, Pallas kernels for 25%

profile of v1, /device:TPU:0, one launch (start us, length us, event | category | flops | bytes accessed | tf_op | source)
XLA Modules:
  0.0 436.8 jit_solution(2445680355275496212)
XLA Ops:
  3.3 3.1 collective-permute-start
  6.4 2.5 fusion.31
  8.8 3.4 collective-permute-done.rest_0_
  17.0 2.2 collective-permute-done.1.rest_8_
  24.2 7.6 %collective-permute-done.19.rest_16_ = bf16[96,768]{1,0:T(8,128)(2,1)} collective-permute-done((bf16[96,768]{1,0:T(8,128)(2,1)S(1)}, bf16[96,768]{1,0:T(8,128)(2,1)}, u32[]{:S(2)}, u32[]{:S(2)}) %collective-permute-start.19) | collective-permute-done | bytes 147488 | tf_op jit(solution)/shard_map/ppermute | solution.py:465
  35.4 3.9 collective-permute-done.21.rest_18_
  47.1 3.7 collective-permute-done.25.rest_22_
  50.8 6.5 %collective-permute-done.27.refs_0_ = bf16[96,768]{1,0:T(8,128)(2,1)S(1)} collective-permute-done((bf16[96,768]{1,0:T(8,128)(2,1)S(1)}, bf16[96,768]{1,0:T(8,128)(2,1)S(1)}, u32[]{:S(2)}, u32[]{:S(2)}) %collective-permute-start.27) | collective-permute-done | bytes 147488 | tf_op jit(solution)/shard_map/ppermute | solution.py:465
  58.7 6.7 %collective-permute-done.28.refs_1_ = bf16[96,768]{1,0:T(8,128)(2,1)S(1)} collective-permute-done((bf16[96,768]{1,0:T(8,128)(2,1)S(1)}, bf16[96,768]{1,0:T(8,128)(2,1)S(1)}, u32[]{:S(2)}, u32[]{:S(2)}) %collective-permute-start.28) | collective-permute-done | bytes 147488 | tf_op jit(solution)/shard_map/ppermute | solution.py:465
  69.5 8.9 %attention_forward.2 = (f32[256,768]{1,0:T(8,128)}, bf16[256,768]{1,0:T(8,128)(2,1)}, bf16[4,256,576]{2,1,0:T(8,128)(2,1)}, f32[256,128]{1,0:T(8,128)}, bf16[4,256,192]{2,1,0:T(8,128)(2,1)}) custom-call(s32[1]{0:T(128)} %bitcast.spot_ref, f32[256,768]{1,0:T(8,128)} %select_add_fusion.x, f32[1,768]{1,0:T(1,128)} %get-tuple-element.327.gain, ...), custom_call_target="tpu_custom_call" | custom-call | flops 40000000000 | bytes 1000000 | tf_op jit(solution)/shard_map/attention_forward/pallas_call | solution.py:205
  79.9 6.9 %collective-permute-done.31.rest_2_.rest_4_ = bf16[3,96,768]{2,1,0:T(8,128)(2,1)S(1)} collective-permute-done((bf16[3,96,768]{2,1,0:T(8,128)(2,1)S(1)}, bf16[3,96,768]{2,1,0:T(8,128)(2,1)S(1)}, u32[]{:S(2)}, u32[]{:S(2)}) %collective-permute-start.31) | collective-permute-done | bytes 442400 | tf_op jit(solution)/shard_map/ppermute | solution.py:461
  89.5 8.1 %collective-permute-done.42.rest_14_.rest_16_ = bf16[3,96,768]{2,1,0:T(8,128)(2,1)S(1)} collective-permute-done((bf16[3,96,768]{2,1,0:T(8,128)(2,1)S(1)}, bf16[3,96,768]{2,1,0:T(8,128)(2,1)S(1)}, u32[]{:S(2)}, u32[]{:S(2)}) %collective-permute-start.42) | collective-permute-done | bytes 442400 | tf_op jit(solution)/shard_map/ppermute | solution.py:461
  98.2 2.5 collective-permute-done.35.rest_6_.rest_8_
  100.7 4.7 %slice_bitcast_fusion = (bf16[768,768]{1,0:T(8,128)(2,1)}, bf16[768,768]{1,0:T(8,128)(2,1)}, bf16[768,768]{1,0:T(8,128)(2,1)}, bf16[768,768]{1,0:T(8,128)(2,1)}) fusion(bf16[2,768,768]{2,1,0:T(8,128)(2,1)} %param.17, bf16[2,768,768]{2,1,0:T(8,128)(2,1)} %param.16), kind=kLoop, calls=%fused_computation.12 | loop fusion | bytes 9437184 | tf_op jit(solution)/shard_map/squeeze | solution.py:734
  108.5 8.1 %mlp_forward.2 = (f32[256,768]{1,0:T(8,128)}, bf16[256,768]{1,0:T(8,128)(2,1)}, f32[4,256,768]{2,1,0:T(8,128)}) custom-call(s32[1]{0:T(128)} %bitcast.spot_ref, f32[256,768]{1,0:T(8,128)} %get-tuple-element.137.x, f32[1,768]{1,0:T(1,128)} %get-tuple-element.328.gain, f32[1,768]{1,0:T(1,128)} %get-tuple-element.315.bias, ...), custom_call_target="tpu_custom_call" | custom-call | flops 40000000000 | bytes 1000000 | tf_op jit(solution)/shard_map/mlp_forward/pallas_call | solution.py:254
  120.5 9.9 %collective-permute-done.52.rest_6_ = bf16[3,96,768]{2,1,0:T(8,128)(2,1)} collective-permute-done((bf16[3,96,768]{2,1,0:T(8,128)(2,1)}, bf16[3,96,768]{2,1,0:T(8,128)(2,1)}, u32[]{:S(2)}, u32[]{:S(2)}) %collective-permute-start.52) | collective-permute-done | bytes 442400 | tf_op jit(solution)/shard_map/ppermute | solution.py:461
  133.7 8.1 %collective-permute-done.46.refs_2_ = bf16[192,768]{1,0:T(8,128)(2,1)S(1)} collective-permute-done((bf16[192,768]{1,0:T(8,128)(2,1)S(1)}, bf16[192,768]{1,0:T(8,128)(2,1)S(1)}, u32[]{:S(2)}, u32[]{:S(2)}) %collective-permute-start.46) | collective-permute-done | bytes 294944 | tf_op jit(solution)/shard_map/ppermute | solution.py:465
  146.1 8.9 %attention_forward.3 = (f32[256,768]{1,0:T(8,128)}, bf16[256,768]{1,0:T(8,128)(2,1)}, bf16[4,256,576]{2,1,0:T(8,128)(2,1)}, f32[256,128]{1,0:T(8,128)}, bf16[4,256,192]{2,1,0:T(8,128)(2,1)}) custom-call(s32[1]{0:T(128)} %bitcast.spot_ref, f32[256,768]{1,0:T(8,128)} %get-tuple-element.146.x, f32[1,768]{1,0:T(1,128)} %get-tuple-element.326.gain, ...), custom_call_target="tpu_custom_call" | custom-call | flops 40000000000 | bytes 1000000 | tf_op jit(solution)/shard_map/attention_forward/pallas_call | solution.py:205
  157.1 7.4 %collective-permute-done.55.rest_2_.rest_4_ = bf16[3,96,768]{2,1,0:T(8,128)(2,1)S(1)} collective-permute-done((bf16[3,96,768]{2,1,0:T(8,128)(2,1)S(1)}, bf16[3,96,768]{2,1,0:T(8,128)(2,1)S(1)}, u32[]{:S(2)}, u32[]{:S(2)}) %collective-permute-start.55) | collective-permute-done | bytes 442400 | tf_op jit(solution)/shard_map/ppermute | solution.py:461
  167.1 5.8 %collective-permute-done.66.rest_14_.rest_16_ = bf16[3,96,768]{2,1,0:T(8,128)(2,1)} collective-permute-done((bf16[3,96,768]{2,1,0:T(8,128)(2,1)S(1)}, bf16[3,96,768]{2,1,0:T(8,128)(2,1)}, u32[]{:S(2)}, u32[]{:S(2)}) %collective-permute-start.66) | collective-permute-done | bytes 442400 | tf_op jit(solution)/shard_map/ppermute | solution.py:461
  173.4 3.9 collective-permute-done.59.rest_6_.rest_8_
  180.7 7.6 %mlp_forward.3 = (bf16[256,768]{1,0:T(8,128)(2,1)}, bf16[256,768]{1,0:T(8,128)(2,1)}, f32[4,48,768]{2,1,0:T(8,128)}) custom-call(s32[1]{0:T(128)} %bitcast.spot_ref, f32[256,768]{1,0:T(8,128)} %get-tuple-element.149.x, f32[1,768]{1,0:T(1,128)} %get-tuple-element.329.gain, f32[1,768]{1,0:T(1,128)} %get-tuple-element.314.bias, ...), custom_call_target="tpu_custom_call" | custom-call | flops 40000000000 | bytes 1000000 | tf_op jit(solution)/shard_map/mlp_forward/pallas_call | solution.py:254
  193.8 7.9 %mlp_backward.3 = (f32[48,768]{1,0:T(8,128)}, f32[48,768]{1,0:T(8,128)}, f32[1,768]{1,0:T(1,128)}, f32[1,768]{1,0:T(1,128)}) custom-call(s32[1]{0:T(128)} %bitcast.spot_ref, f32[48,768]{1,0:T(8,128)} %fusion.15.incoming, f32[48,768]{1,0:T(8,128)} %slice.130.x, f32[1,768]{1,0:T(1,128)} %get-tuple-element.329.gain, bf16[48,768]{1,0:T(8,128)(2,1)} %slice.131.normed, ...), custom_call_target="tpu_custom_call" | custom-call | flops 40000000000 | bytes 1000000 | tf_op jit(solution)/shard_map/mlp_backward/pallas_call | solution.py:334
  206.2 2.5 collective-permute-start.69
  208.6 14.7 %attention_backward.3 = (f32[256,768]{1,0:T(8,128)}, f32[256,768]{1,0:T(8,128)}, f32[1,768]{1,0:T(1,128)}, f32[1,768]{1,0:T(1,128)}, bf16[4,4,1,96,768]{4,3,2,1,...) custom-call(s32[1]{0:T(128)} %bitcast.spot_ref, f32[48,768]{1,0:T(8,128)} %get-tuple-element.161.incoming, ...), custom_call_target="tpu_custom_call" | custom-call | flops 40000000000 | bytes 1000000 | tf_op jit(solution)/shard_map/attention_backward/pallas_call | solution.py:430
  225.1 2.2 collective-permute-start.71
  227.4 8.0 %mlp_backward.4 = (f32[256,768]{1,0:T(8,128)}, bf16[4,2,2,96,768]{4,3,2,1,0:T(8,128)(2,1)}, bf16[4,2,2,96,768]{4,3,2,1,0:T(8,128)(2,1)}) custom-call(s32[1]{0:T(128)} %bitcast.spot_ref, f32[256,768]{1,0:T(8,128)} %get-tuple-element.179.incoming, f32[256,768]{1,0:T(8,128)} %get-tuple-element.137.x, f32[1,768]{1,0:T(1,128)} %get-tuple-element.328.gain, ...), custom_call_target="tpu_custom_call" | custom-call | flops 40000000000 | bytes 1000000 | tf_op jit(solution)/shard_map/mlp_backward/pallas_call | solution.py:334
  236.7 2.2 collective-permute-done.71
  243.6 9.7 %mlp_backward.5 = (f32[256,768]{1,0:T(8,128)}, f32[256,768]{1,0:T(8,128)}, f32[1,768]{1,0:T(1,128)}, f32[1,768]{1,0:T(1,128)}, bf16[4,2,2,96,768]{4,3,2,1,0:T(8,128)(2,1)}, /*index=5*/bf16[4,2,2,96,768]{4,3,2,1,0:T(8,128)(2,1)}) custom-call(s32[1]{0:T(128)} %bitcast.spot_ref, f32[256,768]{1,0:T(8,128)} %get-tuple-element.179.incoming, ...), custom_call_target="tpu_custom_call" | custom-call | flops 40000000000 | bytes 1000000 | tf_op jit(solution)/shard_map/mlp_backward/pallas_call | solution.py:334
  264.4 9.4 %attention_backward.4 = (f32[256,768]{1,0:T(8,128)}, bf16[4,2,1,96,768]{4,3,2,1,0:T(8,128)(2,1)}, bf16[4,2,1,96,768]{4,3,2,1,0:T(8,128)(2,1)}) custom-call(s32[1]{0:T(128)} %bitcast.spot_ref, f32[256,768]{1,0:T(8,128)} %get-tuple-element.208.incoming, f32[256,768]{1,0:T(8,128)} %select_add_fusion.x, f32[1,768]{1,0:T(1,128)} %get-tuple-element.327.gain, ...), custom_call_target="tpu_custom_call" | custom-call | flops 40000000000 | bytes 1000000 | tf_op jit(solution)/shard_map/attention_backward/pallas_call | solution.py:430
  273.8 6.1 %collective-permute-done.81.cb = bf16[1,2,96,768]{3,2,1,0:T(8,128)(2,1)S(1)} collective-permute-done((bf16[1,2,96,768]{3,2,1,0:T(8,128)(2,1)}, bf16[1,2,96,768]{3,2,1,0:T(8,128)(2,1)S(1)}, u32[]{:S(2)}, u32[]{:S(2)}) %collective-permute-start.81) | collective-permute-done | bytes 294944 | tf_op jit(solution)/shard_map/ppermute | solution.py:461
  281.9 2.3 collective-permute-start.111
  286.1 2.5 side_sum.6
  291.2 4.6 %collective-permute-done.111.refs_2_ = bf16[1,1,96,768]{3,2,1,0:T(8,128)(2,1)S(1)} collective-permute-done((bf16[1,1,96,768]{3,2,1,0:T(8,128)(2,1)S(1)}, bf16[1,1,96,768]{3,2,1,0:T(8,128)(2,1)S(1)}, u32[]{:S(2)}, u32[]{:S(2)}) %collective-permute-start.111) | collective-permute-done | bytes 147488 | tf_op jit(solution)/shard_map/ppermute | solution.py:619
  302.0 11.1 %attention_backward.5 = (f32[256,768]{1,0:T(8,128)}, f32[256,768]{1,0:T(8,128)}, f32[1,768]{1,0:T(1,128)}, f32[1,768]{1,0:T(1,128)}, bf16[4,2,1,96,768]{4,3,2,1,...) custom-call(s32[1]{0:T(128)} %bitcast.spot_ref, f32[256,768]{1,0:T(8,128)} %get-tuple-element.208.incoming, ...), custom_call_target="tpu_custom_call" | custom-call | flops 40000000000 | bytes 1000000 | tf_op jit(solution)/shard_map/attention_backward/pallas_call | solution.py:430
  315.2 2.6 concatenate.46
  325.0 2.3 collective-permute-start.97
  327.3 4.2 collective-permute-done.102
  334.9 3.1 collective-permute-done.103
  340.1 3.4 collective-permute-done.104
  353.8 8.8 %collective-permute-done.98 = bf16[256,768]{1,0:T(8,128)(2,1)S(1)} collective-permute-done((bf16[256,768]{1,0:T(8,128)(2,1)S(1)}, bf16[256,768]{1,0:T(8,128)(2,1)S(1)}, u32[]{:S(2)}, u32[]{:S(2)}) %collective-permute-start.98) | collective-permute-done | bytes 393248 | tf_op jit(solution)/shard_map/ppermute | solution.py:465
  367.3 2.5 collective-permute-start.114
  377.7 17.0 %collective-permute-done.114.refs_2_ = bf16[1,2,96,768]{3,2,1,0:T(8,128)(2,1)S(1)} collective-permute-done((bf16[1,2,96,768]{3,2,1,0:T(8,128)(2,1)S(1)}, bf16[1,2,96,768]{3,2,1,0:T(8,128)(2,1)S(1)}, u32[]{:S(2)}, u32[]{:S(2)}) %collective-permute-start.114) | collective-permute-done | bytes 294944 | tf_op jit(solution)/shard_map/ppermute | solution.py:619
  399.5 4.1 collective-permute-done.116
  405.4 3.5 collective-permute-done.106.fx
  409.5 5.2 %collective-permute-done.117 = bf16[8,32,768]{2,1,0:T(8,128)(2,1)S(1)} collective-permute-done((bf16[8,32,768]{2,1,0:T(8,128)(2,1)S(1)}, bf16[8,32,768]{2,1,0:T(8,128)(2,1)S(1)}, u32[]{:S(2)}, u32[]{:S(2)}) %collective-permute-start.117) | collective-permute-done | bytes 393248 | tf_op jit(solution)/shard_map/ppermute | solution.py:461
  417.6 3.9 collective-permute-done.108.refs_2_
  430.4 3.1 fusion.7
  (491 shorter events, 156.8 us)
Async XLA Ops:
  19.2 14.0 %collective-permute-start.2 = (bf16[192,768]{1,0:T(8,128)(2,1)S(1)}, bf16[192,768]{1,0:T(8,128)(2,1)S(1)}, u32[]{:S(2)}, u32[]{:S(2)}) collective-permute-start(bf16[192,768]{1,0:T(8,128)(2,1)S(1)} %pad_maximum_fusion.5), channel_id=1, source_target_pairs={{0,1},{1,2},{2,3},{3,0},{4,5},{5,6},{6,7},{7,4},{8,9},{9,10},{10,1... | collective-permute-start | bytes 884744 | tf_op jit(solution)/shard_map/ppermute | solution.py:465
  44.1 13.2 %collective-permute-start.4 = (bf16[192,768]{1,0:T(8,128)(2,1)S(1)}, bf16[192,768]{1,0:T(8,128)(2,1)S(1)}, u32[]{:S(2)}, u32[]{:S(2)}) collective-permute-start(bf16[192,768]{1,0:T(8,128)(2,1)S(1)} %collective-permute-done.3.refs_1_), channel_id=1, source_target_pairs={{0,1},{1,2},{2,3},{3,0},{4,5},{5,6},{6,7},{7,4},{8,9},{9,10},{10,1... | collective-permute-start | bytes 884744 | tf_op jit(solution)/shard_map/ppermute | solution.py:465
  46.6 20.2 %collective-permute-start.22 = (bf16[96,768]{1,0:T(8,128)(2,1)}, bf16[96,768]{1,0:T(8,128)(2,1)}, u32[]{:S(2)}, u32[]{:S(2)}) collective-permute-start(bf16[96,768]{1,0:T(8,128)(2,1)} %copy-done.81), channel_id=1, source_target_pairs={{0,4},{4,0},{8,12},{12,8},{16,20},{20,16},{24,28},{28,24},{1,5},{5... | collective-permute-start | bytes 442376 | tf_op jit(solution)/shard_map/ppermute | solution.py:461
  46.7 18.7 %collective-permute-start.18 = (bf16[96,768]{1,0:T(8,128)(2,1)}, bf16[96,768]{1,0:T(8,128)(2,1)S(1)}, u32[]{:S(2)}, u32[]{:S(2)}) collective-permute-start(bf16[96,768]{1,0:T(8,128)(2,1)} %collective-permute-done.17.rest_14_), channel_id=1, source_target_pairs={{0,4},{4,0},{8,12},{12,8},{16,20},{20,16},{24,28},{28,24},{1,5},{5... | collective-permute-start | bytes 442376 | tf_op jit(solution)/shard_map/ppermute | solution.py:461
  50.8 16.7 %collective-permute-start.24 = (bf16[96,768]{1,0:T(8,128)(2,1)}, bf16[96,768]{1,0:T(8,128)(2,1)}, u32[]{:S(2)}, u32[]{:S(2)}) collective-permute-start(bf16[96,768]{1,0:T(8,128)(2,1)} %collective-permute-done.23.rest_20_), channel_id=1, source_target_pairs={{0,4},{4,0},{8,12},{12,8},{16,20},{20,16},{24,28},{28,24},{1,5},{5... | collective-permute-start | bytes 442376 | tf_op jit(solution)/shard_map/ppermute | solution.py:461
  65.4 22.7 %collective-permute-start.29 = (bf16[96,768]{1,0:T(8,128)(2,1)S(1)}, bf16[96,768]{1,0:T(8,128)(2,1)S(1)}, u32[]{:S(2)}, u32[]{:S(2)}) collective-permute-start(bf16[96,768]{1,0:T(8,128)(2,1)S(1)} %collective-permute-done.28.refs_1_), channel_id=1, source_target_pairs={{0,1},{1,2},{2,3},{3,0},{4,5},{5,6},{6,7},{7,4},{8,9},{9,10},{10,1... | collective-permute-start | bytes 442376 | tf_op jit(solution)/shard_map/ppermute | solution.py:465
  65.4 13.1 %collective-permute-start.38 = (bf16[3,96,768]{2,1,0:T(8,128)(2,1)S(1)}, bf16[3,96,768]{2,1,0:T(8,128)(2,1)S(1)}, u32[]{:S(2)}, u32[]{:S(2)}) collective-permute-start(bf16[3,96,768]{2,1,0:T(8,128)(2,1)S(1)} %get-tuple-element.133.rest_8_.rest_10_), channel_id=1, source_target_pairs={{0,8},{4,12},{8,0},{12,4},{16,24},{20,28},{24,16},{28,20},{1,9},{5... | collective-permute-start | bytes 1327112 | tf_op jit(solution)/shard_map/ppermute | solution.py:461
  67.5 19.2 %collective-permute-start.31 = (bf16[3,96,768]{2,1,0:T(8,128)(2,1)S(1)}, bf16[3,96,768]{2,1,0:T(8,128)(2,1)S(1)}, u32[]{:S(2)}, u32[]{:S(2)}) collective-permute-start(bf16[3,96,768]{2,1,0:T(8,128)(2,1)S(1)} %get-tuple-element.132.rest_0_.rest_2_), channel_id=1, source_target_pairs={{0,8},{4,12},{8,0},{12,4},{16,24},{20,28},{24,16},{28,20},{1,9},{5... | collective-permute-start | bytes 1327112 | tf_op jit(solution)/shard_map/ppermute | solution.py:461
  68.6 19.4 %collective-permute-start.32 = (bf16[3,96,768]{2,1,0:T(8,128)(2,1)S(1)}, bf16[3,96,768]{2,1,0:T(8,128)(2,1)S(1)}, u32[]{:S(2)}, u32[]{:S(2)}) collective-permute-start(bf16[3,96,768]{2,1,0:T(8,128)(2,1)S(1)} %get-tuple-element.132.rest_0_.rest_2_), channel_id=1, source_target_pairs={{0,16},{4,20},{8,24},{12,28},{16,0},{20,4},{24,8},{28,12},{1,17},{... | collective-permute-start | bytes 1327112 | tf_op jit(solution)/shard_map/ppermute | solution.py:461
  88.9 16.6 %collective-permute-start.41 = (bf16[3,96,768]{2,1,0:T(8,128)(2,1)S(1)}, bf16[3,96,768]{2,1,0:T(8,128)(2,1)S(1)}, u32[]{:S(2)}, u32[]{:S(2)}) collective-permute-start(bf16[3,96,768]{2,1,0:T(8,128)(2,1)S(1)} %collective-permute-done.39.rest_12_.rest_14_), channel_id=1, source_target_pairs={{0,4},{4,0},{8,12},{12,8},{16,20},{20,16},{24,28},{28,24},{1,5},{5... | collective-permute-start | bytes 1327112 | tf_op jit(solution)/shard_map/ppermute | solution.py:461
  89.2 16.5 %collective-permute-start.33 = (bf16[3,96,768]{2,1,0:T(8,128)(2,1)S(1)}, bf16[3,96,768]{2,1,0:T(8,128)(2,1)S(1)}, u32[]{:S(2)}, u32[]{:S(2)}) collective-permute-start(bf16[3,96,768]{2,1,0:T(8,128)(2,1)S(1)} %collective-permute-done.31.rest_2_.rest_4_), channel_id=1, source_target_pairs={{0,4},{4,0},{8,12},{12,8},{16,20},{20,16},{24,28},{28,24},{1,5},{5... | collective-permute-start | bytes 1327112 | tf_op jit(solution)/shard_map/ppermute | solution.py:461
  105.5 14.3 %collective-permute-start.44 = (bf16[192,768]{1,0:T(8,128)(2,1)S(1)}, bf16[192,768]{1,0:T(8,128)(2,1)S(1)}, u32[]{:S(2)}, u32[]{:S(2)}) collective-permute-start(bf16[192,768]{1,0:T(8,128)(2,1)S(1)} %pad_maximum_fusion.6), channel_id=1, source_target_pairs={{0,1},{1,2},{2,3},{3,0},{4,5},{5,6},{6,7},{7,4},{8,9},{9,10},{10,1... | collective-permute-start | bytes 884744 | tf_op jit(solution)/shard_map/ppermute | solution.py:465
  119.9 23.4 %collective-permute-start.47 = (bf16[3,96,768]{2,1,0:T(8,128)(2,1)S(1)}, bf16[3,96,768]{2,1,0:T(8,128)(2,1)}, u32[]{:S(2)}, u32[]{:S(2)}) collective-permute-start(bf16[3,96,768]{2,1,0:T(8,128)(2,1)S(1)} %pack.4.rest_0_), channel_id=1, source_target_pairs={{0,4},{4,0},{8,12},{12,8},{16,20},{20,16},{24,28},{28,24},{1,5},{5... | collective-permute-start | bytes 1327112 | tf_op jit(solution)/shard_map/ppermute | solution.py:461
  120.0 24.1 %collective-permute-start.50 = (bf16[3,96,768]{2,1,0:T(8,128)(2,1)}, bf16[3,96,768]{2,1,0:T(8,128)(2,1)}, u32[]{:S(2)}, u32[]{:S(2)}) collective-permute-start(bf16[3,96,768]{2,1,0:T(8,128)(2,1)} %collective-permute-done.48.rest_2_), channel_id=1, source_target_pairs={{0,4},{4,0},{8,12},{12,8},{16,20},{20,16},{24,28},{28,24},{1,5},{5... | collective-permute-start | bytes 1327112 | tf_op jit(solution)/shard_map/ppermute | solution.py:461
  120.5 24.7 %collective-permute-start.51 = (bf16[3,96,768]{2,1,0:T(8,128)(2,1)}, bf16[3,96,768]{2,1,0:T(8,128)(2,1)}, u32[]{:S(2)}, u32[]{:S(2)}) collective-permute-start(bf16[3,96,768]{2,1,0:T(8,128)(2,1)} %collective-permute-done.49.rest_4_), channel_id=1, source_target_pairs={{0,4},{4,0},{8,12},{12,8},{16,20},{20,16},{24,28},{28,24},{1,5},{5... | collective-permute-start | bytes 1327112 | tf_op jit(solution)/shard_map/ppermute | solution.py:461
  130.5 15.6 %collective-permute-start.53 = (bf16[3,96,768]{2,1,0:T(8,128)(2,1)}, bf16[3,96,768]{2,1,0:T(8,128)(2,1)}, u32[]{:S(2)}, u32[]{:S(2)}) collective-permute-start(bf16[3,96,768]{2,1,0:T(8,128)(2,1)} %collective-permute-done.52.rest_6_), channel_id=1, source_target_pairs={{0,4},{4,0},{8,12},{12,8},{16,20},{20,16},{24,28},{28,24},{1,5},{5... | collective-permute-start | bytes 1327112 | tf_op jit(solution)/shard_map/ppermute | solution.py:461
  144.1 20.5 %collective-permute-start.55 = (bf16[3,96,768]{2,1,0:T(8,128)(2,1)S(1)}, bf16[3,96,768]{2,1,0:T(8,128)(2,1)S(1)}, u32[]{:S(2)}, u32[]{:S(2)}) collective-permute-start(bf16[3,96,768]{2,1,0:T(8,128)(2,1)S(1)} %get-tuple-element.144.rest_0_.rest_2_), channel_id=1, source_target_pairs={{0,8},{4,12},{8,0},{12,4},{16,24},{20,28},{24,16},{28,20},{1,9},{5... | collective-permute-start | bytes 1327112 | tf_op jit(solution)/shard_map/ppermute | solution.py:461
  145.2 19.4 %collective-permute-start.56 = (bf16[3,96,768]{2,1,0:T(8,128)(2,1)S(1)}, bf16[3,96,768]{2,1,0:T(8,128)(2,1)S(1)}, u32[]{:S(2)}, u32[]{:S(2)}) collective-permute-start(bf16[3,96,768]{2,1,0:T(8,128)(2,1)S(1)} %get-tuple-element.144.rest_0_.rest_2_), channel_id=1, source_target_pairs={{0,16},{4,20},{8,24},{12,28},{16,0},{20,4},{24,8},{28,12},{1,17},{... | collective-permute-start | bytes 1327112 | tf_op jit(solution)/shard_map/ppermute | solution.py:461
  146.1 20.4 %collective-permute-start.54 = (bf16[3,96,768]{2,1,0:T(8,128)(2,1)S(1)}, bf16[3,96,768]{2,1,0:T(8,128)(2,1)}, u32[]{:S(2)}, u32[]{:S(2)}) collective-permute-start(bf16[3,96,768]{2,1,0:T(8,128)(2,1)S(1)} %get-tuple-element.144.rest_0_.rest_2_), channel_id=1, source_target_pairs={{0,4},{4,0},{8,12},{12,8},{16,20},{20,16},{24,28},{28,24},{1,5},{5... | collective-permute-start | bytes 1327112 | tf_op jit(solution)/shard_map/ppermute | solution.py:461
  156.4 16.5 %collective-permute-start.66 = (bf16[3,96,768]{2,1,0:T(8,128)(2,1)S(1)}, bf16[3,96,768]{2,1,0:T(8,128)(2,1)}, u32[]{:S(2)}, u32[]{:S(2)}) collective-permute-start(bf16[3,96,768]{2,1,0:T(8,128)(2,1)S(1)} %collective-permute-done.63.rest_12_.rest_14_), channel_id=1, source_target_pairs={{0,8},{4,12},{8,0},{12,4},{16,24},{20,28},{24,16},{28,20},{1,9},{5... | collective-permute-start | bytes 1327112 | tf_op jit(solution)/shard_map/ppermute | solution.py:461
  166.5 13.3 %collective-permute-start.65 = (bf16[3,96,768]{2,1,0:T(8,128)(2,1)S(1)}, bf16[3,96,768]{2,1,0:T(8,128)(2,1)S(1)}, u32[]{:S(2)}, u32[]{:S(2)}) collective-permute-start(bf16[3,96,768]{2,1,0:T(8,128)(2,1)S(1)} %collective-permute-done.63.rest_12_.rest_14_), channel_id=1, source_target_pairs={{0,4},{4,0},{8,12},{12,8},{16,20},{20,16},{24,28},{28,24},{1,5},{5... | collective-permute-start | bytes 1327112 | tf_op jit(solution)/shard_map/ppermute | solution.py:461
  191.0 14.1 %collective-permute-start.70 = (bf16[1,32,768]{2,1,0:T(8,128)(2,1)S(1)}, bf16[1,32,768]{2,1,0:T(8,128)(2,1)S(1)}, u32[]{:S(2)}, u32[]{:S(2)}) collective-permute-start(bf16[1,32,768]{2,1,0:T(8,128)(2,1)S(1)} %maximum_bitcast_fusion), channel_id=1, source_target_pairs={{0,1},{1,2},{2,3},{3,0},{4,5},{5,6},{6,7},{7,4},{8,9},{9,10},{10,1... | collective-permute-start | bytes 147464 | tf_op jit(solution)/shard_map/ppermute | solution.py:465
  191.1 15.1 %collective-permute-start.68 = (bf16[256,768]{1,0:T(8,128)(2,1)}, bf16[256,768]{1,0:T(8,128)(2,1)S(1)}, u32[]{:S(2)}, u32[]{:S(2)}) collective-permute-start(bf16[256,768]{1,0:T(8,128)(2,1)} %get-tuple-element.154), channel_id=1, source_target_pairs={{0,1},{1,2},{2,3},{3,0},{4,5},{5,6},{6,7},{7,4},{8,9},{9,10},{10,1... | collective-permute-start | bytes 1179656 | tf_op jit(solution)/shard_map/ppermute | solution.py:465
  205.1 18.2 %collective-permute-start.72 = (bf16[1,32,768]{2,1,0:T(8,128)(2,1)S(1)}, bf16[1,32,768]{2,1,0:T(8,128)(2,1)S(1)}, u32[]{:S(2)}, u32[]{:S(2)}) collective-permute-start(bf16[1,32,768]{2,1,0:T(8,128)(2,1)S(1)} %collective-permute-done.70), channel_id=1, source_target_pairs={{0,1},{1,2},{2,3},{3,0},{4,5},{5,6},{6,7},{7,4},{8,9},{9,10},{10,1... | collective-permute-start | bytes 147464 | tf_op jit(solution)/shard_map/ppermute | solution.py:465
  206.2 19.0 %collective-permute-start.69 = (bf16[256,768]{1,0:T(8,128)(2,1)S(1)}, bf16[256,768]{1,0:T(8,128)(2,1)S(1)}, u32[]{:S(2)}, u32[]{:S(2)}) collective-permute-start(bf16[256,768]{1,0:T(8,128)(2,1)S(1)} %collective-permute-done.68), channel_id=1, source_target_pairs={{0,1},{1,2},{2,3},{3,0},{4,5},{5,6},{6,7},{7,4},{8,9},{9,10},{10,1... | collective-permute-start | bytes 1179656 | tf_op jit(solution)/shard_map/ppermute | solution.py:465
  223.5 15.4 %collective-permute-start.73 = (bf16[4,4,1,96,768]{4,3,2,1,0:T(8,128)(2,1)}, bf16[4,4,1,96,768]{4,3,2,1,0:T(8,128)(2,1)S(1)}, u32[]{:S(2)}, u32[]{:S(2)}) collective-permute-start(bf16[4,4,1,96,768]{4,3,2,1,0:T(8,128)(2,1)} %get-tuple-element.176), channel_id=1, source_target_pairs={{0,4},{4,0},{8,12},{12,8},{16,20},{20,16},{24,28},{28,24},{1,5},{5... | collective-permute-start | bytes 7077896 | tf_op jit(solution)/shard_map/ppermute | solution.py:461
  225.1 13.7 %collective-permute-start.71 = (bf16[256,768]{1,0:T(8,128)(2,1)S(1)}, bf16[256,768]{1,0:T(8,128)(2,1)S(1)}, u32[]{:S(2)}, u32[]{:S(2)}) collective-permute-start(bf16[256,768]{1,0:T(8,128)(2,1)S(1)} %collective-permute-done.69), channel_id=1, source_target_pairs={{0,1},{1,2},{2,3},{3,0},{4,5},{5,6},{6,7},{7,4},{8,9},{9,10},{10,1... | collective-permute-start | bytes 1179656 | tf_op jit(solution)/shard_map/ppermute | solution.py:465
  235.4 23.4 %collective-permute-start.77 = (bf16[4,2,2,96,768]{4,3,2,1,0:T(8,128)(2,1)}, bf16[4,2,2,96,768]{4,3,2,1,0:T(8,128)(2,1)}, u32[]{:S(2)}, u32[]{:S(2)}) collective-permute-start(bf16[4,2,2,96,768]{4,3,2,1,0:T(8,128)(2,1)} %get-tuple-element.188), channel_id=1, source_target_pairs={{0,4},{4,0},{8,12},{12,8},{16,20},{20,16},{24,28},{28,24},{1,5},{5... | collective-permute-start | bytes 7077896 | tf_op jit(solution)/shard_map/ppermute | solution.py:461
  253.3 45.1 %collective-permute-start.82 = (bf16[4,2,2,96,768]{4,3,2,1,0:T(8,128)(2,1)}, bf16[4,2,2,96,768]{4,3,2,1,0:T(8,128)(2,1)}, u32[]{:S(2)}, u32[]{:S(2)}) collective-permute-start(bf16[4,2,2,96,768]{4,3,2,1,0:T(8,128)(2,1)} %get-tuple-element.205), channel_id=1, source_target_pairs={{0,4},{4,0},{8,12},{12,8},{16,20},{20,16},{24,28},{28,24},{1,5},{5... | collective-permute-start | bytes 7077896 | tf_op jit(solution)/shard_map/ppermute | solution.py:461
  256.8 23.1 %collective-permute-start.78 = (bf16[4,1,96,768]{3,2,1,0:T(8,128)(2,1)}, bf16[4,1,96,768]{3,2,1,0:T(8,128)(2,1)S(1)}, u32[]{:S(2)}, u32[]{:S(2)}) collective-permute-start(bf16[4,1,96,768]{3,2,1,0:T(8,128)(2,1)} %get-tuple-element.185), channel_id=1, source_target_pairs={{0,8},{4,12},{8,0},{12,4},{16,24},{20,28},{24,16},{28,20},{1,9},{5... | collective-permute-start | bytes 1769480 | tf_op jit(solution)/shard_map/ppermute | solution.py:461
  257.9 22.0 %collective-permute-start.79 = (bf16[4,1,96,768]{3,2,1,0:T(8,128)(2,1)}, bf16[4,1,96,768]{3,2,1,0:T(8,128)(2,1)S(1)}, u32[]{:S(2)}, u32[]{:S(2)}) collective-permute-start(bf16[4,1,96,768]{3,2,1,0:T(8,128)(2,1)} %get-tuple-element.186), channel_id=1, source_target_pairs={{0,16},{4,20},{8,24},{12,28},{16,0},{20,4},{24,8},{28,12},{1,17},{... | collective-permute-start | bytes 1769480 | tf_op jit(solution)/shard_map/ppermute | solution.py:461
  262.3 17.5 %collective-permute-start.81 = (bf16[1,2,96,768]{3,2,1,0:T(8,128)(2,1)}, bf16[1,2,96,768]{3,2,1,0:T(8,128)(2,1)S(1)}, u32[]{:S(2)}, u32[]{:S(2)}) collective-permute-start(bf16[1,2,96,768]{3,2,1,0:T(8,128)(2,1)} %corner_sum.13), channel_id=1, source_target_pairs={{0,16},{4,20},{8,24},{12,28},{16,0},{20,4},{24,8},{28,12},{1,17},{... | collective-permute-start | bytes 884744 | tf_op jit(solution)/shard_map/ppermute | solution.py:461
  263.5 16.4 %collective-permute-start.80 = (bf16[1,2,96,768]{3,2,1,0:T(8,128)(2,1)}, bf16[1,2,96,768]{3,2,1,0:T(8,128)(2,1)S(1)}, u32[]{:S(2)}, u32[]{:S(2)}) collective-permute-start(bf16[1,2,96,768]{3,2,1,0:T(8,128)(2,1)} %corner_sum.12), channel_id=1, source_target_pairs={{0,8},{4,12},{8,0},{12,4},{16,24},{20,28},{24,16},{28,20},{1,9},{5... | collective-permute-start | bytes 884744 | tf_op jit(solution)/shard_map/ppermute | solution.py:461
  279.9 33.2 %collective-permute-start.87 = (bf16[4,2,1,96,768]{4,3,2,1,0:T(8,128)(2,1)}, bf16[4,2,1,96,768]{4,3,2,1,0:T(8,128)(2,1)}, u32[]{:S(2)}, u32[]{:S(2)}) collective-permute-start(bf16[4,2,1,96,768]{4,3,2,1,0:T(8,128)(2,1)} %get-tuple-element.218), channel_id=1, source_target_pairs={{0,4},{4,0},{8,12},{12,8},{16,20},{20,16},{24,28},{28,24},{1,5},{5... | collective-permute-start | bytes 3538952 | tf_op jit(solution)/shard_map/ppermute | solution.py:461
  281.9 14.0 %collective-permute-start.111 = (bf16[1,1,96,768]{3,2,1,0:T(8,128)(2,1)S(1)}, bf16[1,1,96,768]{3,2,1,0:T(8,128)(2,1)S(1)}, u32[]{:S(2)}, u32[]{:S(2)}) collective-permute-start(bf16[1,1,96,768]{3,2,1,0:T(8,128)(2,1)S(1)} %own_sum.14), channel_id=1, source_target_pairs={{0,2},{1,3},{2,0},{3,1},{4,6},{5,7},{6,4},{7,5},{8,10},{9,11},{10,... | collective-permute-start | bytes 442376 | tf_op jit(solution)/shard_map/ppermute | solution.py:619
  290.3 34.7 %collective-permute-start.83 = (bf16[2,2,96,768]{3,2,1,0:T(8,128)(2,1)}, bf16[2,2,96,768]{3,2,1,0:T(8,128)(2,1)}, u32[]{:S(2)}, u32[]{:S(2)}) collective-permute-start(bf16[2,2,96,768]{3,2,1,0:T(8,128)(2,1)} %get-tuple-element.202), channel_id=1, source_target_pairs={{0,8},{4,12},{8,0},{12,4},{16,24},{20,28},{24,16},{28,20},{1,9},{5... | collective-permute-start | bytes 1769480 | tf_op jit(solution)/shard_map/ppermute | solution.py:461
  295.8 29.2 %collective-permute-start.84 = (bf16[2,2,96,768]{3,2,1,0:T(8,128)(2,1)}, bf16[2,2,96,768]{3,2,1,0:T(8,128)(2,1)}, u32[]{:S(2)}, u32[]{:S(2)}) collective-permute-start(bf16[2,2,96,768]{3,2,1,0:T(8,128)(2,1)} %get-tuple-element.203), channel_id=1, source_target_pairs={{0,16},{4,20},{8,24},{12,28},{16,0},{20,4},{24,8},{28,12},{1,17},{... | collective-permute-start | bytes 1769480 | tf_op jit(solution)/shard_map/ppermute | solution.py:461
  321.6 23.0 %collective-permute-start.86 = (bf16[1,2,96,768]{3,2,1,0:T(8,128)(2,1)S(1)}, bf16[1,2,96,768]{3,2,1,0:T(8,128)(2,1)S(1)}, u32[]{:S(2)}, u32[]{:S(2)}) collective-permute-start(bf16[1,2,96,768]{3,2,1,0:T(8,128)(2,1)S(1)} %copy-done.15), channel_id=1, source_target_pairs={{0,16},{4,20},{8,24},{12,28},{16,0},{20,4},{24,8},{28,12},{1,17},{... | collective-permute-start | bytes 884744 | tf_op jit(solution)/shard_map/ppermute | solution.py:461
  322.5 24.5 %collective-permute-start.85 = (bf16[1,2,96,768]{3,2,1,0:T(8,128)(2,1)S(1)}, bf16[1,2,96,768]{3,2,1,0:T(8,128)(2,1)S(1)}, u32[]{:S(2)}, u32[]{:S(2)}) collective-permute-start(bf16[1,2,96,768]{3,2,1,0:T(8,128)(2,1)S(1)} %copy-done.13), channel_id=1, source_target_pairs={{0,8},{4,12},{8,0},{12,4},{16,24},{20,28},{24,16},{28,20},{1,9},{5... | collective-permute-start | bytes 884744 | tf_op jit(solution)/shard_map/ppermute | solution.py:461
  325.0 23.4 %collective-permute-start.97 = (bf16[256,768]{1,0:T(8,128)(2,1)S(1)}, bf16[256,768]{1,0:T(8,128)(2,1)S(1)}, u32[]{:S(2)}, u32[]{:S(2)}) collective-permute-start(bf16[256,768]{1,0:T(8,128)(2,1)S(1)} %get-tuple-element.274), channel_id=1, source_target_pairs={{0,1},{1,2},{2,3},{3,0},{4,5},{5,6},{6,7},{7,4},{8,9},{9,10},{10,1... | collective-permute-start | bytes 1179656 | tf_op jit(solution)/shard_map/ppermute | solution.py:465
  340.0 27.3 %collective-permute-start.92 = (bf16[4,2,1,96,768]{4,3,2,1,0:T(8,128)(2,1)S(1)}, bf16[4,2,1,96,768]{4,3,2,1,0:T(8,128)(2,1)S(1)}, u32[]{:S(2)}, u32[]{:S(2)}) collective-permute-start(bf16[4,2,1,96,768]{4,3,2,1,0:T(8,128)(2,1)S(1)} %copy-done.53), channel_id=1, source_target_pairs={{0,4},{4,0},{8,12},{12,8},{16,20},{20,16},{24,28},{28,24},{1,5},{5... | collective-permute-start | bytes 3538952 | tf_op jit(solution)/shard_map/ppermute | solution.py:461
  346.9 26.9 %collective-permute-start.113 = (bf16[1,2,96,768]{3,2,1,0:T(8,128)(2,1)S(1)}, bf16[1,2,96,768]{3,2,1,0:T(8,128)(2,1)S(1)}, u32[]{:S(2)}, u32[]{:S(2)}) collective-permute-start(bf16[1,2,96,768]{3,2,1,0:T(8,128)(2,1)S(1)} %own_sum.17), channel_id=1, source_target_pairs={{0,3},{1,0},{2,1},{3,2},{4,7},{5,4},{6,5},{7,6},{8,11},{9,8},{10,9... | collective-permute-start | bytes 884744 | tf_op jit(solution)/shard_map/ppermute | solution.py:619
  348.4 14.2 %collective-permute-start.98 = (bf16[256,768]{1,0:T(8,128)(2,1)S(1)}, bf16[256,768]{1,0:T(8,128)(2,1)S(1)}, u32[]{:S(2)}, u32[]{:S(2)}) collective-permute-start(bf16[256,768]{1,0:T(8,128)(2,1)S(1)} %collective-permute-done.97), channel_id=1, source_target_pairs={{0,1},{1,2},{2,3},{3,0},{4,5},{5,6},{6,7},{7,4},{8,9},{9,10},{10,1... | collective-permute-start | bytes 1179656 | tf_op jit(solution)/shard_map/ppermute | solution.py:465
  367.3 27.5 %collective-permute-start.114 = (bf16[1,2,96,768]{3,2,1,0:T(8,128)(2,1)S(1)}, bf16[1,2,96,768]{3,2,1,0:T(8,128)(2,1)S(1)}, u32[]{:S(2)}, u32[]{:S(2)}) collective-permute-start(bf16[1,2,96,768]{3,2,1,0:T(8,128)(2,1)S(1)} %own_sum.18), channel_id=1, source_target_pairs={{0,2},{1,3},{2,0},{3,1},{4,6},{5,7},{6,4},{7,5},{8,10},{9,11},{10,... | collective-permute-start | bytes 884744 | tf_op jit(solution)/shard_map/ppermute | solution.py:619
  369.9 25.0 %collective-permute-start.96 = (bf16[1,1,96,768]{3,2,1,0:T(8,128)(2,1)S(1)}, bf16[1,1,96,768]{3,2,1,0:T(8,128)(2,1)S(1)}, u32[]{:S(2)}, u32[]{:S(2)}) collective-permute-start(bf16[1,1,96,768]{3,2,1,0:T(8,128)(2,1)S(1)} %corner_sum.19), channel_id=1, source_target_pairs={{0,16},{4,20},{8,24},{12,28},{16,0},{20,4},{24,8},{28,12},{1,17},{... | collective-permute-start | bytes 442376 | tf_op jit(solution)/shard_map/ppermute | solution.py:461
  370.9 24.0 %collective-permute-start.95 = (bf16[1,1,96,768]{3,2,1,0:T(8,128)(2,1)S(1)}, bf16[1,1,96,768]{3,2,1,0:T(8,128)(2,1)S(1)}, u32[]{:S(2)}, u32[]{:S(2)}) collective-permute-start(bf16[1,1,96,768]{3,2,1,0:T(8,128)(2,1)S(1)} %corner_sum.18), channel_id=1, source_target_pairs={{0,8},{4,12},{8,0},{12,4},{16,24},{20,28},{24,16},{28,20},{1,9},{5... | collective-permute-start | bytes 442376 | tf_op jit(solution)/shard_map/ppermute | solution.py:461
  373.8 31.4 %collective-permute-start.99 = (bf16[256,768]{1,0:T(8,128)(2,1)S(1)}, bf16[256,768]{1,0:T(8,128)(2,1)S(1)}, u32[]{:S(2)}, u32[]{:S(2)}) collective-permute-start(bf16[256,768]{1,0:T(8,128)(2,1)S(1)} %collective-permute-done.98), channel_id=1, source_target_pairs={{0,1},{1,2},{2,3},{3,0},{4,5},{5,6},{6,7},{7,4},{8,9},{9,10},{10,1... | collective-permute-start | bytes 1179656 | tf_op jit(solution)/shard_map/ppermute | solution.py:465
  377.5 39.0 %collective-permute-start.105 = (bf16[1,1,96,768]{3,2,1,0:T(8,128)(2,1)S(1)}, bf16[1,1,96,768]{3,2,1,0:T(8,128)(2,1)S(1)}, u32[]{:S(2)}, u32[]{:S(2)}) collective-permute-start(bf16[1,1,96,768]{3,2,1,0:T(8,128)(2,1)S(1)} %own_sum.21), channel_id=1, source_target_pairs={{0,3},{1,0},{2,1},{3,2},{4,7},{5,4},{6,5},{7,6},{8,11},{9,8},{10,9... | collective-permute-start | bytes 442376 | tf_op jit(solution)/shard_map/ppermute | solution.py:619
  (159 other events, 1502.7 us)

commit v2 on v1

v2 whole, which is shorter than its diff:
```python
import functools

import jax
import jax.numpy as jnp
from jax import lax
from jax.experimental import pallas as pl
from jax.experimental.pallas import tpu as pltpu
from jax.sharding import PartitionSpec as P

HD = 64
WORDS = 40
TOP_ROWS = 48
SLOT_ROWS = 16
EPSILON = 1e-06
ROOT_HALF = 0.7071067811865476
ROOT_TWO_PI = 2.5066282746310002
GROUP = 8
STEP = 32
SIDES_FIRST = True
F32 = jnp.float32
BF16 = jnp.bfloat16
SMALL_VMEM = 16 * 1024 * 1024
VMEM_BYTES = 60 * 1024 * 1024


def dot(left, right, dims):
    return lax.dot_general(left, right, (dims, ((), ())), preferred_element_type=F32)


def nn(left, right):
    return dot(left, right, ((1,), (0,)))


def nt(left, right):
    return dot(left, right, ((1,), (1,)))


def tn(left, right):
    return dot(left, right, ((0,), (0,)))


def gelu(values):
    return 0.5 * values * (1.0 + lax.erf(values * ROOT_HALF))


def gelu_slope(values):
    return 0.5 * (1.0 + lax.erf(values * ROOT_HALF)) + values * jnp.exp(-0.5 * values * values) / ROOT_TWO_PI


def norm_parts(values):
    average = jnp.mean(values, axis=-1, keepdims=True)
    centred = values - average
    spread = jnp.mean(centred * centred, axis=-1, keepdims=True)
    rate = lax.rsqrt(spread + EPSILON)
    return centred * rate, rate


def norm_rows(source, gain, bias, target):
    step = STEP if source.shape[0] % STEP == 0 else STEP // 2
    for r in range(0, source.shape[0], step):
        rows = slice(r, r + step)
        target[rows, :] = (norm_parts(source[rows, :])[0] * gain[...] + bias[...]).astype(BF16)


def norm_back_rows(rows, values, gain, incoming, gain_grad, bias_grad):
    unit, rate = norm_parts(values[rows, :])
    e = incoming[rows, :]
    scaled = e * gain[...]
    inner = jnp.mean(scaled * unit, axis=-1, keepdims=True)
    gain_grad[...] += jnp.sum(e * unit, axis=0, keepdims=True)
    bias_grad[...] += jnp.sum(e, axis=0, keepdims=True)
    return rate * (scaled - jnp.mean(scaled, axis=-1, keepdims=True) - unit * inner)


def flops(count):
    return pl.CostEstimate(flops=count, bytes_accessed=1_000_000, transcendentals=0)


KERNEL_COST = pl.CostEstimate(flops=40_000_000_000, bytes_accessed=1_000_000, transcendentals=0)
SMALL_COST = pl.CostEstimate(flops=1_000_000_000, bytes_accessed=1_000_000, transcendentals=0)


class Pieces:
    def __init__(self, at):
        self.arrays = []
        self.plan = []
        for matrix in at:
            for k, slices in enumerate(matrix, 1):
                for s, (array, lead, row) in enumerate(slices):
                    found = [i for i, v in enumerate(self.arrays) if v is array]
                    if not found:
                        self.arrays.append(array)
                        found = [len(self.arrays) - 1]
                    self.plan.append((len(self.plan) // (len(matrix) * GROUP), k, s, found[0], lead, row))


def fetch(spot, layer, own, plan, sources, scratches, sems, quarters):
    rows = scratches[0].shape[1] // GROUP
    for k in quarters:
        for m, scratch in enumerate(scratches):
            if k == 0 and own:
                pltpu.make_async_copy(own[m].at[layer], scratch.at[0], sems.at[0]).start()
        for m, at_k, s, which, lead, row in plan:
            if at_k == k:
                source = sources[which].at[lead]
                at = pl.multiple_of((spot ^ s) * rows, rows)
                pltpu.make_async_copy(
                    source.at[pl.ds(row, rows)],
                    scratches[m].at[k - quarters[0], pl.ds(at, rows)],
                    sems.at[k - quarters[0]],
                ).start()


def arrived(k, scratches, sems):
    for scratch in scratches:
        pltpu.make_async_copy(scratch.at[k], scratch.at[k], sems.at[k]).wait()


def own_copies(layer, own_qkv, own_out, raw_qkv, raw_out, sem):
    return [
        pltpu.make_async_copy(own_qkv.at[layer], raw_qkv, sem),
        pltpu.make_async_copy(own_out.at[layer], raw_out, sem),
    ]


def own_block(copies, raw_qkv, raw_out, block):
    for copy in copies:
        copy.wait()
    inner = raw_qkv.shape[2]
    for c in range(3):
        block[0, :, c * inner : (c + 1) * inner] = raw_qkv[c]
    block[0, :, 3 * inner :] = raw_out[...].astype(F32).T.astype(BF16)


def flip(spot, source, target):
    width = source.shape[1]
    rows = width // GROUP
    turned = source.astype(F32).T.astype(BF16)
    for j in range(GROUP):
        s = spot ^ j
        at = pl.multiple_of(((s & 1) * (GROUP // 2) + (s >> 1)) * rows, rows)
        target[pl.ds(at, rows), :] = turned[j * rows : (j + 1) * rows, :]


def put_block(block, keep, send, part, columns=slice(None)):
    half = block.shape[0] // 2
    rows = half // (GROUP // 2)
    for i in range(GROUP // 2):
        keep[i, 0, part, :, columns] = block[i * rows : (i + 1) * rows].astype(BF16)
        send[i, 0, part, :, columns] = block[half + i * rows : half + (i + 1) * rows].astype(BF16)


def any_spec():
    return pl.BlockSpec(memory_space=pl.ANY)


def smem_spec():
    return pl.BlockSpec(memory_space=pltpu.SMEM)


def whole(shape):
    return pl.BlockSpec(shape, lambda k: (0,) * len(shape))


def per_quarter(shape, first=0):
    return pl.BlockSpec((1,) + shape, lambda k: (first + k,) + (0,) * len(shape))


def block_specs(matrices, rows, width):
    return [pl.BlockSpec((GROUP // 2, 1, matrices, rows, width), lambda k: (0, k, 0, 0, 0))] * 2


def block_shapes(quarters, matrices, rows, width):
    return [jax.ShapeDtypeStruct((GROUP // 2, quarters, matrices, rows, width), BF16)] * 2


def params(limit=VMEM_BYTES):
    return pltpu.CompilerParams(vmem_limit_bytes=limit)


def cost(flops, moved):
    return pl.CostEstimate(flops=flops, bytes_accessed=moved, transcendentals=0)


def attention_forward_kernel(layer, plan, count, spot_ref, x, gain, bias, own_qkv, own_out, *rest):
    middle, normed, proj, logsum, mixed, block, sems, raw_qkv, raw_out = rest[count:]
    k = pl.program_id(0)
    inner = mixed.shape[-1]
    heads = inner // HD

    @pl.when(k == 0)
    def _():
        copies = own_copies(layer, own_qkv, own_out, raw_qkv, raw_out, sems.at[0])
        for copy in copies:
            copy.start()
        fetch(spot_ref[0], layer, [], plan, rest[:count], [block], sems, range(block.shape[0]))
        norm_rows(x, gain, bias, normed)
        middle[...] = x[...]
        logsum[...] = jnp.zeros_like(logsum)
        own_block(copies, raw_qkv, raw_out, block)

    @pl.when(k > 0)
    def _():
        arrived(k, [block], sems)

    proj[0] = nn(normed[...], block[k, :, : 3 * inner]).astype(BF16)
    lane = lax.broadcasted_iota(jnp.int32, logsum.shape, 1)
    for h in range(heads):
        own_lanes = slice(h * HD, (h + 1) * HD)
        queries = proj[0, :, own_lanes] * jnp.asarray(HD**-0.5, BF16)
        keys = proj[0, :, inner + h * HD : inner + (h + 1) * HD]
        values = proj[0, :, 2 * inner + h * HD : 2 * inner + (h + 1) * HD]
        scores = nt(queries, keys)
        top = jnp.max(scores, axis=-1, keepdims=True)
        powers = jnp.exp(scores - top)
        total = jnp.sum(powers, axis=-1, keepdims=True)
        logsum[...] = jnp.where(lane == k * heads + h, top + jnp.log(total), logsum[...])
        weights = (powers * (1.0 / total)).astype(BF16)
        mixed[0, :, own_lanes] = nn(weights, values).astype(BF16)
    middle[...] += nt(mixed[0], block[k, :, 3 * inner :]).astype(BF16).astype(F32)


def attention_forward(spot, x, gain, bias, layer, own, pieces, n_t, work):
    length, width = x.shape
    inner = own[1].shape[1]
    count = len(pieces.arrays)
    out = [
        jax.ShapeDtypeStruct((length, width), F32),
        jax.ShapeDtypeStruct((length, width), BF16),
        jax.ShapeDtypeStruct((n_t, length, 3 * inner), BF16),
        jax.ShapeDtypeStruct((length, 128), F32),
        jax.ShapeDtypeStruct((n_t, length, inner), BF16),
    ]
    return pl.pallas_call(
        functools.partial(attention_forward_kernel, layer, pieces.plan, count),
        grid=(n_t,),
        out_shape=out,
        in_specs=[smem_spec(), whole((length, width)), whole((1, width)), whole((1, width))] + [any_spec()] * (2 + count),
        out_specs=[
            whole((length, width)),
            whole((length, width)),
            per_quarter((length, 3 * inner)),
            whole((length, 128)),
            per_quarter((length, inner)),
        ],
        scratch_shapes=[
            pltpu.VMEM((n_t, width, 4 * inner), BF16),
            pltpu.SemaphoreType.DMA((n_t,)),
            pltpu.VMEM((3, width, inner), BF16),
            pltpu.VMEM((inner, width), BF16),
        ],
        compiler_params=params(),
        cost_estimate=flops(work),
        name="attention_forward",
    )(spot, x, gain, bias, *own, *pieces.arrays)


def mlp_forward_kernel(kept_rows, layer, plan, count, spot_ref, x, gain, bias, own_up, own_down, *rest):
    if kept_rows:
        out, normed, upward, ups, downs, total, sems = rest[count:]
    else:
        out, ups, downs, total, sems, normed = rest[count:]
    k = pl.program_id(0)

    @pl.when(k == 0)
    def _():
        fetch(spot_ref[0], layer, [own_up, own_down], plan, rest[:count], [ups, downs], sems, range(ups.shape[0]))
        norm_rows(x, gain, bias, normed)
        total[...] = x[...]

    arrived(k, [ups, downs], sems)
    up = nn(normed[...], ups[k])
    if kept_rows:
        upward[0] = up
    active = gelu(up).astype(BF16)
    total[...] += nn(active, downs[k]).astype(BF16).astype(F32)

    @pl.when(k == pl.num_programs(0) - 1)
    def _():
        out[...] = total[...].astype(out.dtype)


def mlp_forward(spot, x, gain, bias, layer, own, pieces, n_t, kept_rows, out_type):
    length, width = x.shape
    hidden = own[0].shape[2]
    count = len(pieces.arrays)
    out = [jax.ShapeDtypeStruct((length, width), out_type)]
    out_specs = [whole((length, width))]
    scratch = []
    if kept_rows:
        out += [jax.ShapeDtypeStruct((length, width), BF16), jax.ShapeDtypeStruct((n_t, length, hidden), F32)]
        out_specs += [whole((length, width)), per_quarter((length, hidden))]
    else:
        scratch.append(pltpu.VMEM((length, width), BF16))
    return pl.pallas_call(
        functools.partial(mlp_forward_kernel, kept_rows, layer, pieces.plan, count),
        grid=(n_t,),
        out_shape=out,
        in_specs=[smem_spec(), whole((length, width)), whole((1, width)), whole((1, width))]
        + [any_spec()] * (2 + count),
        out_specs=out_specs,
        scratch_shapes=[
            pltpu.VMEM((n_t,) + own[0].shape[1:], BF16),
            pltpu.VMEM((n_t,) + own[1].shape[1:], BF16),
            pltpu.VMEM((length, width), F32),
            pltpu.SemaphoreType.DMA((n_t,)),
        ]
        + scratch,
        compiler_params=params(),
        cost_estimate=KERNEL_COST,
        name="mlp_forward",
    )(spot, x, gain, bias, *own, *pieces.arrays)


def mlp_backward_kernel(quarters, last, blocks, layer, plan, count, spot_ref, incoming, x, gain, normed, upward, total_in, *rest):
    own, sources = rest[:2], rest[2 : 2 + count]
    rest = list(rest[2 + count :])
    total = rest.pop(0)
    if last:
        grad, gain_grad, bias_grad = (rest.pop(0) for _ in range(3))
    if blocks:
        keep, send = rest.pop(0), rest.pop(0)
    ups, downs, sems, *flipped = rest
    k = pl.program_id(0)

    @pl.when(k == 0)
    def _():
        fetch(spot_ref[0], layer, own, plan, sources, [ups, downs], sems, quarters)
        total[...] = jnp.zeros_like(total) if quarters[0] == 0 else total_in[...]
        if blocks:
            flip(spot_ref[0], incoming[...], flipped[0])
            flip(spot_ref[0], normed[...], flipped[1])

    arrived(k, [ups, downs], sems)
    up = upward[0]
    grad_active = nt(incoming[...].astype(BF16), downs[k])
    bell = 0.5 * (1.0 + lax.erf(up * ROOT_HALF))
    grad_up = (grad_active * (bell + up * jnp.exp(-0.5 * up * up) * (1.0 / ROOT_TWO_PI))).astype(BF16)
    total[...] += nt(grad_up, ups[k])
    if blocks:
        put_block(nn(flipped[0][...], (up * bell).astype(BF16)), keep, send, 0)
        put_block(nn(flipped[1][...], grad_up), keep, send, 1)

    if last:

        @pl.when(k == pl.num_programs(0) - 1)
        def _():
            gain_grad[...] = jnp.zeros_like(gain_grad)
            bias_grad[...] = jnp.zeros_like(bias_grad)
            for r in range(0, x.shape[0], 16):
                rows = slice(r, r + 16)
                grad[rows, :] = incoming[rows, :] + norm_back_rows(rows, x, gain, total, gain_grad, bias_grad)


def mlp_backward(spot, incoming, x, gain, normed, upward, total, layer, own, pieces, quarters, blocks):
    length, width = incoming.shape
    n_t, hidden = upward.shape[0], upward.shape[2]
    last = quarters[-1] == n_t - 1
    count = len(quarters)
    if total is None:
        total = jnp.zeros((8, 128), F32)
    out = [jax.ShapeDtypeStruct((length, width), F32)]
    out_specs = [whole((length, width))]
    if last:
        out += [jax.ShapeDtypeStruct(v, F32) for v in ((length, width), (1, width), (1, width))]
        out_specs += [whole((length, width)), whole((1, width)), whole((1, width))]
    scratch = [
        pltpu.VMEM((count,) + own[0].shape[1:], BF16),
        pltpu.VMEM((count,) + own[1].shape[1:], BF16),
        pltpu.SemaphoreType.DMA((count,)),
    ]
    if blocks:
        out += block_shapes(count, 2, width // GROUP, hidden)
        out_specs += block_specs(2, width // GROUP, hidden)
        scratch += [pltpu.VMEM((width, length), BF16)] * 2
    return pl.pallas_call(
        functools.partial(mlp_backward_kernel, quarters, last, blocks, layer, pieces.plan, len(pieces.arrays)),
        grid=(count,),
        out_shape=out,
        in_specs=[
            smem_spec(),
            whole((length, width)),
            whole((length, width)),
            whole((1, width)),
            whole((length, width)),
            per_quarter((length, hidden), quarters[0]),
            whole(total.shape),
        ]
        + [any_spec()] * (2 + len(pieces.arrays)),
        out_specs=out_specs,
        scratch_shapes=scratch,
        compiler_params=params(),
        cost_estimate=KERNEL_COST,
        name="mlp_backward",
    )(spot, incoming, x, gain, normed, upward, total, *own, *pieces.arrays)


def top_kernel(layer, plan, count, spot_ref, incoming, x, gain, bias, own_up, own_down, *rest):
    grad, gain_grad, bias_grad, normed, ups, downs, total, sems = rest[count:]
    k = pl.program_id(0)

    @pl.when(k == 0)
    def _():
        fetch(spot_ref[0], layer, [own_up, own_down], plan, rest[:count], [ups, downs], sems, range(ups.shape[0]))
        norm_rows(x, gain, bias, normed)
        total[...] = jnp.zeros_like(total)

    arrived(k, [ups, downs], sems)
    up = nn(normed[...], ups[k])
    grad_up = (nt(incoming[...].astype(BF16), downs[k]) * gelu_slope(up)).astype(BF16)
    total[...] += nt(grad_up, ups[k])

    @pl.when(k == pl.num_programs(0) - 1)
    def _():
        gain_grad[...] = jnp.zeros_like(gain_grad)
        bias_grad[...] = jnp.zeros_like(bias_grad)
        for r in range(0, incoming.shape[0], 16):
            rows = slice(r, r + 16)
            grad[rows, :] = incoming[rows, :] + norm_back_rows(rows, x, gain, total, gain_grad, bias_grad)


def top_backward(spot, incoming, x, gain, bias, layer, own, pieces, n_t):
    length, width = incoming.shape
    rows = pl.BlockSpec((length, width), lambda k: (0, 0))
    row = whole((1, width))
    return pl.pallas_call(
        functools.partial(top_kernel, layer, pieces.plan, len(pieces.arrays)),
        grid=(n_t,),
        out_shape=[
            jax.ShapeDtypeStruct((length, width), F32),
            jax.ShapeDtypeStruct((1, width), F32),
            jax.ShapeDtypeStruct((1, width), F32),
            jax.ShapeDtypeStruct((length, width), BF16),
        ],
        in_specs=[smem_spec(), rows, rows, row, row] + [any_spec()] * (2 + len(pieces.arrays)),
        out_specs=[rows, row, row, rows],
        scratch_shapes=[
            pltpu.VMEM((n_t,) + own[0].shape[1:], BF16),
            pltpu.VMEM((n_t,) + own[1].shape[1:], BF16),
            pltpu.VMEM((length, width), F32),
            pltpu.SemaphoreType.DMA((n_t,)),
        ],
        compiler_params=params(),
        cost_estimate=KERNEL_COST,
        name="top_backward",
    )(spot, incoming, x, gain, bias, *own, *pieces.arrays)


def attention_backward_kernel(
    quarters, last, layer, plan, count, spot_ref, incoming, x, gain, normed, proj, logsum, mixed, total_in, own_qkv, own_out, *rest
):
    sources = rest[:count]
    rest = list(rest[count:])
    total = rest.pop(0)
    if last:
        grad, gain_grad, bias_grad = (rest.pop(0) for _ in range(3))
    keep, send, block, grad_proj, sems, low_t, normed_t, raw_qkv, raw_out = rest
    k = pl.program_id(0)
    top = incoming.shape[0]
    inner = mixed.shape[-1]
    heads = inner // HD

    @pl.when(k == 0)
    def _():
        if quarters[0] == 0:
            copies = own_copies(layer, own_qkv, own_out, raw_qkv, raw_out, sems.at[0])
            for copy in copies:
                copy.start()
        fetch(spot_ref[0], layer, [], plan, sources, [block], sems, quarters)
        total[...] = jnp.zeros_like(total) if quarters[0] == 0 else total_in[...]
        grad_proj[...] = jnp.zeros_like(grad_proj)
        flip(spot_ref[0], incoming[...], low_t)
        flip(spot_ref[0], normed[...], normed_t)
        if quarters[0] == 0:
            own_block(copies, raw_qkv, raw_out, block)

    @pl.when(quarters[0] + k > 0)
    def _():
        arrived(k, [block], sems)

    grad_mixed = nn(incoming[...].astype(BF16), block[k, :, 3 * inner :]).astype(BF16)
    lane = lax.broadcasted_iota(jnp.int32, (top, 128), 1)
    for h in range(heads):
        own_lanes = slice(h * HD, (h + 1) * HD)
        key_lanes = slice(inner + h * HD, inner + (h + 1) * HD)
        value_lanes = slice(2 * inner + h * HD, 2 * inner + (h + 1) * HD)
        queries = proj[0, :top, own_lanes] * jnp.asarray(HD**-0.5, BF16)
        keys = proj[0, :, key_lanes]
        values = proj[0, :, value_lanes]
        head_grad = grad_mixed[:, own_lanes]
        at = lane == (quarters[0] + k) * heads + h
        row_sum = jnp.sum(jnp.where(at, logsum[:top, :], 0.0), axis=-1, keepdims=True)
        weights = jnp.exp(nt(queries, keys) - row_sum)
        grad_weights = nt(head_grad, values)
        inner_sum = jnp.sum(weights * grad_weights, axis=-1, keepdims=True)
        grad_scores = (weights * (grad_weights - inner_sum)).astype(BF16)
        grad_proj[:top, own_lanes] = (nn(grad_scores, keys) * HD**-0.5).astype(BF16)
        grad_proj[:, key_lanes] = tn(grad_scores, queries).astype(BF16)
        grad_proj[:, value_lanes] = tn(weights.astype(BF16), head_grad).astype(BF16)
    total[...] += nt(grad_proj[...], block[k, :, : 3 * inner])
    put_block(nn(normed_t[...], grad_proj[...]), keep, send, 0, slice(0, 3 * inner))
    put_block(nn(low_t[...], mixed[0, :top, :]), keep, send, 0, slice(3 * inner, 4 * inner))

    if last:

        @pl.when(k == pl.num_programs(0) - 1)
        def _():
            gain_grad[...] = jnp.zeros_like(gain_grad)
            bias_grad[...] = jnp.zeros_like(bias_grad)
            for r in range(0, x.shape[0], 16):
                rows = slice(r, r + 16)
                back = norm_back_rows(rows, x, gain, total, gain_grad, bias_grad)
                grad[rows, :] = back + incoming[rows, :] if r < top else back


def attention_backward(spot, incoming, x, gain, normed, proj, logsum, mixed, total, layer, own, pieces, quarters):
    length, width = x.shape
    top = incoming.shape[0]
    n_t = proj.shape[0]
    last = quarters[-1] == n_t - 1
    count = len(quarters)
    inner = own[1].shape[1]
    if total is None:
        total = jnp.zeros((8, 128), F32)
    out = [jax.ShapeDtypeStruct((length, width), F32)]
    out_specs = [whole((length, width))]
    if last:
        out += [jax.ShapeDtypeStruct(v, F32) for v in ((length, width), (1, width), (1, width))]
        out_specs += [whole((length, width)), whole((1, width)), whole((1, width))]
    out += block_shapes(count, 1, width // GROUP, 4 * inner)
    out_specs += block_specs(1, width // GROUP, 4 * inner)
    return pl.pallas_call(
        functools.partial(attention_backward_kernel, quarters, last, layer, pieces.plan, len(pieces.arrays)),
        grid=(count,),
        out_shape=out,
        in_specs=[
            smem_spec(),
            whole((top, width)),
            whole((length, width)),
            whole((1, width)),
            whole((length, width)),
            per_quarter((length, 3 * inner), quarters[0]),
            whole((length, 128)),
            per_quarter((length, inner), quarters[0]),
            whole(total.shape),
        ]
        + [any_spec()] * (2 + len(pieces.arrays)),
        out_specs=out_specs,
        scratch_shapes=[
            pltpu.VMEM((count, width, 4 * inner), BF16),
            pltpu.VMEM((length, 3 * inner), BF16),
            pltpu.SemaphoreType.DMA((count,)),
            pltpu.VMEM((width, top), BF16),
            pltpu.VMEM((width, length), BF16),
            pltpu.VMEM((3, width, inner), BF16),
            pltpu.VMEM((inner, width), BF16),
        ],
        compiler_params=params(),
        cost_estimate=KERNEL_COST,
        name="attention_backward",
    )(spot, incoming, x, gain, normed, proj, logsum, mixed, total, *own, *pieces.arrays)


def swap(values, bit, size):
    return lax.ppermute(values, "dp", [(i, i ^ bit) for i in range(size)])


def after(values, *others):
    return lax.optimization_barrier((values, others))[0]


def gate(outs, *others):
    return lax.optimization_barrier((outs, others))


def small_call(kernel, grid, in_specs, out_specs, out_shape, name):
    return pl.pallas_call(
        kernel,
        grid=grid,
        in_specs=in_specs,
        out_specs=out_specs,
        out_shape=out_shape,
        compiler_params=params(SMALL_VMEM),
        cost_estimate=SMALL_COST,
        name=name,
    )


def pack_kernel(groups, *refs):
    sources, targets = refs[: -len(groups)], refs[-len(groups) :]
    rows = targets[0].shape[2]
    for k, source in enumerate(sources):
        for target, (first, count) in zip(targets, groups):
            for m in range(count):
                target[m, k] = source[(first + m) * rows : (first + m + 1) * rows, :]


def pack(sources, *counts):
    total, width = sources[0].shape
    rows = total // sum(counts)
    groups = [(sum(counts[:i]), count) for i, count in enumerate(counts)]
    shapes = [(count, len(sources), rows, width) for count in counts]
    return small_call(
        functools.partial(pack_kernel, groups),
        (1,),
        [whole((total, width))] * len(sources),
        [whole(shape) for shape in shapes],
        [jax.ShapeDtypeStruct(shape, BF16) for shape in shapes],
        "pack",
    )(*sources)


def corner(x_piece, y_piece, n_dp, by_x):
    return swap(y_piece, 2, n_dp) if by_x else swap(x_piece, 4, n_dp)


def sum_kernel(*refs):
    *operands, out = refs
    total = operands[0][...].astype(F32)
    for operand in operands[1:]:
        total = total + operand[...].astype(F32).reshape(total.shape)
    out[...] = total.astype(out.dtype).reshape(out.shape)


def mine_kernel(*refs):
    kept, got, first, second, *outs = refs
    for i, out in enumerate(outs):
        total = kept[0, i].astype(F32) + got[0, i].astype(F32) + first[0, i].astype(F32) + second[i].astype(F32)
        out[0] = total.astype(out.dtype)


def last_kernel(*refs):
    *parts, out = refs
    total = parts[0][...].astype(F32)
    for part in parts[1:]:
        total = total + part[...].astype(F32)
    out[...] = total


class Reduction:
    def __init__(self, keep, got, first, quarters, by_x, n_dp, n_t):
        self.keep, self.got, self.first, self.quarters = keep, got, first, quarters
        self.near, self.far = (2, 4) if by_x else (4, 2)
        self.n_dp, self.n_t = n_dp, n_t
        self.shape = keep.shape[2:]

    def plane(self, i):
        count = len(self.quarters)
        zeros = (0,) * len(self.shape)
        return pl.BlockSpec((1, count) + self.shape, lambda _: (i, self.first // count) + zeros)

    def near_sum(self, token):
        self.got = after(self.got, token)
        zeros = (0,) * len(self.shape)
        count = len(self.quarters)
        near = self.near // 2
        spec = pl.BlockSpec(
            (1, count) + self.shape, lambda i: (jnp.where(i == 0, near, 3), self.first // count) + zeros
        )
        out = small_call(
            sum_kernel,
            (2,),
            [spec, spec],
            pl.BlockSpec((1, count) + self.shape, lambda i: (i, 0) + zeros),
            jax.ShapeDtypeStruct((2, count) + self.shape, BF16),
            "near_sum",
        )(self.keep, self.got)
        self.from_near = swap(out, self.near, self.n_dp)
        return out

    def far_sum(self, token):
        self.from_near = after(self.from_near, token)
        zeros = (0,) * len(self.shape)
        count = len(self.quarters)
        full = (count,) + self.shape
        out = small_call(
            sum_kernel,
            (1,),
            [
                self.plane(self.far // 2),
                self.plane(self.far // 2),
                pl.BlockSpec((1,) + full, lambda _: (1, 0) + zeros),
            ],
            whole(full),
            jax.ShapeDtypeStruct(full, BF16),
            "far_sum",
        )(self.keep, self.got, self.from_near)
        self.from_far = swap(out, self.far, self.n_dp)
        return out

    def own_sum(self, token):
        self.from_far = after(self.from_far, token)
        zeros = (0,) * len(self.shape)
        full = (len(self.quarters),) + self.shape
        one = (1,) + self.shape
        outs = small_call(
            mine_kernel,
            (1,),
            [self.plane(0), self.plane(0), pl.BlockSpec((1,) + full, lambda _: (0, 0) + zeros), whole(full)],
            [whole(one)] * len(self.quarters),
            [jax.ShapeDtypeStruct(one, BF16 if k else F32) for k in self.quarters],
            "own_sum",
        )(self.keep, self.got, self.from_near, self.from_far)
        self.parts = [
            lax.ppermute(v, "tensor", [(j, (j - k) % self.n_t) for j in range(self.n_t)]) if k else v
            for k, v in zip(self.quarters, outs)
        ]
        return list(outs)


def finish(parts, n_dp):
    shape = parts[0].shape
    total = small_call(
        last_kernel, (1,), [whole(shape)] * len(parts), whole(shape), jax.ShapeDtypeStruct(shape, F32), "last_sum"
    )(*parts)
    return [spread_rows(total[0, m], n_dp) for m in range(shape[1])]


def spread_rows(total, n_dp):
    groups = n_dp // GROUP
    me = lax.axis_index("dp")
    rows = total.shape[0]
    bit = n_dp // 2
    while bit >= GROUP:
        rows //= 2
        second = (me // bit) % 2
        kept = lax.dynamic_slice_in_dim(total, second * rows, rows, 0)
        sent = lax.dynamic_slice_in_dim(total, (1 - second) * rows, rows, 0)
        total = kept + swap(sent, bit, n_dp)
        bit //= 2
    if groups > 1:
        total = lax.ppermute(
            total, "dp", [(h * GROUP + s, s * groups + h) for h in range(groups) for s in range(GROUP)]
        )
    return total


class SumAll:
    def __init__(self, values, n_dp, n_t):
        self.values, self.n_dp, self.n_t = values, n_dp, n_t
        self.bits = [("dp", 1 << i) for i in range(n_dp.bit_length() - 1)]
        self.bits += [("tensor", 1 << i) for i in range(n_t.bit_length() - 1)]
        self.got = None

    def step(self, token):
        if self.got is not None:
            self.values = self.values + after(self.got, token)
            self.got = None
        if self.bits:
            axis, bit = self.bits.pop(0)
            size = self.n_dp if axis == "dp" else self.n_t
            self.got = lax.ppermute(after(self.values, token), axis, [(i, i ^ bit) for i in range(size)])

    def result(self, token):
        while self.got is not None:
            self.step(token)
        return self.values


def shards(tokens, type_table, norm_gain, norm_bias, w_qkv, w_out, w_up, w_down, cotangent, positions, n_dp, n_t):
    total_rows, width = tokens.shape
    pair_count, slots = positions.shape
    assert pair_count == n_t
    length = total_rows // pair_count
    layers = w_qkv.shape[0]
    top = layers - 1
    inner = w_qkv.shape[3]
    me, quarter = lax.axis_index("dp"), lax.axis_index("tensor")
    rows = width // GROUP
    unit = width // n_dp
    spot = me % GROUP
    spots = jnp.reshape(spot, (1,)).astype(jnp.int32)

    def part_of(block):
        return lax.dynamic_slice_in_dim(block, spot * rows, rows, 0)

    mine = lax.dynamic_slice_in_dim(tokens, quarter * length, length, 0).astype(F32)
    row_ids = lax.broadcasted_iota(jnp.int32, (length, 1), 0)
    stream = mine + jnp.where(row_ids < WORDS, type_table[0], type_table[1])
    gains = [[norm_gain[l, i][None] for i in range(2)] for l in range(layers)]
    biases = [[norm_bias[l, i][None] for i in range(2)] for l in range(layers)]
    own_attn = (w_qkv.transpose(0, 2, 1, 3), w_out)
    own_mlp = (w_up, w_down)

    def attn_part(l):
        left = lax.dynamic_slice(w_qkv, (l, spot * rows, 0, 0), (1, rows, 3, inner)).reshape(rows, 3 * inner)
        right = lax.dynamic_slice(w_out, (l, 0, spot * rows), (1, inner, rows))[0].T
        return jnp.concatenate([left, right], 1)

    def mlp_part(l):
        return jnp.concatenate(
            [lax.dynamic_slice(w, (l, spot * rows, 0), (1, rows, w.shape[2]))[0] for w in (w_up, w_down)], 0
        )

    assert layers == 2
    near, far = 1, n_t - 1

    def hand_on(part, step):
        return lax.ppermute(part, "tensor", [(i, (i + step) % n_t) for i in range(n_t)])

    def to_neighbours(part):
        held = [None] * n_t
        held[near], held[far] = hand_on(part, 1), hand_on(part, -1)
        return held

    def passed_on(held):
        for k in range(2, far):
            held[k] = hand_on(held[k - 1], 1)
        return held[1:]

    def slices_of(matrices):
        return Pieces([[[(v, lead + (k,), 0) for v, lead in slices] for k in range(n_t - 1)] for slices in matrices])

    def core_swap(v):
        return swap(v, 1, n_dp)

    def one_matrix(own, x_piece, y_piece, way):
        own_c, x_c, y_c = core_swap(own), core_swap(x_piece), core_swap(y_piece)
        last = corner(x_piece, y_piece, n_dp, way)
        all_of = [own, own_c, x_piece, x_c, y_piece, y_c, last, core_swap(last)]
        return slices_of([[(v, (0,)) for v in all_of]])

    def two_matrices(own, x_piece, y_piece, token):
        own_c, x_c, y_c = core_swap(own), core_swap(x_piece), core_swap(y_piece)
        first, second = swap(after(x_piece, token)[0], 4, n_dp), swap(after(y_piece, token)[1], 2, n_dp)
        sides = [own, own_c, x_piece, x_c, y_piece, y_c]
        ends = [(first, core_swap(first)), (second, core_swap(second))]
        return slices_of(
            [[(v, (m,)) for v in sides] + [(v, ()) for v in ends[m]] for m in range(2)]
        )

    def sides_of(own):
        return swap(own, 2, n_dp), swap(own, 4, n_dp)

    def run_attention(l, x, pieces, work):
        return attention_forward(spots, x, gains[l][0], biases[l][0], l, own_attn, pieces, n_t, work)

    def run_feed_forward(l, x, pieces, keep, out_type):
        return mlp_forward(spots, x, gains[l][1], biases[l][1], l, own_mlp, pieces, n_t, keep, out_type)

    part_a, part_m = attn_part(0), mlp_part(0)
    part_l = jnp.concatenate([attn_part(1), mlp_part(1)], 0)
    held_a = to_neighbours(part_a)
    held_m = to_neighbours(after(part_m, (held_a[near], held_a[far])))
    hops_a = passed_on(held_a)
    hops_a[0] = after(hops_a[0], part_m)
    (own_a,) = pack(hops_a, 1)
    x_a, y_a = sides_of(own_a)
    held_m[near], held_m[far] = after((held_m[near], held_m[far]), (x_a, y_a))
    attn_pieces = [one_matrix(own_a, *after((x_a, y_a), held_m[near], held_m[far]), False)]
    held_l = to_neighbours(after(part_l, held_m[near], held_m[far]))
    hops_m = passed_on(held_m)
    hops_m[0] = after(hops_m[0], part_l)
    (own_m,) = pack(hops_m, 2)
    x_m, y_m = sides_of(own_m)
    first = run_attention(0, after(stream, own_m), attn_pieces[0], 40_000_000_000)
    first, ((held_l[near], held_l[far]),) = gate(first, (held_l[near], held_l[far]))
    x_m, y_m = after((x_m, y_m), first[0])
    mlp_pieces = [two_matrices(own_m, x_m, y_m, first[0])]
    hops_l = passed_on(held_l)
    own_a, own_m = pack(hops_l, 1, 2)
    x_a, y_a = sides_of(own_a)
    x_m, y_m = sides_of(own_m)
    second = run_feed_forward(0, after(first[0], own_a), mlp_pieces[0], True, F32)
    second, ((x_a, y_a),) = gate(second, (x_a, y_a))
    attn_pieces.append(one_matrix(own_a, x_a, y_a, True))
    third = run_attention(1, second[0], attn_pieces[1], 1_000_000)
    if SIDES_FIRST:
        x_m, y_m = after((x_m, y_m), third[0])
        third, ((x_m, y_m),) = gate(third, (x_m, y_m))
    mlp_pieces.append(two_matrices(own_m, x_m, y_m, third[0]))
    saved = [(stream, *first[1:], first[0], *second[1:]), (second[0], *third[1:], third[0])]

    def put_pairs(held):
        out = jnp.zeros((total_rows, width), F32)
        for k, v in enumerate(held):
            out = lax.dynamic_update_slice(out, v.astype(F32), (((quarter - k) % n_t) * length, 0))
        return out

    place = lax.dynamic_slice_in_dim(positions, quarter, 1, 0)[0]
    cot = lax.dynamic_slice_in_dim(cotangent, quarter, 1, 0)[0]
    onehot = (row_ids[:TOP_ROWS] == place[None, :]).astype(BF16)
    incoming = nn(onehot, cot)

    everything = tuple(range(n_t))
    halves = (everything[: n_t // 2], everything[n_t // 2 :])
    gain_grads = [[None, None] for _ in range(layers)]
    bias_grads = [[None, None] for _ in range(layers)]
    def reductions_of(keep, got, quarters):
        out = []
        for i, half in enumerate(halves):
            chosen = [k for k in half if k in quarters]
            if chosen:
                out.append(Reduction(keep, got, chosen[0] - quarters[0], chosen, i == 0, n_dp, n_t))
        return out

    stream_l, normed, proj, logsum, mixed, middle = saved[top]
    grad_middle, gain_grads[top][1], bias_grads[top][1], top_normed = top_backward(
        spots, incoming, middle, gains[top][1], biases[top][1], top, own_mlp, mlp_pieces[top], n_t
    )
    slot_rows = tn(onehot, top_normed).astype(BF16)
    slot_cot = jnp.where(place[:, None] >= 0, cot, 0)
    spare = jnp.zeros((SLOT_ROWS - slots, width), BF16)
    all_rows = lax.all_gather(jnp.concatenate([slot_cot, spare, slot_rows, spare], 0), ("dp", "tensor"))
    total, incoming, gain_grads[top][0], bias_grads[top][0], keep, send = attention_backward(
        spots, grad_middle, stream_l, gains[top][0], normed, proj, logsum, mixed, None,
        top, own_attn, attn_pieces[top], everything,
    )
    got = swap(send, 1, n_dp)
    (last_stream,) = run_feed_forward(top, after(middle, total), mlp_pieces[top], False, BF16)
    last_stream, (got,) = gate(last_stream, got)
    attn_top = reductions_of(keep, got, everything)
    ready = [r.near_sum(last_stream) for r in attn_top]
    hidden_held = to_neighbours(after(last_stream, ready))
    hidden_held[0] = last_stream

    stream_l, normed, proj, logsum, mixed, middle, normed_mlp, upward = saved[0]
    outs = mlp_backward(
        spots, after(incoming, ready), middle, gains[0][1], normed_mlp, upward, None,
        0, own_mlp, mlp_pieces[0], everything, True,
    )
    near_of = [r.from_near for r in attn_top]
    outs, (near_of, hidden_held) = gate(outs, near_of, hidden_held)
    for r, v in zip(attn_top, near_of):
        r.from_near = v
    incoming, gain_grads[0][1], bias_grads[0][1], keep, send = outs[1:]
    got = swap(send, 1, n_dp)
    hidden_held[1:] = passed_on(hidden_held)
    ready = [r.far_sum(incoming) for r in attn_top]

    outs = attention_backward(
        spots, after(incoming, ready), stream_l, gains[0][0], normed, proj, logsum, mixed, None,
        0, own_attn, attn_pieces[0], halves[0],
    )
    outs, (got, far_of, hidden_held) = gate(outs, got, [r.from_far for r in attn_top], hidden_held)
    for r, v in zip(attn_top, far_of):
        r.from_far = v
    total, keep_a, send_a = outs
    got_a = swap(send_a, 1, n_dp)
    mlp_low = reductions_of(keep, got, everything)
    ready = [r.near_sum(total) for r in mlp_low]
    ready += [r.own_sum(ready) for r in attn_top]

    outs = attention_backward(
        spots, after(incoming, ready), stream_l, gains[0][0], normed, proj, logsum, mixed, total,
        0, own_attn, attn_pieces[0], halves[1],
    )
    outs, (got_a,) = gate(outs, got_a)
    incoming, gain_grads[0][0], bias_grads[0][0], keep_b, send_b = outs[1:]
    (low_a,) = reductions_of(keep_a, got_a, halves[0])
    (low_b,) = reductions_of(keep_b, swap(send_b, 1, n_dp), halves[1])
    ready = low_a.near_sum(incoming)
    grad_tokens = lax.all_gather(incoming.astype(BF16), "tensor", tiled=True)

    all_rows = after(all_rows, ready)
    all_cot = all_rows[:, :SLOT_ROWS].reshape(-1, width)
    all_normed = all_rows[:, SLOT_ROWS:].reshape(-1, width)
    slot_up = nn(all_normed, w_up[top])
    slot_grad = (nt(all_cot, w_down[top]) * gelu_slope(slot_up)).astype(BF16)
    grad_up_top = tn(lax.dynamic_slice_in_dim(all_normed, me * unit, unit, 1), slot_grad)
    grad_down_top = tn(
        gelu(slot_up).astype(BF16), lax.dynamic_slice_in_dim(all_cot, me * unit, unit, 1)
    )

    ready = low_b.near_sum(ready)
    type_grad = jnp.stack([jnp.sum(incoming[:WORDS], 0), jnp.sum(incoming[WORDS:], 0)])
    rows_all = SumAll(
        jnp.concatenate(
            [type_grad] + [g for pair in gain_grads for g in pair] + [b for pair in bias_grads for b in pair], 0
        ),
        n_dp,
        n_t,
    )
    rows_all.step(ready)
    hidden_out = put_pairs(after(hidden_held, ready))
    ready = (hidden_out, grad_up_top, grad_down_top)
    for r in mlp_low:
        ready = r.far_sum(ready)
    rows_all.step(ready)
    sums = {}

    def finished(reductions, token):
        return finish(after([p for r in reductions for p in r.parts], token), n_dp)

    (sums["attn", top],) = finished(attn_top, ready)
    for r in (low_a, low_b):
        ready = r.far_sum(ready)
        rows_all.step(ready)
    for r in (*mlp_low, low_a, low_b):
        ready = r.own_sum(ready)
        rows_all.step(ready)
    rows_all = rows_all.result(ready)
    grad_tokens = after(grad_tokens, ready).astype(F32)
    sums["down", 0], sums["up", 0] = finished(mlp_low, ready)
    (sums["attn", 0],) = finished([low_a, low_b], (ready, grad_tokens, sums["down", 0], sums["up", 0]))

    rows_mine = lax.dynamic_slice_in_dim(rows_all, me * unit, unit, 1)
    grad_gain = rows_mine[2 : 2 + 2 * layers].reshape(layers, 2, unit)
    grad_bias = rows_mine[2 + 2 * layers :].reshape(layers, 2, unit)
    grad_qkv = jnp.stack([sums["attn", l][:, : 3 * inner].reshape(unit, 3, inner) for l in range(layers)])
    grad_out = jnp.stack([sums["attn", l][:, 3 * inner :].T for l in range(layers)])
    grad_up = jnp.stack([grad_up_top if l == top else sums["up", l] for l in range(layers)])
    grad_down = jnp.stack([grad_down_top if l == top else sums["down", l].T for l in range(layers)])
    return hidden_out, grad_tokens, rows_mine[:2], grad_gain, grad_bias, grad_qkv, grad_out, grad_up, grad_down


def solution(mesh):
    n_dp, n_t = mesh.shape["dp"], mesh.shape["tensor"]
    placed = (
        P("dp", None),
        P(),
        P(),
        P(),
        P(None, None, None, "tensor"),
        P(None, "tensor", None),
        P(None, None, "tensor"),
        P(None, "tensor", None),
        P("dp", None, None),
        P("dp", None),
    )

    def run(*args):
        return shards(*args, n_dp, n_t)

    return jax.shard_map(
        run,
        mesh=mesh,
        in_specs=placed,
        out_specs=(
            P("dp", None),
            P("dp", None),
            P(None, "dp"),
            P(None, None, "dp"),
            P(None, None, "dp"),
            P(None, "dp", None, "tensor"),
            P(None, "tensor", "dp"),
            P(None, "dp", "tensor"),
            P(None, "tensor", "dp"),
        ),
        check_vma=False,
    )
```

time: 445 us -> 393 us (0.88); the launches traced: 437 us -> 391 us
  waiting for transfers between devices: 164 us -> 121 us
  starting transfers between devices: 83 us -> 63.7 us
  between operations: 2.73 us -> 16.7 us
  local copies, waits for them, and re-layouts: 47.6 us -> 42.3 us
    ppermute x87 -> x48, waiting for transfers between devices: 80.5 us -> 37.3 us  [swap(): return lax.ppermute(values, 'dp', [(i, i ^ bit) for i in range(size)])]
    ppermute x87 -> x48, starting transfers between devices: 54.6 us -> 30 us  [swap(): return lax.ppermute(values, 'dp', [(i, i ^ bit) for i in range(size)])]
    all_gather x0 -> x2, waiting for transfers between devices: none -> 14.1 us  [the longest x1 14.1 us: shards(): lax.all_gather(jnp.concatenate([slot_cot, spare, slot_rows, spare], 0), (...]
    ppermute x32 -> x26, waiting for transfers between devices: 83.7 us -> 70 us  [the longest x12 38.3 us: hand_on(): lax.ppermute(part, 'tensor', [(i, (i + step) % n_t) for i in range(n_t)])]
    pallas_call x3 -> x1, Pallas kernels: 25.6 us -> 13 us  [mlp_backward(): pl.pallas_call(functools.partial(mlp_backward_kernel, quarters, last, blo...]
    pallas_call x34 -> x26, Pallas kernels: 55.9 us -> 67.4 us  [the longest x2 18.6 us: attention_forward(): pl.pallas_call(functools.partial(attention_forward_kernel, layer, pieces....]
    slice x4 -> x0, local copies, waits for them, and re-layouts: 6.31 us -> none  [the longest x1 2.46 us: shards(): w_qkv[l].reshape(width, 3 * inner)]
    convert_element_type x0 -> x2, other arithmetic: none -> 5.65 us  [the longest x1 3.3 us: shards(): grad_tokens = after(grad_tokens, ready).astype(F32)]
  transfers between devices with their start and end apart: 119 -> 76, of which waited for: 39 -> 30; matrix products, arithmetic and copies ran while one was open for 10% -> 12% of each run, Pallas kernels for 25% -> 23%
where the time goes in v2:
time: 393 us; the launch traced here: 391 us
  waiting for transfers between devices  121 us (31%)
  Pallas kernels  118 us (30%)
  starting transfers between devices  63.7 us (16%)
  local copies, waits for them, and re-layouts  42.3 us (11%)
  other arithmetic  18.3 us (5%)
  between operations  16.7 us (4%)
  matrix products  10.8 us (3%)
    ppermute x12, waiting for transfers between devices, hand_on(): lax.ppermute(part, 'tensor', [(i, (i + step) % n_t) for i in range(n_t)])  38.3 us
    ppermute x48, waiting for transfers between devices, swap(): return lax.ppermute(values, 'dp', [(i, i ^ bit) for i in range(size)])  37.3 us
    pallas_call x3, Pallas kernels, attention_backward(): pl.pallas_call(functools.partial(attention_backward_kernel, quarters, las...  36.2 us
    ppermute x48, starting transfers between devices, swap(): return lax.ppermute(values, 'dp', [(i, i ^ bit) for i in range(size)])  30 us
    ppermute x5, waiting for transfers between devices, step(): lax.ppermute(after(self.values, token), axis, [(i, i ^ bit) for i in rang...  24.3 us
    unnamed x159, local copies, waits for them, and re-layouts  24.1 us
    ppermute x12, starting transfers between devices, hand_on(): lax.ppermute(part, 'tensor', [(i, (i + step) % n_t) for i in range(n_t)])  19.5 us
    pallas_call x2, Pallas kernels, attention_forward(): pl.pallas_call(functools.partial(attention_forward_kernel, layer, pieces....  18.6 us
  transfers between devices with their start and end apart: 76, of which 30 were waited for; matrix products, arithmetic and copies ran while one was open for 12% of the time, Pallas kernels for 23%

profile of v2, /device:TPU:0, one launch (start us, length us, event | category | flops | bytes accessed | tf_op | source)
XLA Modules:
  0.0 391.0 jit_solution(14495382441474051442)
XLA Ops:
  10.7 3.1 collective-permute-start
  13.8 2.1 collective-permute-start.1
  15.9 4.7 %collective-permute-done.refs_0_ = bf16[96,768]{1,0:T(8,128)(2,1)S(1)} collective-permute-done((bf16[96,768]{1,0:T(8,128)(2,1)S(1)}, bf16[96,768]{1,0:T(8,128)(2,1)S(1)}, u32[]{:S(2)}, u32[]{:S(2)}) %collective-permute-start) | collective-permute-done | bytes 147488 | tf_op jit(solution)/shard_map/ppermute | solution.py:799
  22.3 5.2 %collective-permute-done.4.refs_1_ = bf16[96,768]{1,0:T(8,128)(2,1)S(1)} collective-permute-done((bf16[96,768]{1,0:T(8,128)(2,1)S(1)}, bf16[96,768]{1,0:T(8,128)(2,1)S(1)}, u32[]{:S(2)}, u32[]{:S(2)}) %collective-permute-start.4) | collective-permute-done | bytes 147488 | tf_op jit(solution)/shard_map/ppermute | solution.py:799
  30.8 3.8 collective-permute-start.3
  34.9 5.8 %collective-permute-done.2.refs_0_ = bf16[192,768]{1,0:T(8,128)(2,1)S(1)} collective-permute-done((bf16[192,768]{1,0:T(8,128)(2,1)S(1)}, bf16[192,768]{1,0:T(8,128)(2,1)S(1)}, u32[]{:S(2)}, u32[]{:S(2)}) %collective-permute-start.2) | collective-permute-done | bytes 294944 | tf_op jit(solution)/shard_map/ppermute | solution.py:799
  44.9 5.5 %collective-permute-done.11.rest_6_ = bf16[1,3,96,768]{3,2,1,0:T(8,128)(2,1)} collective-permute-done((bf16[1,3,96,768]{3,2,1,0:T(8,128)(2,1)S(1)}, bf16[1,3,96,768]{3,2,1,0:T(8,128)(2,1)}, u32[]{:S(2)}, u32[]{:S(2)}) %collective-permute-start.11) | collective-permute-done | bytes 442400 | tf_op jit(solution)/shard_map/ppermute | solution.py:565
  50.4 4.0 %copy.32 = bf16[2,768,3,192]{3,1,2,0:T(8,128)(2,1)} copy(bf16[2,768,3,192]{1,3,2,0:T(8,128)(2,1)} %param.14) | data formatting | bytes 3538944 | tf_op args[4]
  54.4 2.1 select_add_fusion.x
  56.5 3.3 collective-permute-start.13
  62.3 9.3 %attention_forward.2 = (f32[256,768]{1,0:T(8,128)}, bf16[256,768]{1,0:T(8,128)(2,1)}, bf16[4,256,576]{2,1,0:T(8,128)(2,1)}, f32[256,128]{1,0:T(8,128)}, bf16[4,256,192]{2,1,0:T(8,128)(2,1)}) custom-call(s32[1]{0:T(128)} %bitcast.spot_ref, f32[256,768]{1,0:T(8,128)} %select_add_fusion.x, f32[1,768]{1,0:T(1,128)} %get-tuple-element.380.gain, ...), custom_call_target="tpu_custom_call" | custom-call | flops 40000000000 | bytes 1000000 | tf_op jit(solution)/shard_map/attention_forward/pallas_call | solution.py:234
  71.6 8.8 %collective-permute-done.14.refs_2_ = bf16[288,768]{1,0:T(8,128)(2,1)S(1)} collective-permute-done((bf16[288,768]{1,0:T(8,128)(2,1)S(1)}, bf16[288,768]{1,0:T(8,128)(2,1)S(1)}, u32[]{:S(2)}, u32[]{:S(2)}) %collective-permute-start.14) | collective-permute-done | bytes 442400 | tf_op jit(solution)/shard_map/ppermute | solution.py:799
  86.9 7.4 %collective-permute-done.15.refs_1_ = bf16[288,768]{1,0:T(8,128)(2,1)S(1)} collective-permute-done((bf16[288,768]{1,0:T(8,128)(2,1)S(1)}, bf16[288,768]{1,0:T(8,128)(2,1)S(1)}, u32[]{:S(2)}, u32[]{:S(2)}) %collective-permute-start.15) | collective-permute-done | bytes 442400 | tf_op jit(solution)/shard_map/ppermute | solution.py:799
  100.0 8.0 %mlp_forward.2 = (f32[256,768]{1,0:T(8,128)}, bf16[256,768]{1,0:T(8,128)(2,1)}, f32[4,256,768]{2,1,0:T(8,128)}) custom-call(s32[1]{0:T(128)} %bitcast.spot_ref, f32[256,768]{1,0:T(8,128)} %get-tuple-element.189.x, f32[1,768]{1,0:T(1,128)} %get-tuple-element.381.gain, f32[1,768]{1,0:T(1,128)} %get-tuple-element.368.bias, bf16[2,768,768]{2,1,0:T(8,128)(2,1)} %rest_0_.1, ...), custom_call_target="tpu_custom_call" | custom-call | flops 40000000000 | bytes 1000000 | tf_op jit(solution)/shard_map/mlp_forward/pallas_call | solution.py:295
  113.5 9.7 %collective-permute-done.30.rest_6_ = bf16[1,3,96,768]{3,2,1,0:T(8,128)(2,1)S(1)} collective-permute-done((bf16[1,3,96,768]{3,2,1,0:T(8,128)(2,1)S(1)}, bf16[1,3,96,768]{3,2,1,0:T(8,128)(2,1)S(1)}, u32[]{:S(2)}, u32[]{:S(2)}) %collective-permute-start.30) | collective-permute-done | bytes 442400 | tf_op jit(solution)/shard_map/ppermute | solution.py:565
  125.8 9.3 %attention_forward.3 = (f32[256,768]{1,0:T(8,128)}, bf16[256,768]{1,0:T(8,128)(2,1)}, bf16[4,256,576]{2,1,0:T(8,128)(2,1)}, f32[256,128]{1,0:T(8,128)}, bf16[4,256,192]{2,1,0:T(8,128)(2,1)}) custom-call(s32[1]{0:T(128)} %bitcast.spot_ref, f32[256,768]{1,0:T(8,128)} %get-tuple-element.197.x, f32[1,768]{1,0:T(1,128)} %get-tuple-element.379.gain, ...), custom_call_target="tpu_custom_call" | custom-call | flops 1000000 | bytes 1000000 | tf_op jit(solution)/shard_map/attention_forward/pallas_call | solution.py:234
  135.1 4.9 %collective-permute-done.32.rest_2_ = bf16[2,3,96,768]{3,2,1,0:T(8,128)(2,1)} collective-permute-done((bf16[2,3,96,768]{3,2,1,0:T(8,128)(2,1)S(1)}, bf16[2,3,96,768]{3,2,1,0:T(8,128)(2,1)}, u32[]{:S(2)}, u32[]{:S(2)}) %collective-permute-start.32) | collective-permute-done | bytes 884768 | tf_op jit(solution)/shard_map/ppermute | solution.py:565
  145.9 5.1 %collective-permute-done.39.rest_8_ = bf16[3,96,768]{2,1,0:T(8,128)(2,1)S(1)} collective-permute-done((bf16[3,96,768]{2,1,0:T(8,128)(2,1)S(1)}, bf16[3,96,768]{2,1,0:T(8,128)(2,1)S(1)}, u32[]{:S(2)}, u32[]{:S(2)}) %collective-permute-start.39) | collective-permute-done | bytes 442400 | tf_op jit(solution)/shard_map/ppermute | solution.py:565
  151.0 2.0 collective-permute-done.37.rest_6_
  155.8 7.9 %top_backward.1 = (f32[48,768]{1,0:T(8,128)}, f32[1,768]{1,0:T(1,128)}, f32[1,768]{1,0:T(1,128)}, bf16[48,768]{1,0:T(8,128)(2,1)}) custom-call(s32[1]{0:T(128)} %bitcast.spot_ref, f32[48,768]{1,0:T(8,128)} %fusion.22.incoming, f32[256,768]{1,0:T(8,128)} %get-tuple-element.208.x, f32[1,768]{1,0:T(1,128)} %get-tuple-element.382.gain, ...), custom_call_target="tpu_custom_call" | custom-call | flops 40000000000 | bytes 1000000 | tf_op jit(solution)/shard_map/top_backward/pallas_call | solution.py:426
  164.3 15.2 %attention_backward.3 = (f32[256,768]{1,0:T(8,128)}, f32[256,768]{1,0:T(8,128)}, f32[1,768]{1,0:T(1,128)}, f32[1,768]{1,0:T(1,128)}, bf16[4,4,1,96,768]{4,3,2,1,...) custom-call(s32[1]{0:T(128)} %bitcast.spot_ref, f32[48,768]{1,0:T(8,128)} %get-tuple-element.213.incoming, ...), custom_call_target="tpu_custom_call" | custom-call | flops 40000000000 | bytes 1000000 | tf_op jit(solution)/shard_map/attention_backward/pallas_call | solution.py:532
  179.7 7.5 %mlp_forward.3 = bf16[256,768]{1,0:T(8,128)(2,1)} custom-call(s32[1]{0:T(128)} %bitcast.spot_ref, f32[256,768]{1,0:T(8,128)} %get-tuple-element.208.x, f32[1,768]{1,0:T(1,128)} %get-tuple-element.382.gain, f32[1,768]{1,0:T(1,128)} %get-tuple-element.367.bias, bf16[2,768,768]{2,1,0:T(8,128)(2,1)} %rest_0_.1, bf16[2,768,768]{2,1,0:T(8,128)(2,1)} %rest_1_.1, ...), custom_call_target="tpu_custom_call" | custom-call | flops 40000000000 | bytes 1000000 | tf_op jit(solution)/shard_map/mlp_forward/pallas_call | solution.py:295
  189.1 1.9 near_sum.6
  192.5 2.4 collective-permute-start.45
  196.7 13.0 %mlp_backward.1 = (f32[256,768]{1,0:T(8,128)}, f32[256,768]{1,0:T(8,128)}, f32[1,768]{1,0:T(1,128)}, f32[1,768]{1,0:T(1,128)}, bf16[4,4,2,96,768]{4,3,2,1,0:T(8,128)(2,1)}, /*index=5*/bf16[4,4,2,96,768]{4,3,2,1,0:T(8,128)(2,1)}) custom-call(s32[1]{0:T(128)} %bitcast.spot_ref, f32[256,768]{1,0:T(8,128)} %get-tuple-element.224.incoming, ...), custom_call_target="tpu_custom_call" | custom-call | flops 40000000000 | bytes 1000000 | tf_op jit(solution)/shard_map/mlp_backward/pallas_call | solution.py:376
  209.8 2.4 collective-permute-done.45
  220.5 9.9 %attention_backward.4 = (f32[256,768]{1,0:T(8,128)}, bf16[4,2,1,96,768]{4,3,2,1,0:T(8,128)(2,1)}, bf16[4,2,1,96,768]{4,3,2,1,0:T(8,128)(2,1)}) custom-call(s32[1]{0:T(128)} %bitcast.spot_ref, f32[256,768]{1,0:T(8,128)} %get-tuple-element.266.incoming, f32[256,768]{1,0:T(8,128)} %select_add_fusion.x, f32[1,768]{1,0:T(1,128)} %get-tuple-element.380.gain, ...), custom_call_target="tpu_custom_call" | custom-call | flops 40000000000 | bytes 1000000 | tf_op jit(solution)/shard_map/attention_backward/pallas_call | solution.py:532
  230.4 2.4 collective-permute-done.49
  232.8 2.5 copy-done.2
  235.3 2.2 near_sum.9
  237.5 2.4 near_sum.8
  247.3 11.1 %attention_backward.5 = (f32[256,768]{1,0:T(8,128)}, f32[256,768]{1,0:T(8,128)}, f32[1,768]{1,0:T(1,128)}, f32[1,768]{1,0:T(1,128)}, bf16[4,2,1,96,768]{4,3,2,1,...) custom-call(s32[1]{0:T(128)} %bitcast.spot_ref, f32[256,768]{1,0:T(8,128)} %get-tuple-element.266.incoming, ...), custom_call_target="tpu_custom_call" | custom-call | flops 40000000000 | bytes 1000000 | tf_op jit(solution)/shard_map/attention_backward/pallas_call | solution.py:532
  258.5 2.3 convert_element_type.38
  262.3 14.1 %all-gather.6.cloned.1.call-done = bf16[1024,768]{1,0:T(8,128)(2,1)} async-done(((bf16[32,768]{1,0:T(8,128)(2,1)}), bf16[1024,768]{1,0:T(8,128)(2,1)}) %all-gather.6.cloned.1.call-update) | async-done | bytes 1572880 | tf_op jit(solution)/shard_map/all_gather | solution.py:904
  276.3 2.6 fusion.36
  280.2 2.3 fusion.7
  283.6 2.2 fusion.14
  285.8 4.3 %fusion.6 = f32[96,768]{1,0:T(8,128)} fusion(f32[512,768]{1,0:T(8,128)} %copy-done.75, bf16[512,768]{1,0:T(8,128)(2,1)} %bitcast.104, bf16[2,768,768]{2,1,0:T(8,128)(2,1)} %rest_1_.1, bf16[512,768]{1,0:T(8,128)(2,1)} %bitcast.106, s32[]{:T(128)S(6)} %select_n.79), kind=kOutput, calls=%fused_computation.9 | convolution fusion | flops 683409408 | bytes 3964932 | tf_op jit(solution)/shard_map/dot_general | solution.py:27
  304.5 2.3 collective-permute-start.71
  313.4 3.1 collective-permute-done.71.refs_1_
  322.9 3.8 collective-permute-done.61
  332.8 2.3 copy-done.3
  336.6 2.4 collective-permute-start.68
  342.6 4.9 %collective-permute-done.63 = f32[10,768]{1,0:T(8,128)S(1)} collective-permute-done((f32[10,768]{1,0:T(8,128)S(1)}, f32[10,768]{1,0:T(8,128)S(1)}, u32[]{:S(2)}, u32[]{:S(2)}) %collective-permute-start.63) | collective-permute-done | bytes 30752 | tf_op jit(solution)/shard_map/ppermute | solution.py:752
  349.0 15.4 %collective-permute-done.64 = f32[10,768]{1,0:T(8,128)S(1)} collective-permute-done((f32[10,768]{1,0:T(8,128)S(1)}, f32[10,768]{1,0:T(8,128)S(1)}, u32[]{:S(2)}, u32[]{:S(2)}) %collective-permute-start.64) | collective-permute-done | bytes 30752 | tf_op jit(solution)/shard_map/ppermute | solution.py:752
  364.4 4.1 %collective-permute-start.65 = (bf16[1,1,96,768]{3,2,1,0:T(8,128)(2,1)S(1)}, bf16[1,1,96,768]{3,2,1,0:T(8,128)(2,1)S(1)}, u32[]{:S(2)}, u32[]{:S(2)}) collective-permute-start(bf16[1,1,96,768]{3,2,1,0:T(8,128)(2,1)S(1)} %get-tuple-element.298), channel_id=1, source_target_pairs={{0,3},{1,0},{2,1},{3,2},{4,7},{5,4},{6,5},{7,6},{8,11},{9,8},{10,9... | collective-permute-start | bytes 442376 | tf_op jit(solution)/shard_map/ppermute | solution.py:705
  373.6 3.3 convert_element_type.42
  376.9 4.3 %collective-permute-done.66.refs_2_ = bf16[1,1,96,768]{3,2,1,0:T(8,128)(2,1)S(1)} collective-permute-done((bf16[1,1,96,768]{3,2,1,0:T(8,128)(2,1)S(1)}, bf16[1,1,96,768]{3,2,1,0:T(8,128)(2,1)S(1)}, u32[]{:S(2)}, u32[]{:S(2)}) %collective-permute-start.66) | collective-permute-done | bytes 147488 | tf_op jit(solution)/shard_map/ppermute | solution.py:705
  (360 shorter events, 115.9 us)
Async XLA Ops:
  8.0 268.3 %all-gather.6.cloned.1.call-start = ((), (), s32[]{:S(2)}) async-start(), calls=%async_computation.1 | async-start | bytes 1622016 | tf_op jit(solution)/shard_map/all_gather | solution.py:904
  27.5 14.4 %collective-permute-start.5 = (bf16[1,3,96,768]{3,2,1,0:T(8,128)(2,1)S(1)}, bf16[1,3,96,768]{3,2,1,0:T(8,128)(2,1)S(1)}, u32[]{:S(2)}, u32[]{:S(2)}) collective-permute-start(bf16[1,3,96,768]{3,2,1,0:T(8,128)(2,1)S(1)} %pack.3.rest_0_), channel_id=1, source_target_pairs={{0,8},{4,12},{8,0},{12,4},{16,24},{20,28},{24,16},{28,20},{1,9},{5... | collective-permute-start | bytes 1327112 | tf_op jit(solution)/shard_map/ppermute | solution.py:565
  29.3 12.6 %collective-permute-start.6 = (bf16[1,3,96,768]{3,2,1,0:T(8,128)(2,1)S(1)}, bf16[1,3,96,768]{3,2,1,0:T(8,128)(2,1)S(1)}, u32[]{:S(2)}, u32[]{:S(2)}) collective-permute-start(bf16[1,3,96,768]{3,2,1,0:T(8,128)(2,1)S(1)} %pack.3.rest_0_), channel_id=1, source_target_pairs={{0,16},{4,20},{8,24},{12,28},{16,0},{20,4},{24,8},{28,12},{1,17},{... | collective-permute-start | bytes 1327112 | tf_op jit(solution)/shard_map/ppermute | solution.py:565
  43.7 16.2 %collective-permute-start.8 = (bf16[1,3,96,768]{3,2,1,0:T(8,128)(2,1)S(1)}, bf16[1,3,96,768]{3,2,1,0:T(8,128)(2,1)}, u32[]{:S(2)}, u32[]{:S(2)}) collective-permute-start(bf16[1,3,96,768]{3,2,1,0:T(8,128)(2,1)S(1)} %pack.3.rest_0_), channel_id=1, source_target_pairs={{0,4},{4,0},{8,12},{12,8},{16,20},{20,16},{24,28},{28,24},{1,5},{5... | collective-permute-start | bytes 1327112 | tf_op jit(solution)/shard_map/ppermute | solution.py:565
  43.7 17.7 %collective-permute-start.9 = (bf16[1,3,96,768]{3,2,1,0:T(8,128)(2,1)S(1)}, bf16[1,3,96,768]{3,2,1,0:T(8,128)(2,1)}, u32[]{:S(2)}, u32[]{:S(2)}) collective-permute-start(bf16[1,3,96,768]{3,2,1,0:T(8,128)(2,1)S(1)} %collective-permute-done.5.rest_2_), channel_id=1, source_target_pairs={{0,4},{4,0},{8,12},{12,8},{16,20},{20,16},{24,28},{28,24},{1,5},{5... | collective-permute-start | bytes 1327112 | tf_op jit(solution)/shard_map/ppermute | solution.py:565
  44.2 12.3 %collective-permute-start.7 = (bf16[192,768]{1,0:T(8,128)(2,1)S(1)}, bf16[192,768]{1,0:T(8,128)(2,1)S(1)}, u32[]{:S(2)}, u32[]{:S(2)}) collective-permute-start(bf16[192,768]{1,0:T(8,128)(2,1)S(1)} %collective-permute-done.2.refs_0_), channel_id=1, source_target_pairs={{0,1},{1,2},{2,3},{3,0},{4,5},{5,6},{6,7},{7,4},{8,9},{9,10},{10,1... | collective-permute-start | bytes 884744 | tf_op jit(solution)/shard_map/ppermute | solution.py:799
  44.9 15.5 %collective-permute-start.10 = (bf16[1,3,96,768]{3,2,1,0:T(8,128)(2,1)}, bf16[1,3,96,768]{3,2,1,0:T(8,128)(2,1)}, u32[]{:S(2)}, u32[]{:S(2)}) collective-permute-start(bf16[1,3,96,768]{3,2,1,0:T(8,128)(2,1)} %copy-done.67), channel_id=1, source_target_pairs={{0,4},{4,0},{8,12},{12,8},{16,20},{20,16},{24,28},{28,24},{1,5},{5... | collective-permute-start | bytes 1327112 | tf_op jit(solution)/shard_map/ppermute | solution.py:565
  50.4 11.9 %collective-permute-start.12 = (bf16[1,3,96,768]{3,2,1,0:T(8,128)(2,1)}, bf16[1,3,96,768]{3,2,1,0:T(8,128)(2,1)}, u32[]{:S(2)}, u32[]{:S(2)}) collective-permute-start(bf16[1,3,96,768]{3,2,1,0:T(8,128)(2,1)} %collective-permute-done.11.rest_6_), channel_id=1, source_target_pairs={{0,4},{4,0},{8,12},{12,8},{16,20},{20,16},{24,28},{28,24},{1,5},{5... | collective-permute-start | bytes 1327112 | tf_op jit(solution)/shard_map/ppermute | solution.py:565
  56.5 15.1 %collective-permute-start.13 = (bf16[288,768]{1,0:T(8,128)(2,1)S(1)}, bf16[288,768]{1,0:T(8,128)(2,1)S(1)}, u32[]{:S(2)}, u32[]{:S(2)}) collective-permute-start(bf16[288,768]{1,0:T(8,128)(2,1)S(1)} %pad_maximum_fusion.3), channel_id=1, source_target_pairs={{0,1},{1,2},{2,3},{3,0},{4,5},{5,6},{6,7},{7,4},{8,9},{9,10},{10,1... | collective-permute-start | bytes 1327112 | tf_op jit(solution)/shard_map/ppermute | solution.py:799
  59.8 20.5 %collective-permute-start.14 = (bf16[288,768]{1,0:T(8,128)(2,1)S(1)}, bf16[288,768]{1,0:T(8,128)(2,1)S(1)}, u32[]{:S(2)}, u32[]{:S(2)}) collective-permute-start(bf16[288,768]{1,0:T(8,128)(2,1)S(1)} %pad_maximum_fusion.3), channel_id=1, source_target_pairs={{0,3},{1,0},{2,1},{3,2},{4,7},{5,4},{6,5},{7,6},{8,11},{9,8},{10,9... | collective-permute-start | bytes 1327112 | tf_op jit(solution)/shard_map/ppermute | solution.py:799
  60.4 21.6 %collective-permute-start.17 = (bf16[2,3,96,768]{3,2,1,0:T(8,128)(2,1)S(1)}, bf16[2,3,96,768]{3,2,1,0:T(8,128)(2,1)}, u32[]{:S(2)}, u32[]{:S(2)}) collective-permute-start(bf16[2,3,96,768]{3,2,1,0:T(8,128)(2,1)S(1)} %pack.4.rest_0_.rest_2_), channel_id=1, source_target_pairs={{0,8},{4,12},{8,0},{12,4},{16,24},{20,28},{24,16},{28,20},{1,9},{5... | collective-permute-start | bytes 2654216 | tf_op jit(solution)/shard_map/ppermute | solution.py:565
  61.4 21.3 %collective-permute-start.18 = (bf16[2,3,96,768]{3,2,1,0:T(8,128)(2,1)S(1)}, bf16[2,3,96,768]{3,2,1,0:T(8,128)(2,1)}, u32[]{:S(2)}, u32[]{:S(2)}) collective-permute-start(bf16[2,3,96,768]{3,2,1,0:T(8,128)(2,1)S(1)} %pack.4.rest_0_.rest_2_), channel_id=1, source_target_pairs={{0,16},{4,20},{8,24},{12,28},{16,0},{20,4},{24,8},{28,12},{1,17},{... | collective-permute-start | bytes 2654216 | tf_op jit(solution)/shard_map/ppermute | solution.py:565
  62.3 35.1 %collective-permute-start.16 = (bf16[2,3,96,768]{3,2,1,0:T(8,128)(2,1)S(1)}, bf16[2,3,96,768]{3,2,1,0:T(8,128)(2,1)}, u32[]{:S(2)}, u32[]{:S(2)}) collective-permute-start(bf16[2,3,96,768]{3,2,1,0:T(8,128)(2,1)S(1)} %pack.4.rest_0_.rest_2_), channel_id=1, source_target_pairs={{0,4},{4,0},{8,12},{12,8},{16,20},{20,16},{24,28},{28,24},{1,5},{5... | collective-permute-start | bytes 2654216 | tf_op jit(solution)/shard_map/ppermute | solution.py:565
  80.4 14.0 %collective-permute-start.15 = (bf16[288,768]{1,0:T(8,128)(2,1)S(1)}, bf16[288,768]{1,0:T(8,128)(2,1)S(1)}, u32[]{:S(2)}, u32[]{:S(2)}) collective-permute-start(bf16[288,768]{1,0:T(8,128)(2,1)S(1)} %collective-permute-done.13.refs_0_), channel_id=1, source_target_pairs={{0,1},{1,2},{2,3},{3,0},{4,5},{5,6},{6,7},{7,4},{8,9},{9,10},{10,1... | collective-permute-start | bytes 1327112 | tf_op jit(solution)/shard_map/ppermute | solution.py:799
  86.9 13.0 %collective-permute-start.19 = (bf16[2,3,96,768]{3,2,1,0:T(8,128)(2,1)}, bf16[2,3,96,768]{3,2,1,0:T(8,128)(2,1)}, u32[]{:S(2)}, u32[]{:S(2)}) collective-permute-start(bf16[2,3,96,768]{3,2,1,0:T(8,128)(2,1)} %collective-permute-done.17.rest_2_.rest_4_), channel_id=1, source_target_pairs={{0,4},{4,0},{8,12},{12,8},{16,20},{20,16},{24,28},{28,24},{1,5},{5... | collective-permute-start | bytes 2654216 | tf_op jit(solution)/shard_map/ppermute | solution.py:565
  97.4 12.0 %collective-permute-start.25 = (bf16[1,3,96,768]{3,2,1,0:T(8,128)(2,1)S(1)}, bf16[1,3,96,768]{3,2,1,0:T(8,128)(2,1)S(1)}, u32[]{:S(2)}, u32[]{:S(2)}) collective-permute-start(bf16[1,3,96,768]{3,2,1,0:T(8,128)(2,1)S(1)} %get-tuple-element.188.rest_0_), channel_id=1, source_target_pairs={{0,8},{4,12},{8,0},{12,4},{16,24},{20,28},{24,16},{28,20},{1,9},{5... | collective-permute-start | bytes 1327112 | tf_op jit(solution)/shard_map/ppermute | solution.py:565
  98.3 11.7 %collective-permute-start.26 = (bf16[1,3,96,768]{3,2,1,0:T(8,128)(2,1)S(1)}, bf16[1,3,96,768]{3,2,1,0:T(8,128)(2,1)S(1)}, u32[]{:S(2)}, u32[]{:S(2)}) collective-permute-start(bf16[1,3,96,768]{3,2,1,0:T(8,128)(2,1)S(1)} %get-tuple-element.188.rest_0_), channel_id=1, source_target_pairs={{0,16},{4,20},{8,24},{12,28},{16,0},{20,4},{24,8},{28,12},{1,17},{... | collective-permute-start | bytes 1327112 | tf_op jit(solution)/shard_map/ppermute | solution.py:565
  99.2 13.7 %collective-permute-start.27 = (bf16[1,3,96,768]{3,2,1,0:T(8,128)(2,1)S(1)}, bf16[1,3,96,768]{3,2,1,0:T(8,128)(2,1)S(1)}, u32[]{:S(2)}, u32[]{:S(2)}) collective-permute-start(bf16[1,3,96,768]{3,2,1,0:T(8,128)(2,1)S(1)} %get-tuple-element.188.rest_0_), channel_id=1, source_target_pairs={{0,4},{4,0},{8,12},{12,8},{16,20},{20,16},{24,28},{28,24},{1,5},{5... | collective-permute-start | bytes 1327112 | tf_op jit(solution)/shard_map/ppermute | solution.py:565
  110.0 13.1 %collective-permute-start.30 = (bf16[1,3,96,768]{3,2,1,0:T(8,128)(2,1)S(1)}, bf16[1,3,96,768]{3,2,1,0:T(8,128)(2,1)S(1)}, u32[]{:S(2)}, u32[]{:S(2)}) collective-permute-start(bf16[1,3,96,768]{3,2,1,0:T(8,128)(2,1)S(1)} %collective-permute-done.26.rest_4_), channel_id=1, source_target_pairs={{0,8},{4,12},{8,0},{12,4},{16,24},{20,28},{24,16},{28,20},{1,9},{5... | collective-permute-start | bytes 1327112 | tf_op jit(solution)/shard_map/ppermute | solution.py:565
  111.1 28.8 %collective-permute-start.32 = (bf16[2,3,96,768]{3,2,1,0:T(8,128)(2,1)S(1)}, bf16[2,3,96,768]{3,2,1,0:T(8,128)(2,1)}, u32[]{:S(2)}, u32[]{:S(2)}) collective-permute-start(bf16[2,3,96,768]{3,2,1,0:T(8,128)(2,1)S(1)} %get-tuple-element.205.rest_0_), channel_id=1, source_target_pairs={{0,8},{4,12},{8,0},{12,4},{16,24},{20,28},{24,16},{28,20},{1,9},{5... | collective-permute-start | bytes 2654216 | tf_op jit(solution)/shard_map/ppermute | solution.py:565
  112.1 27.9 %collective-permute-start.33 = (bf16[2,3,96,768]{3,2,1,0:T(8,128)(2,1)S(1)}, bf16[2,3,96,768]{3,2,1,0:T(8,128)(2,1)}, u32[]{:S(2)}, u32[]{:S(2)}) collective-permute-start(bf16[2,3,96,768]{3,2,1,0:T(8,128)(2,1)S(1)} %get-tuple-element.205.rest_0_), channel_id=1, source_target_pairs={{0,16},{4,20},{8,24},{12,28},{16,0},{20,4},{24,8},{28,12},{1,17},{... | collective-permute-start | bytes 2654216 | tf_op jit(solution)/shard_map/ppermute | solution.py:565
  191.0 18.7 %collective-permute-start.44 = (bf16[256,768]{1,0:T(8,128)(2,1)S(1)}, bf16[256,768]{1,0:T(8,128)(2,1)}, u32[]{:S(2)}, u32[]{:S(2)}) collective-permute-start(bf16[256,768]{1,0:T(8,128)(2,1)S(1)} %copy-done.41), channel_id=1, source_target_pairs={{0,1},{1,2},{2,3},{3,0},{4,5},{5,6},{6,7},{7,4},{8,9},{9,10},{10,1... | collective-permute-start | bytes 1179656 | tf_op jit(solution)/shard_map/ppermute | solution.py:799
  192.5 19.6 %collective-permute-start.45 = (bf16[256,768]{1,0:T(8,128)(2,1)S(1)}, bf16[256,768]{1,0:T(8,128)(2,1)}, u32[]{:S(2)}, u32[]{:S(2)}) collective-permute-start(bf16[256,768]{1,0:T(8,128)(2,1)S(1)} %copy-done.41), channel_id=1, source_target_pairs={{0,3},{1,0},{2,1},{3,2},{4,7},{5,4},{6,5},{7,6},{8,11},{9,8},{10,9... | collective-permute-start | bytes 1179656 | tf_op jit(solution)/shard_map/ppermute | solution.py:799
  194.9 17.3 %collective-permute-start.43 = (bf16[2,2,1,96,768]{4,3,2,1,0:T(8,128)(2,1)}, bf16[2,2,1,96,768]{4,3,2,1,0:T(8,128)(2,1)S(1)}, u32[]{:S(2)}, u32[]{:S(2)}) collective-permute-start(bf16[2,2,1,96,768]{4,3,2,1,0:T(8,128)(2,1)} %near_sum.7), channel_id=1, source_target_pairs={{0,16},{4,20},{8,24},{12,28},{16,0},{20,4},{24,8},{28,12},{1,17},{... | collective-permute-start | bytes 1769480 | tf_op jit(solution)/shard_map/ppermute | solution.py:565
  195.8 16.4 %collective-permute-start.42 = (bf16[2,2,1,96,768]{4,3,2,1,0:T(8,128)(2,1)}, bf16[2,2,1,96,768]{4,3,2,1,0:T(8,128)(2,1)S(1)}, u32[]{:S(2)}, u32[]{:S(2)}) collective-permute-start(bf16[2,2,1,96,768]{4,3,2,1,0:T(8,128)(2,1)} %near_sum.6), channel_id=1, source_target_pairs={{0,8},{4,12},{8,0},{12,4},{16,24},{20,28},{24,16},{28,20},{1,9},{5... | collective-permute-start | bytes 1769480 | tf_op jit(solution)/shard_map/ppermute | solution.py:565
  212.2 20.7 %collective-permute-start.46 = (bf16[4,4,2,96,768]{4,3,2,1,0:T(8,128)(2,1)}, bf16[4,4,2,96,768]{4,3,2,1,0:T(8,128)(2,1)}, u32[]{:S(2)}, u32[]{:S(2)}) collective-permute-start(bf16[4,4,2,96,768]{4,3,2,1,0:T(8,128)(2,1)} %get-tuple-element.246), channel_id=1, source_target_pairs={{0,4},{4,0},{8,12},{12,8},{16,20},{20,16},{24,28},{28,24},{1,5},{5... | collective-permute-start | bytes 14155784 | tf_op jit(solution)/shard_map/ppermute | solution.py:565
  215.0 158.6 %all-gather.4.cloned.1.call-start = ((), (), s32[]{:S(2)}) async-start(), calls=%async_computation | async-start | bytes 1966080 | tf_op jit(solution)/shard_map/all_gather | solution.py:953
  216.9 13.5 %collective-permute-start.48 = (bf16[2,1,96,768]{3,2,1,0:T(8,128)(2,1)}, bf16[2,1,96,768]{3,2,1,0:T(8,128)(2,1)}, u32[]{:S(2)}, u32[]{:S(2)}) collective-permute-start(bf16[2,1,96,768]{3,2,1,0:T(8,128)(2,1)} %far_sum.7), channel_id=1, source_target_pairs={{0,8},{4,12},{8,0},{12,4},{16,24},{20,28},{24,16},{28,20},{1,9},{5... | collective-permute-start | bytes 884744 | tf_op jit(solution)/shard_map/ppermute | solution.py:565
  218.7 11.8 %collective-permute-start.47 = (bf16[2,1,96,768]{3,2,1,0:T(8,128)(2,1)S(1)}, bf16[2,1,96,768]{3,2,1,0:T(8,128)(2,1)S(1)}, u32[]{:S(2)}, u32[]{:S(2)}) collective-permute-start(bf16[2,1,96,768]{3,2,1,0:T(8,128)(2,1)S(1)} %far_sum.6), channel_id=1, source_target_pairs={{0,16},{4,20},{8,24},{12,28},{16,0},{20,4},{24,8},{28,12},{1,17},{... | collective-permute-start | bytes 884744 | tf_op jit(solution)/shard_map/ppermute | solution.py:565
  219.0 13.8 %collective-permute-start.49 = (bf16[256,768]{1,0:T(8,128)(2,1)}, bf16[256,768]{1,0:T(8,128)(2,1)S(1)}, u32[]{:S(2)}, u32[]{:S(2)}) collective-permute-start(bf16[256,768]{1,0:T(8,128)(2,1)} %collective-permute-done.44), channel_id=1, source_target_pairs={{0,1},{1,2},{2,3},{3,0},{4,5},{5,6},{6,7},{7,4},{8,9},{9,10},{10,1... | collective-permute-start | bytes 1179656 | tf_op jit(solution)/shard_map/ppermute | solution.py:799
  239.9 59.9 %collective-permute-start.55 = (bf16[2,2,2,96,768]{4,3,2,1,0:T(8,128)(2,1)}, bf16[2,2,2,96,768]{4,3,2,1,0:T(8,128)(2,1)}, u32[]{:S(2)}, u32[]{:S(2)}) collective-permute-start(bf16[2,2,2,96,768]{4,3,2,1,0:T(8,128)(2,1)} %near_sum.8), channel_id=1, source_target_pairs={{0,8},{4,12},{8,0},{12,4},{16,24},{20,28},{24,16},{28,20},{1,9},{5... | collective-permute-start | bytes 3538952 | tf_op jit(solution)/shard_map/ppermute | solution.py:565
  241.3 63.2 %collective-permute-start.54 = (bf16[2,2,2,96,768]{4,3,2,1,0:T(8,128)(2,1)}, bf16[2,2,2,96,768]{4,3,2,1,0:T(8,128)(2,1)S(1)}, u32[]{:S(2)}, u32[]{:S(2)}) collective-permute-start(bf16[2,2,2,96,768]{4,3,2,1,0:T(8,128)(2,1)} %near_sum.9), channel_id=1, source_target_pairs={{0,16},{4,20},{8,24},{12,28},{16,0},{20,4},{24,8},{28,12},{1,17},{... | collective-permute-start | bytes 3538952 | tf_op jit(solution)/shard_map/ppermute | solution.py:565
  246.7 64.4 %collective-permute-start.72 = (bf16[1,1,96,768]{3,2,1,0:T(8,128)(2,1)}, bf16[1,1,96,768]{3,2,1,0:T(8,128)(2,1)}, u32[]{:S(2)}, u32[]{:S(2)}) collective-permute-start(bf16[1,1,96,768]{3,2,1,0:T(8,128)(2,1)} %get-tuple-element.264), channel_id=1, source_target_pairs={{0,2},{1,3},{2,0},{3,1},{4,6},{5,7},{6,4},{7,5},{8,10},{9,11},{10,... | collective-permute-start | bytes 442376 | tf_op jit(solution)/shard_map/ppermute | solution.py:705
  246.7 66.1 %collective-permute-start.73 = (bf16[1,1,96,768]{3,2,1,0:T(8,128)(2,1)}, bf16[1,1,96,768]{3,2,1,0:T(8,128)(2,1)}, u32[]{:S(2)}, u32[]{:S(2)}) collective-permute-start(bf16[1,1,96,768]{3,2,1,0:T(8,128)(2,1)} %get-tuple-element.265), channel_id=1, source_target_pairs={{0,1},{1,2},{2,3},{3,0},{4,5},{5,6},{6,7},{7,4},{8,9},{9,10},{10,1... | collective-permute-start | bytes 442376 | tf_op jit(solution)/shard_map/ppermute | solution.py:705
  279.0 13.7 %collective-permute-start.51 = (bf16[4,2,1,96,768]{4,3,2,1,0:T(8,128)(2,1)}, bf16[4,2,1,96,768]{4,3,2,1,0:T(8,128)(2,1)S(1)}, u32[]{:S(2)}, u32[]{:S(2)}) collective-permute-start(bf16[4,2,1,96,768]{4,3,2,1,0:T(8,128)(2,1)} %get-tuple-element.274), channel_id=1, source_target_pairs={{0,4},{4,0},{8,12},{12,8},{16,20},{20,16},{24,28},{28,24},{1,5},{5... | collective-permute-start | bytes 3538952 | tf_op jit(solution)/shard_map/ppermute | solution.py:565
  292.7 15.5 %collective-permute-start.53 = (bf16[2,2,1,96,768]{4,3,2,1,0:T(8,128)(2,1)S(1)}, bf16[2,2,1,96,768]{4,3,2,1,0:T(8,128)(2,1)S(1)}, u32[]{:S(2)}, u32[]{:S(2)}) collective-permute-start(bf16[2,2,1,96,768]{4,3,2,1,0:T(8,128)(2,1)S(1)} %near_sum.10), channel_id=1, source_target_pairs={{0,8},{4,12},{8,0},{12,4},{16,24},{20,28},{24,16},{28,20},{1,9},{5... | collective-permute-start | bytes 1769480 | tf_op jit(solution)/shard_map/ppermute | solution.py:565
  301.5 26.6 %collective-permute-start.52 = (bf16[2,2,1,96,768]{4,3,2,1,0:T(8,128)(2,1)}, bf16[2,2,1,96,768]{4,3,2,1,0:T(8,128)(2,1)}, u32[]{:S(2)}, u32[]{:S(2)}) collective-permute-start(bf16[2,2,1,96,768]{4,3,2,1,0:T(8,128)(2,1)} %near_sum.11), channel_id=1, source_target_pairs={{0,16},{4,20},{8,24},{12,28},{16,0},{20,4},{24,8},{28,12},{1,17},{... | collective-permute-start | bytes 1769480 | tf_op jit(solution)/shard_map/ppermute | solution.py:565
  304.5 12.1 %collective-permute-start.71 = (bf16[1,1,96,768]{3,2,1,0:T(8,128)(2,1)S(1)}, bf16[1,1,96,768]{3,2,1,0:T(8,128)(2,1)S(1)}, u32[]{:S(2)}, u32[]{:S(2)}) collective-permute-start(bf16[1,1,96,768]{3,2,1,0:T(8,128)(2,1)S(1)} %copy-done.24), channel_id=1, source_target_pairs={{0,3},{1,0},{2,1},{3,2},{4,7},{5,4},{6,5},{7,6},{8,11},{9,8},{10,9... | collective-permute-start | bytes 442376 | tf_op jit(solution)/shard_map/ppermute | solution.py:705
  308.2 24.6 %collective-permute-start.59 = (bf16[2,2,96,768]{3,2,1,0:T(8,128)(2,1)S(1)}, bf16[2,2,96,768]{3,2,1,0:T(8,128)(2,1)S(1)}, u32[]{:S(2)}, u32[]{:S(2)}) collective-permute-start(bf16[2,2,96,768]{3,2,1,0:T(8,128)(2,1)S(1)} %far_sum.8), channel_id=1, source_target_pairs={{0,16},{4,20},{8,24},{12,28},{16,0},{20,4},{24,8},{28,12},{1,17},{... | collective-permute-start | bytes 1769480 | tf_op jit(solution)/shard_map/ppermute | solution.py:565
  311.1 27.9 %collective-permute-start.58 = (bf16[2,2,96,768]{3,2,1,0:T(8,128)(2,1)S(1)}, bf16[2,2,96,768]{3,2,1,0:T(8,128)(2,1)S(1)}, u32[]{:S(2)}, u32[]{:S(2)}) collective-permute-start(bf16[2,2,96,768]{3,2,1,0:T(8,128)(2,1)S(1)} %far_sum.9), channel_id=1, source_target_pairs={{0,8},{4,12},{8,0},{12,4},{16,24},{20,28},{24,16},{28,20},{1,9},{5... | collective-permute-start | bytes 1769480 | tf_op jit(solution)/shard_map/ppermute | solution.py:565
  312.8 28.4 %collective-permute-start.57 = (bf16[2,1,96,768]{3,2,1,0:T(8,128)(2,1)}, bf16[2,1,96,768]{3,2,1,0:T(8,128)(2,1)}, u32[]{:S(2)}, u32[]{:S(2)}) collective-permute-start(bf16[2,1,96,768]{3,2,1,0:T(8,128)(2,1)} %far_sum.10), channel_id=1, source_target_pairs={{0,16},{4,20},{8,24},{12,28},{16,0},{20,4},{24,8},{28,12},{1,17},{... | collective-permute-start | bytes 884744 | tf_op jit(solution)/shard_map/ppermute | solution.py:565
  327.6 11.4 %collective-permute-start.62 = (f32[10,768]{1,0:T(8,128)S(1)}, f32[10,768]{1,0:T(8,128)S(1)}, u32[]{:S(2)}, u32[]{:S(2)}) collective-permute-start(f32[10,768]{1,0:T(8,128)S(1)} %add.95), channel_id=1, source_target_pairs={{0,16},{4,20},{8,24},{12,28},{16,0},{20,4},{24,8},{28,12},{1,17},{... | collective-permute-start | bytes 92168 | tf_op jit(solution)/shard_map/ppermute | solution.py:752
  331.7 38.0 %collective-permute-start.56 = (bf16[2,1,96,768]{3,2,1,0:T(8,128)(2,1)S(1)}, bf16[2,1,96,768]{3,2,1,0:T(8,128)(2,1)S(1)}, u32[]{:S(2)}, u32[]{:S(2)}) collective-permute-start(bf16[2,1,96,768]{3,2,1,0:T(8,128)(2,1)S(1)} %far_sum.11), channel_id=1, source_target_pairs={{0,8},{4,12},{8,0},{12,4},{16,24},{20,28},{24,16},{28,20},{1,9},{5... | collective-permute-start | bytes 884744 | tf_op jit(solution)/shard_map/ppermute | solution.py:565
  336.6 34.9 %collective-permute-start.68 = (bf16[1,2,96,768]{3,2,1,0:T(8,128)(2,1)S(1)}, bf16[1,2,96,768]{3,2,1,0:T(8,128)(2,1)S(1)}, u32[]{:S(2)}, u32[]{:S(2)}) collective-permute-start(bf16[1,2,96,768]{3,2,1,0:T(8,128)(2,1)S(1)} %get-tuple-element.292), channel_id=1, source_target_pairs={{0,3},{1,0},{2,1},{3,2},{4,7},{5,4},{6,5},{7,6},{8,11},{9,8},{10,9... | collective-permute-start | bytes 884744 | tf_op jit(solution)/shard_map/ppermute | solution.py:705
  340.6 30.3 %collective-permute-start.69 = (bf16[1,2,96,768]{3,2,1,0:T(8,128)(2,1)S(1)}, bf16[1,2,96,768]{3,2,1,0:T(8,128)(2,1)S(1)}, u32[]{:S(2)}, u32[]{:S(2)}) collective-permute-start(bf16[1,2,96,768]{3,2,1,0:T(8,128)(2,1)S(1)} %get-tuple-element.294), channel_id=1, source_target_pairs={{0,2},{1,3},{2,0},{3,1},{4,6},{5,7},{6,4},{7,5},{8,10},{9,11},{10,... | collective-permute-start | bytes 884744 | tf_op jit(solution)/shard_map/ppermute | solution.py:705
  341.3 30.2 %collective-permute-start.70 = (bf16[1,2,96,768]{3,2,1,0:T(8,128)(2,1)S(1)}, bf16[1,2,96,768]{3,2,1,0:T(8,128)(2,1)S(1)}, u32[]{:S(2)}, u32[]{:S(2)}) collective-permute-start(bf16[1,2,96,768]{3,2,1,0:T(8,128)(2,1)S(1)} %get-tuple-element.295), channel_id=1, source_target_pairs={{0,1},{1,2},{2,3},{3,0},{4,5},{5,6},{6,7},{7,4},{8,9},{9,10},{10,1... | collective-permute-start | bytes 884744 | tf_op jit(solution)/shard_map/ppermute | solution.py:705
  347.5 16.9 %collective-permute-start.64 = (f32[10,768]{1,0:T(8,128)S(1)}, f32[10,768]{1,0:T(8,128)S(1)}, u32[]{:S(2)}, u32[]{:S(2)}) collective-permute-start(f32[10,768]{1,0:T(8,128)S(1)} %add.97), channel_id=1, source_target_pairs={{0,2},{1,3},{2,0},{3,1},{4,6},{5,7},{6,4},{7,5},{8,10},{9,11},{10,... | collective-permute-start | bytes 92168 | tf_op jit(solution)/shard_map/ppermute | solution.py:752
  364.4 12.5 %collective-permute-start.65 = (bf16[1,1,96,768]{3,2,1,0:T(8,128)(2,1)S(1)}, bf16[1,1,96,768]{3,2,1,0:T(8,128)(2,1)S(1)}, u32[]{:S(2)}, u32[]{:S(2)}) collective-permute-start(bf16[1,1,96,768]{3,2,1,0:T(8,128)(2,1)S(1)} %get-tuple-element.298), channel_id=1, source_target_pairs={{0,3},{1,0},{2,1},{3,2},{4,7},{5,4},{6,5},{7,6},{8,11},{9,8},{10,9... | collective-permute-start | bytes 442376 | tf_op jit(solution)/shard_map/ppermute | solution.py:705
  (106 other events, 939.0 us)
Sparse Core Ops, SparseCore 0:
  215.2 61.1 all-gather.5
Sparse Core Ops, SparseCore 1:
  279.3 39.5 all-gather.3

commit v3 on v2

--- a/solution.py
+++ b/solution.py
@@ -146,7 +146,7 @@
     half = block.shape[0] // 2
     rows = half // (GROUP // 2)
     for i in range(GROUP // 2):
-        keep[i, 0, part, :, columns] = block[i * rows : (i + 1) * rows].astype(BF16)
+        keep[i][0, part, :, columns] = block[i * rows : (i + 1) * rows].astype(BF16)
         send[i, 0, part, :, columns] = block[half + i * rows : half + (i + 1) * rows].astype(BF16)
 
 
@@ -167,11 +167,15 @@
 
 
 def block_specs(matrices, rows, width):
-    return [pl.BlockSpec((GROUP // 2, 1, matrices, rows, width), lambda k: (0, k, 0, 0, 0))] * 2
+    own = pl.BlockSpec((1, matrices, rows, width), lambda k: (k, 0, 0, 0))
+    return [own] * (GROUP // 2) + [
+        pl.BlockSpec((GROUP // 2, 1, matrices, rows, width), lambda k: (0, k, 0, 0, 0))
+    ]
 
 
 def block_shapes(quarters, matrices, rows, width):
-    return [jax.ShapeDtypeStruct((GROUP // 2, quarters, matrices, rows, width), BF16)] * 2
+    own = jax.ShapeDtypeStruct((quarters, matrices, rows, width), BF16)
+    return [own] * (GROUP // 2) + [jax.ShapeDtypeStruct((GROUP // 2, quarters, matrices, rows, width), BF16)]
 
 
 def params(limit=VMEM_BYTES):
@@ -185,7 +189,7 @@
 def attention_forward_kernel(layer, plan, count, spot_ref, x, gain, bias, own_qkv, own_out, *rest):
     middle, normed, proj, logsum, mixed, block, sems, raw_qkv, raw_out = rest[count:]
     k = pl.program_id(0)
-    inner = mixed.shape[-1]
+    inner = raw_out.shape[0]
     heads = inner // HD
 
     @pl.when(k == 0)
@@ -203,21 +207,25 @@
     def _():
         arrived(k, [block], sems)
 
-    proj[0] = nn(normed[...], block[k, :, : 3 * inner]).astype(BF16)
+    proj[0] = nn(normed[...], block[k])[:, : 3 * inner].astype(BF16)
     lane = lax.broadcasted_iota(jnp.int32, logsum.shape, 1)
-    for h in range(heads):
-        own_lanes = slice(h * HD, (h + 1) * HD)
-        queries = proj[0, :, own_lanes] * jnp.asarray(HD**-0.5, BF16)
-        keys = proj[0, :, inner + h * HD : inner + (h + 1) * HD]
-        values = proj[0, :, 2 * inner + h * HD : 2 * inner + (h + 1) * HD]
-        scores = nt(queries, keys)
-        top = jnp.max(scores, axis=-1, keepdims=True)
-        powers = jnp.exp(scores - top)
-        total = jnp.sum(powers, axis=-1, keepdims=True)
-        logsum[...] = jnp.where(lane == k * heads + h, top + jnp.log(total), logsum[...])
-        weights = (powers * (1.0 / total)).astype(BF16)
-        mixed[0, :, own_lanes] = nn(weights, values).astype(BF16)
-    middle[...] += nt(mixed[0], block[k, :, 3 * inner :]).astype(BF16).astype(F32)
+    every = range(heads)
+    lanes = [slice(h * HD, (h + 1) * HD) for h in range(3 * heads)]
+    scores = [
+        nt(proj[0, :, lanes[h]] * jnp.asarray(HD**-0.5, BF16), proj[0, :, lanes[heads + h]]) for h in every
+    ]
+    tops = [jnp.max(v, axis=-1, keepdims=True) for v in scores]
+    powers = [jnp.exp(v - t) for v, t in zip(scores, tops)]
+    totals = [jnp.sum(v, axis=-1, keepdims=True) for v in powers]
+    kept = logsum[...]
+    for h in every:
+        kept = jnp.where(lane == k * heads + h, tops[h] + jnp.log(totals[h]), kept)
+    logsum[...] = kept
+    weights = [(v * (1.0 / t)).astype(BF16) for v, t in zip(powers, totals)]
+    mixes = [nn(weights[h], proj[0, :, lanes[2 * heads + h]]).astype(BF16) for h in every]
+    pad = mixed.shape[2] - inner
+    mixed[0] = jnp.concatenate([jnp.zeros((normed.shape[0], pad), BF16)] + mixes, 1)
+    middle[...] += nt(mixed[0], block[k, :, 3 * inner - pad :]).astype(BF16).astype(F32)
 
 
 def attention_forward(spot, x, gain, bias, layer, own, pieces, n_t, work):
@@ -229,7 +237,7 @@
         jax.ShapeDtypeStruct((length, width), BF16),
         jax.ShapeDtypeStruct((n_t, length, 3 * inner), BF16),
         jax.ShapeDtypeStruct((length, 128), F32),
-        jax.ShapeDtypeStruct((n_t, length, inner), BF16),
+        jax.ShapeDtypeStruct((n_t, length, inner + inner % 128), BF16),
     ]
     return pl.pallas_call(
         functools.partial(attention_forward_kernel, layer, pieces.plan, count),
@@ -241,7 +249,7 @@
             whole((length, width)),
             per_quarter((length, 3 * inner)),
             whole((length, 128)),
-            per_quarter((length, inner)),
+            per_quarter((length, inner + inner % 128)),
         ],
         scratch_shapes=[
             pltpu.VMEM((n_t, width, 4 * inner), BF16),
@@ -319,7 +327,7 @@
     if last:
         grad, gain_grad, bias_grad = (rest.pop(0) for _ in range(3))
     if blocks:
-        keep, send = rest.pop(0), rest.pop(0)
+        keep, send = [rest.pop(0) for _ in range(GROUP // 2)], rest.pop(0)
     ups, downs, sems, *flipped = rest
     k = pl.program_id(0)
 
@@ -358,7 +366,7 @@
     last = quarters[-1] == n_t - 1
     count = len(quarters)
     if total is None:
-        total = jnp.zeros((8, 128), F32)
+        total = gain
     out = [jax.ShapeDtypeStruct((length, width), F32)]
     out_specs = [whole((length, width))]
     if last:
@@ -395,8 +403,8 @@
     )(spot, incoming, x, gain, normed, upward, total, *own, *pieces.arrays)
 
 
-def top_kernel(layer, plan, count, spot_ref, incoming, x, gain, bias, own_up, own_down, *rest):
-    grad, gain_grad, bias_grad, normed, ups, downs, total, sems = rest[count:]
+def top_kernel(layer, plan, count, spot_ref, incoming, x, gain, bias, pick, slots, own_up, own_down, *rest):
+    grad, gain_grad, bias_grad, packed, ups, downs, total, sems, normed = rest[count:]
     k = pl.program_id(0)
 
     @pl.when(k == 0)
@@ -404,6 +412,8 @@
         fetch(spot_ref[0], layer, [own_up, own_down], plan, rest[:count], [ups, downs], sems, range(ups.shape[0]))
         norm_rows(x, gain, bias, normed)
         total[...] = jnp.zeros_like(total)
+        packed[:SLOT_ROWS, :] = slots[...]
+        packed[SLOT_ROWS:, :] = nn(pick[...], normed[...]).astype(BF16)
 
     arrived(k, [ups, downs], sems)
     up = nn(normed[...], ups[k])
@@ -419,7 +429,7 @@
             grad[rows, :] = incoming[rows, :] + norm_back_rows(rows, x, gain, total, gain_grad, bias_grad)
 
 
-def top_backward(spot, incoming, x, gain, bias, layer, own, pieces, n_t):
+def top_backward(spot, incoming, x, gain, bias, pick, slots, layer, own, pieces, n_t):
     length, width = incoming.shape
     rows = pl.BlockSpec((length, width), lambda k: (0, 0))
     row = whole((1, width))
@@ -430,20 +440,21 @@
             jax.ShapeDtypeStruct((length, width), F32),
             jax.ShapeDtypeStruct((1, width), F32),
             jax.ShapeDtypeStruct((1, width), F32),
-            jax.ShapeDtypeStruct((length, width), BF16),
+            jax.ShapeDtypeStruct((2 * SLOT_ROWS, width), BF16),
         ],
-        in_specs=[smem_spec(), rows, rows, row, row] + [any_spec()] * (2 + len(pieces.arrays)),
-        out_specs=[rows, row, row, rows],
+        in_specs=[smem_spec(), rows, rows, row, row, whole(pick.shape), whole(slots.shape)] + [any_spec()] * (2 + len(pieces.arrays)),
+        out_specs=[rows, row, row, whole((2 * SLOT_ROWS, width))],
         scratch_shapes=[
             pltpu.VMEM((n_t,) + own[0].shape[1:], BF16),
             pltpu.VMEM((n_t,) + own[1].shape[1:], BF16),
             pltpu.VMEM((length, width), F32),
             pltpu.SemaphoreType.DMA((n_t,)),
+            pltpu.VMEM((length, width), BF16),
         ],
         compiler_params=params(),
         cost_estimate=KERNEL_COST,
         name="top_backward",
-    )(spot, incoming, x, gain, bias, *own, *pieces.arrays)
+    )(spot, incoming, x, gain, bias, pick, slots, *own, *pieces.arrays)
 
 
 def attention_backward_kernel(
@@ -453,11 +464,12 @@
     rest = list(rest[count:])
     total = rest.pop(0)
     if last:
-        grad, gain_grad, bias_grad = (rest.pop(0) for _ in range(3))
-    keep, send, block, grad_proj, sems, low_t, normed_t, raw_qkv, raw_out = rest
+        grad, gain_grad, bias_grad, types = (rest.pop(0) for _ in range(4))
+    keep = [rest.pop(0) for _ in range(GROUP // 2)]
+    send, block, grad_proj, sems, low_t, normed_t, raw_qkv, raw_out = rest
     k = pl.program_id(0)
     top = incoming.shape[0]
-    inner = mixed.shape[-1]
+    inner = raw_out.shape[0]
     heads = inner // HD
 
     @pl.when(k == 0)
@@ -478,28 +490,38 @@
     def _():
         arrived(k, [block], sems)
 
-    grad_mixed = nn(incoming[...].astype(BF16), block[k, :, 3 * inner :]).astype(BF16)
+    pad = mixed.shape[2] - inner
+    grad_mixed = nn(incoming[...].astype(BF16), block[k, :, 3 * inner - pad :]).astype(BF16)
     lane = lax.broadcasted_iota(jnp.int32, (top, 128), 1)
-    for h in range(heads):
-        own_lanes = slice(h * HD, (h + 1) * HD)
-        key_lanes = slice(inner + h * HD, inner + (h + 1) * HD)
-        value_lanes = slice(2 * inner + h * HD, 2 * inner + (h + 1) * HD)
-        queries = proj[0, :top, own_lanes] * jnp.asarray(HD**-0.5, BF16)
-        keys = proj[0, :, key_lanes]
-        values = proj[0, :, value_lanes]
-        head_grad = grad_mixed[:, own_lanes]
-        at = lane == (quarters[0] + k) * heads + h
-        row_sum = jnp.sum(jnp.where(at, logsum[:top, :], 0.0), axis=-1, keepdims=True)
-        weights = jnp.exp(nt(queries, keys) - row_sum)
-        grad_weights = nt(head_grad, values)
-        inner_sum = jnp.sum(weights * grad_weights, axis=-1, keepdims=True)
-        grad_scores = (weights * (grad_weights - inner_sum)).astype(BF16)
-        grad_proj[:top, own_lanes] = (nn(grad_scores, keys) * HD**-0.5).astype(BF16)
-        grad_proj[:, key_lanes] = tn(grad_scores, queries).astype(BF16)
-        grad_proj[:, value_lanes] = tn(weights.astype(BF16), head_grad).astype(BF16)
-    total[...] += nt(grad_proj[...], block[k, :, : 3 * inner])
-    put_block(nn(normed_t[...], grad_proj[...]), keep, send, 0, slice(0, 3 * inner))
-    put_block(nn(low_t[...], mixed[0, :top, :]), keep, send, 0, slice(3 * inner, 4 * inner))
+    every = range(heads)
+    lanes = [slice(h * HD, (h + 1) * HD) for h in range(3 * heads)]
+    queries = [proj[0, :top, lanes[h]] * jnp.asarray(HD**-0.5, BF16) for h in every]
+    keys = [proj[0, :, lanes[heads + h]] for h in every]
+    head_grads = [grad_mixed[:, pad + h * HD : pad + (h + 1) * HD] for h in every]
+    scores = [nt(queries[h], keys[h]) for h in every]
+    grad_weights = [nt(head_grads[h], proj[0, :, lanes[2 * heads + h]]) for h in every]
+    row_sums = [
+        jnp.sum(
+            jnp.where(lane == (quarters[0] + k) * heads + h, logsum[:top, :], 0.0), axis=-1, keepdims=True
+        )
+        for h in every
+    ]
+    weights = [jnp.exp(scores[h] - row_sums[h]) for h in every]
+    for h in every:
+        grad_proj[:, lanes[2 * heads + h]] = tn(weights[h].astype(BF16), head_grads[h]).astype(BF16)
+    inner_sums = [jnp.sum(weights[h] * grad_weights[h], axis=-1, keepdims=True) for h in every]
+    grad_scores = [(weights[h] * (grad_weights[h] - inner_sums[h])).astype(BF16) for h in every]
+    for h in every:
+        grad_proj[:top, lanes[h]] = (nn(grad_scores[h], keys[h]) * HD**-0.5).astype(BF16)
+        grad_proj[:, lanes[heads + h]] = tn(grad_scores[h], queries[h]).astype(BF16)
+    wide = grad_proj.shape[1]
+    total[...] += nt(grad_proj[...], block[k, :, :wide])
+    left = nn(normed_t[...], grad_proj[...])
+    right = nn(low_t[...], mixed[0, :top, :])
+    at = 3 * inner - pad
+    put_block(left[:, :at], keep, send, 0, slice(0, at))
+    put_block(left[:, at:] + right[:, : wide - at], keep, send, 0, slice(at, wide))
+    put_block(right[:, wide - at :], keep, send, 0, slice(wide, 4 * inner))
 
     if last:
 
@@ -507,13 +529,21 @@
         def _():
             gain_grad[...] = jnp.zeros_like(gain_grad)
             bias_grad[...] = jnp.zeros_like(bias_grad)
-            for r in range(0, x.shape[0], 16):
-                rows = slice(r, r + 16)
+            types[...] = jnp.zeros_like(types)
+            step = 8
+            for r in range(0, x.shape[0], step):
+                rows = slice(r, r + step)
                 back = norm_back_rows(rows, x, gain, total, gain_grad, bias_grad)
-                grad[rows, :] = back + incoming[rows, :] if r < top else back
-
-
-def attention_backward(spot, incoming, x, gain, normed, proj, logsum, mixed, total, layer, own, pieces, quarters):
+                if r < top:
+                    back = back + incoming[rows, :]
+                grad[rows, :] = back.astype(grad.dtype)
+                which = slice(0, 1) if r < WORDS else slice(1, 2)
+                types[which, :] += jnp.sum(back, axis=0, keepdims=True)
+
+
+def attention_backward(
+    spot, incoming, x, gain, normed, proj, logsum, mixed, total, layer, own, pieces, quarters, out_type=F32
+):
     length, width = x.shape
     top = incoming.shape[0]
     n_t = proj.shape[0]
@@ -521,12 +551,13 @@
     count = len(quarters)
     inner = own[1].shape[1]
     if total is None:
-        total = jnp.zeros((8, 128), F32)
+        total = gain
     out = [jax.ShapeDtypeStruct((length, width), F32)]
     out_specs = [whole((length, width))]
     if last:
-        out += [jax.ShapeDtypeStruct(v, F32) for v in ((length, width), (1, width), (1, width))]
-        out_specs += [whole((length, width)), whole((1, width)), whole((1, width))]
+        out.append(jax.ShapeDtypeStruct((length, width), out_type))
+        out += [jax.ShapeDtypeStruct(v, F32) for v in ((1, width), (1, width), (2, width))]
+        out_specs += [whole(v.shape) for v in out[1:]]
     out += block_shapes(count, 1, width // GROUP, 4 * inner)
     out_specs += block_specs(1, width // GROUP, 4 * inner)
     return pl.pallas_call(
@@ -541,14 +572,14 @@
             whole((length, width)),
             per_quarter((length, 3 * inner), quarters[0]),
             whole((length, 128)),
-            per_quarter((length, inner), quarters[0]),
+            per_quarter((length, inner + inner % 128), quarters[0]),
             whole(total.shape),
         ]
         + [any_spec()] * (2 + len(pieces.arrays)),
         out_specs=out_specs,
         scratch_shapes=[
             pltpu.VMEM((count, width, 4 * inner), BF16),
-            pltpu.VMEM((length, 3 * inner), BF16),
+            pltpu.VMEM((length, 3 * inner + (3 * inner) % 128), BF16),
             pltpu.SemaphoreType.DMA((count,)),
             pltpu.VMEM((width, top), BF16),
             pltpu.VMEM((width, length), BF16),
@@ -614,19 +645,54 @@
     return swap(y_piece, 2, n_dp) if by_x else swap(x_piece, 4, n_dp)
 
 
-def sum_kernel(*refs):
-    *operands, out = refs
-    total = operands[0][...].astype(F32)
-    for operand in operands[1:]:
-        total = total + operand[...].astype(F32).reshape(total.shape)
-    out[...] = total.astype(out.dtype).reshape(out.shape)
-
-
-def mine_kernel(*refs):
-    kept, got, first, second, *outs = refs
+def near_kernel(*refs):
+    *operands, x_out, y_out = refs
+    for out, four in ((x_out, operands[:4]), (y_out, operands[4:])):
+        for i in range(2):
+            out[i] = (four[2 * i][...].astype(F32) + four[2 * i + 1][0].astype(F32)).astype(BF16)
+
+
+def far_kernel(*refs):
+    *operands, x_out, y_out = refs
+    for out, (kept, got, near) in ((x_out, operands[:3]), (y_out, operands[3:])):
+        out[...] = (kept[...].astype(F32) + got[0].astype(F32) + near[0].astype(F32)).astype(BF16)
+
+
+def own_kernel(*refs):
+    operands, outs = refs[:8], refs[8:]
+    half = len(outs) // 2
     for i, out in enumerate(outs):
-        total = kept[0, i].astype(F32) + got[0, i].astype(F32) + first[0, i].astype(F32) + second[i].astype(F32)
+        kept, got, near, far = operands[4 * (i // half) : 4 * (i // half) + 4]
+        j = i % half
+        total = kept[j].astype(F32) + got[0, j].astype(F32) + near[0, j].astype(F32) + far[j].astype(F32)
         out[0] = total.astype(out.dtype)
+
+
+def rows_kernel(*refs):
+    *sources, target = refs
+    target[...] = jnp.zeros_like(target)
+    at = 0
+    for source in sources:
+        count = source.shape[0]
+        target[at : at + count, :] = source[...]
+        at += count
+
+
+def stack_rows(sources):
+    width = sources[0].shape[1]
+    count = -(-sum(v.shape[0] for v in sources) // 8) * 8
+    return small_call(
+        rows_kernel,
+        (1,),
+        [whole(v.shape) for v in sources],
+        whole((count, width)),
+        jax.ShapeDtypeStruct((count, width), F32),
+        "stack_rows",
+    )(*sources)
+
+
+def relay_kernel(first, second, out):
+    out[...] = (first[...].astype(F32) + second[...].astype(F32)).astype(BF16)
 
 
 def last_kernel(*refs):
@@ -638,74 +704,93 @@
 
 
 class Reduction:
-    def __init__(self, keep, got, first, quarters, by_x, n_dp, n_t):
-        self.keep, self.got, self.first, self.quarters = keep, got, first, quarters
-        self.near, self.far = (2, 4) if by_x else (4, 2)
+    def __init__(self, blocks, n_dp, n_t):
+        self.keep, self.got = [], []
         self.n_dp, self.n_t = n_dp, n_t
-        self.shape = keep.shape[2:]
-
-    def plane(self, i):
-        count = len(self.quarters)
-        zeros = (0,) * len(self.shape)
-        return pl.BlockSpec((1, count) + self.shape, lambda _: (i, self.first // count) + zeros)
-
-    def near_sum(self, token):
-        self.got = after(self.got, token)
-        zeros = (0,) * len(self.shape)
-        count = len(self.quarters)
-        near = self.near // 2
-        spec = pl.BlockSpec(
-            (1, count) + self.shape, lambda i: (jnp.where(i == 0, near, 3), self.first // count) + zeros
+        self.half = n_t // 2
+        for keep, send in blocks:
+            self.add(keep, send)
+        self.shape = self.keep[0][0].shape[1:]
+        self.zeros = (0,) * len(self.shape)
+
+    def add(self, keep, send):
+        self.keep.append(keep)
+        self.got.append(swap(send, 1, self.n_dp))
+
+    def pair(self, plane, half):
+        n = len(self.keep)
+        at = half // n
+        specs = [
+            pl.BlockSpec((self.half,) + self.shape, lambda _: (at,) + self.zeros),
+            pl.BlockSpec((1, self.half) + self.shape, lambda _: (plane, at) + self.zeros),
+        ]
+        return list(zip([self.keep[half % n][plane], self.got[half % n]], specs))
+
+    def call(self, kernel, operands, shapes, name):
+        return small_call(
+            kernel,
+            (1,),
+            [spec for _, spec in operands],
+            [whole(v.shape) for v in shapes],
+            shapes,
+            name,
+        )(*[v for v, _ in operands])
+
+    def near(self):
+        shape = jax.ShapeDtypeStruct((2, self.half) + self.shape, BF16)
+        x, y = self.call(
+            near_kernel,
+            self.pair(1, 0) + self.pair(3, 0) + self.pair(2, 1) + self.pair(3, 1),
+            [shape, shape],
+            "near_sum",
         )
-        out = small_call(
-            sum_kernel,
-            (2,),
-            [spec, spec],
-            pl.BlockSpec((1, count) + self.shape, lambda i: (i, 0) + zeros),
-            jax.ShapeDtypeStruct((2, count) + self.shape, BF16),
-            "near_sum",
-        )(self.keep, self.got)
-        self.from_near = swap(out, self.near, self.n_dp)
+        self.from_near = [swap(x, 2, self.n_dp), swap(y, 4, self.n_dp)]
+        return [x, y]
+
+    def came(self, half, i):
+        spec = pl.BlockSpec((1, self.half) + self.shape, lambda _: (i, 0) + self.zeros)
+        return [(self.from_near[half], spec)]
+
+    def far(self):
+        shape = jax.ShapeDtypeStruct((self.half,) + self.shape, BF16)
+        x, y = self.call(
+            far_kernel,
+            self.pair(2, 0) + self.came(0, 1) + self.pair(1, 1) + self.came(1, 1),
+            [shape, shape],
+            "far_sum",
+        )
+        self.from_far = [swap(x, 4, self.n_dp), swap(y, 2, self.n_dp)]
+        return [x, y]
+
+    def own(self, all_at_once=False):
+        full = whole((self.half,) + self.shape)
+        outs = self.call(
+            own_kernel,
+            [v for i in range(2) for v in self.pair(0, i) + self.came(i, 0) + [(self.from_far[i], full)]],
+            [jax.ShapeDtypeStruct((1,) + self.shape, BF16 if k else F32) for k in range(self.n_t)],
+            "own_sum",
+        )
+        if all_at_once:
+            self.parts = [self.along(v, -k) if k else v for k, v in enumerate(outs)]
+        else:
+            self.waiting = outs[1]
+            self.passed = self.along(outs[2], -1)
+            self.parts = [outs[0], self.along(outs[3], 1)]
+        return list(outs)
+
+    def along(self, part, step):
+        return lax.ppermute(part, "tensor", [(j, (j + step) % self.n_t) for j in range(self.n_t)])
+
+    def pass_on(self):
+        full = whole(self.waiting.shape)
+        (out,) = self.call(
+            relay_kernel,
+            [(self.waiting, full), (self.passed, full)],
+            [jax.ShapeDtypeStruct(self.waiting.shape, BF16)],
+            "relay_sum",
+        )
+        self.parts.append(self.along(out, -1))
         return out
-
-    def far_sum(self, token):
-        self.from_near = after(self.from_near, token)
-        zeros = (0,) * len(self.shape)
-        count = len(self.quarters)
-        full = (count,) + self.shape
-        out = small_call(
-            sum_kernel,
-            (1,),
-            [
-                self.plane(self.far // 2),
-                self.plane(self.far // 2),
-                pl.BlockSpec((1,) + full, lambda _: (1, 0) + zeros),
-            ],
-            whole(full),
-            jax.ShapeDtypeStruct(full, BF16),
-            "far_sum",
-        )(self.keep, self.got, self.from_near)
-        self.from_far = swap(out, self.far, self.n_dp)
-        return out
-
-    def own_sum(self, token):
-        self.from_far = after(self.from_far, token)
-        zeros = (0,) * len(self.shape)
-        full = (len(self.quarters),) + self.shape
-        one = (1,) + self.shape
-        outs = small_call(
-            mine_kernel,
-            (1,),
-            [self.plane(0), self.plane(0), pl.BlockSpec((1,) + full, lambda _: (0, 0) + zeros), whole(full)],
-            [whole(one)] * len(self.quarters),
-            [jax.ShapeDtypeStruct(one, BF16 if k else F32) for k in self.quarters],
-            "own_sum",
-        )(self.keep, self.got, self.from_near, self.from_far)
-        self.parts = [
-            lax.ppermute(v, "tensor", [(j, (j - k) % self.n_t) for j in range(self.n_t)]) if k else v
-            for k, v in zip(self.quarters, outs)
-        ]
-        return list(outs)
 
 
 def finish(parts, n_dp):
@@ -738,8 +823,8 @@
 class SumAll:
     def __init__(self, values, n_dp, n_t):
         self.values, self.n_dp, self.n_t = values, n_dp, n_t
-        self.bits = [("dp", 1 << i) for i in range(n_dp.bit_length() - 1)]
-        self.bits += [("tensor", 1 << i) for i in range(n_t.bit_length() - 1)]
+        self.bits = [("tensor", 1 << i) for i in range(n_t.bit_length() - 1)]
+        self.bits += [("dp", 1 << i) for i in range(n_dp.bit_length() - 1)]
         self.got = None
 
     def step(self, token):
@@ -843,7 +928,7 @@
     held_a = to_neighbours(part_a)
     held_m = to_neighbours(after(part_m, (held_a[near], held_a[far])))
     hops_a = passed_on(held_a)
-    hops_a[0] = after(hops_a[0], part_m)
+    hops_a[0] = after(hops_a[0], part_m, stream, own_attn)
     (own_a,) = pack(hops_a, 1)
     x_a, y_a = sides_of(own_a)
     held_m[near], held_m[far] = after((held_m[near], held_m[far]), (x_a, y_a))
@@ -879,78 +964,92 @@
 
     place = lax.dynamic_slice_in_dim(positions, quarter, 1, 0)[0]
     cot = lax.dynamic_slice_in_dim(cotangent, quarter, 1, 0)[0]
-    onehot = (row_ids[:TOP_ROWS] == place[None, :]).astype(BF16)
-    incoming = nn(onehot, cot)
+    pick = (lax.broadcasted_iota(jnp.int32, (1, TOP_ROWS), 1) == place[:, None]).astype(BF16)
+    pick = jnp.concatenate([pick, jnp.zeros((SLOT_ROWS - slots, TOP_ROWS), BF16)], 0)
+    slot_cot = jnp.concatenate(
+        [jnp.where(place[:, None] >= 0, cot, 0), jnp.zeros((SLOT_ROWS - slots, width), BF16)], 0
+    )
+    incoming = tn(pick, slot_cot)
 
     everything = tuple(range(n_t))
     halves = (everything[: n_t // 2], everything[n_t // 2 :])
     gain_grads = [[None, None] for _ in range(layers)]
     bias_grads = [[None, None] for _ in range(layers)]
-    def reductions_of(keep, got, quarters):
-        out = []
-        for i, half in enumerate(halves):
-            chosen = [k for k in half if k in quarters]
-            if chosen:
-                out.append(Reduction(keep, got, chosen[0] - quarters[0], chosen, i == 0, n_dp, n_t))
-        return out
-
     stream_l, normed, proj, logsum, mixed, middle = saved[top]
-    grad_middle, gain_grads[top][1], bias_grads[top][1], top_normed = top_backward(
-        spots, incoming, middle, gains[top][1], biases[top][1], top, own_mlp, mlp_pieces[top], n_t
+    grad_middle, gain_grads[top][1], bias_grads[top][1], slot_rows = top_backward(
+        spots, incoming, middle, gains[top][1], biases[top][1], pick, slot_cot, top, own_mlp, mlp_pieces[top], n_t
     )
-    slot_rows = tn(onehot, top_normed).astype(BF16)
-    slot_cot = jnp.where(place[:, None] >= 0, cot, 0)
-    spare = jnp.zeros((SLOT_ROWS - slots, width), BF16)
-    all_rows = lax.all_gather(jnp.concatenate([slot_cot, spare, slot_rows, spare], 0), ("dp", "tensor"))
-    total, incoming, gain_grads[top][0], bias_grads[top][0], keep, send = attention_backward(
+    all_rows = lax.all_gather(slot_rows, ("dp", "tensor"))
+    total, incoming, gain_grads[top][0], bias_grads[top][0], _, *keep, send = attention_backward(
         spots, grad_middle, stream_l, gains[top][0], normed, proj, logsum, mixed, None,
         top, own_attn, attn_pieces[top], everything,
     )
-    got = swap(send, 1, n_dp)
+    top_attn = Reduction([(keep, send)], n_dp, n_t)
+
     (last_stream,) = run_feed_forward(top, after(middle, total), mlp_pieces[top], False, BF16)
-    last_stream, (got,) = gate(last_stream, got)
-    attn_top = reductions_of(keep, got, everything)
-    ready = [r.near_sum(last_stream) for r in attn_top]
-    hidden_held = to_neighbours(after(last_stream, ready))
+    last_stream, (top_attn.got,) = gate(last_stream, top_attn.got)
+    hidden_held = to_neighbours(last_stream)
     hidden_held[0] = last_stream
-
-    stream_l, normed, proj, logsum, mixed, middle, normed_mlp, upward = saved[0]
+    ready = top_attn.near()
+
+    stream_l, normed, proj, logsum, mixed, middle_l, normed_mlp, upward = saved[0]
     outs = mlp_backward(
-        spots, after(incoming, ready), middle, gains[0][1], normed_mlp, upward, None,
+        spots, after(incoming, ready), middle_l, gains[0][1], normed_mlp, upward, None,
         0, own_mlp, mlp_pieces[0], everything, True,
     )
-    near_of = [r.from_near for r in attn_top]
-    outs, (near_of, hidden_held) = gate(outs, near_of, hidden_held)
-    for r, v in zip(attn_top, near_of):
-        r.from_near = v
-    incoming, gain_grads[0][1], bias_grads[0][1], keep, send = outs[1:]
-    got = swap(send, 1, n_dp)
+    outs, (top_attn.from_near, hidden_held) = gate(outs, top_attn.from_near, hidden_held)
+    grad_middle, gain_grads[0][1], bias_grads[0][1], *keep, send = outs[1:]
+    low_mlp = Reduction([(keep, send)], n_dp, n_t)
     hidden_held[1:] = passed_on(hidden_held)
-    ready = [r.far_sum(incoming) for r in attn_top]
+    ready = top_attn.far()
 
     outs = attention_backward(
-        spots, after(incoming, ready), stream_l, gains[0][0], normed, proj, logsum, mixed, None,
+        spots, after(grad_middle, ready), stream_l, gains[0][0], normed, proj, logsum, mixed, None,
         0, own_attn, attn_pieces[0], halves[0],
     )
-    outs, (got, far_of, hidden_held) = gate(outs, got, [r.from_far for r in attn_top], hidden_held)
-    for r, v in zip(attn_top, far_of):
-        r.from_far = v
-    total, keep_a, send_a = outs
-    got_a = swap(send_a, 1, n_dp)
-    mlp_low = reductions_of(keep, got, everything)
-    ready = [r.near_sum(total) for r in mlp_low]
-    ready += [r.own_sum(ready) for r in attn_top]
+    outs, (low_mlp.got, top_attn.from_far, hidden_held) = gate(
+        outs, low_mlp.got, top_attn.from_far, hidden_held
+    )
+    total, *keep, send = outs
+    first_half = (keep, send)
+    ready = low_mlp.near()
+    top_attn.from_far = after(top_attn.from_far, ready)
+    ready = top_attn.own(True)
 
     outs = attention_backward(
-        spots, after(incoming, ready), stream_l, gains[0][0], normed, proj, logsum, mixed, total,
-        0, own_attn, attn_pieces[0], halves[1],
+        spots, after(grad_middle, ready), stream_l, gains[0][0], normed, proj, logsum, mixed, total,
+        0, own_attn, attn_pieces[0], halves[1], BF16,
     )
-    outs, (got_a,) = gate(outs, got_a)
-    incoming, gain_grads[0][0], bias_grads[0][0], keep_b, send_b = outs[1:]
-    (low_a,) = reductions_of(keep_a, got_a, halves[0])
-    (low_b,) = reductions_of(keep_b, swap(send_b, 1, n_dp), halves[1])
-    ready = low_a.near_sum(incoming)
-    grad_tokens = lax.all_gather(incoming.astype(BF16), "tensor", tiled=True)
+    outs, (low_mlp.from_near, top_attn.parts) = gate(outs, low_mlp.from_near, top_attn.parts)
+    incoming, gain_grads[0][0], bias_grads[0][0], type_grad, *keep, send = outs[1:]
+    low_attn = Reduction([after(first_half, send), (keep, send)], n_dp, n_t)
+    grad_tokens = lax.all_gather(incoming, "tensor", tiled=True)
+    ready = low_mlp.far()
+    low_attn.got = after(low_attn.got, ready)
+    ready = low_attn.near()
+
+    rows_all = SumAll(
+        stack_rows(
+            [after(type_grad, ready)]
+            + [g for pair in gain_grads for g in pair]
+            + [g for pair in bias_grads for g in pair]
+        ),
+        n_dp,
+        n_t,
+    )
+
+    def finished(reduction, token):
+        return finish(after(reduction.parts, token), n_dp)
+
+    sums = {}
+    rows_all.step(ready)
+    hidden_out = put_pairs(after(hidden_held, ready))
+    rows_all.step(hidden_out)
+    low_mlp.from_far = after(low_mlp.from_far, hidden_out)
+    ready = low_mlp.own()
+    rows_all.step(ready)
+    low_attn.from_near = after(low_attn.from_near, rows_all.values)
+    ready = low_attn.far()
 
     all_rows = after(all_rows, ready)
     all_cot = all_rows[:, :SLOT_ROWS].reshape(-1, width)
@@ -961,42 +1060,24 @@
     grad_down_top = tn(
         gelu(slot_up).astype(BF16), lax.dynamic_slice_in_dim(all_cot, me * unit, unit, 1)
     )
-
-    ready = low_b.near_sum(ready)
-    type_grad = jnp.stack([jnp.sum(incoming[:WORDS], 0), jnp.sum(incoming[WORDS:], 0)])
-    rows_all = SumAll(
-        jnp.concatenate(
-            [type_grad] + [g for pair in gain_grads for g in pair] + [b for pair in bias_grads for b in pair], 0
-        ),
-        n_dp,
-        n_t,
-    )
+    ready = (grad_up_top, grad_down_top)
+    ready, (low_attn.from_far, low_mlp.passed) = gate(ready, low_attn.from_far, low_mlp.passed)
+    ready = low_mlp.pass_on()
+    low_attn.from_far = after(low_attn.from_far, ready)
+    ready = low_attn.own()
     rows_all.step(ready)
-    hidden_out = put_pairs(after(hidden_held, ready))
-    ready = (hidden_out, grad_up_top, grad_down_top)
-    for r in mlp_low:
-        ready = r.far_sum(ready)
+    (sums["attn", top],) = finished(top_attn, ready)
+    low_attn.passed = after(low_attn.passed, rows_all.got if rows_all.got is not None else ready)
+    ready = low_attn.pass_on()
     rows_all.step(ready)
-    sums = {}
-
-    def finished(reductions, token):
-        return finish(after([p for r in reductions for p in r.parts], token), n_dp)
-
-    (sums["attn", top],) = finished(attn_top, ready)
-    for r in (low_a, low_b):
-        ready = r.far_sum(ready)
-        rows_all.step(ready)
-    for r in (*mlp_low, low_a, low_b):
-        ready = r.own_sum(ready)
-        rows_all.step(ready)
     rows_all = rows_all.result(ready)
-    grad_tokens = after(grad_tokens, ready).astype(F32)
-    sums["down", 0], sums["up", 0] = finished(mlp_low, ready)
-    (sums["attn", 0],) = finished([low_a, low_b], (ready, grad_tokens, sums["down", 0], sums["up", 0]))
+    grad_tokens = after(grad_tokens, rows_all).astype(F32)
+    sums["down", 0], sums["up", 0] = finished(low_mlp, grad_tokens)
+    (sums["attn", 0],) = finished(low_attn, (sums["down", 0], sums["up", 0]))
 
     rows_mine = lax.dynamic_slice_in_dim(rows_all, me * unit, unit, 1)
     grad_gain = rows_mine[2 : 2 + 2 * layers].reshape(layers, 2, unit)
-    grad_bias = rows_mine[2 + 2 * layers :].reshape(layers, 2, unit)
+    grad_bias = rows_mine[2 + 2 * layers : 2 + 4 * layers].reshape(layers, 2, unit)
     grad_qkv = jnp.stack([sums["attn", l][:, : 3 * inner].reshape(unit, 3, inner) for l in range(layers)])
     grad_out = jnp.stack([sums["attn", l][:, 3 * inner :].T for l in range(layers)])
     grad_up = jnp.stack([grad_up_top if l == top else sums["up", l] for l in range(layers)])

time: 393 us -> 350 us (0.89)
  waiting for transfers between devices: 121 us -> 99.3 us
  Pallas kernels: 118 us -> 107 us
  other arithmetic: 18.3 us -> 13.7 us
    ppermute x48, waiting for transfers between devices: 37.3 us -> 60.7 us  [swap(): return lax.ppermute(values, 'dp', [(i, i ^ bit) for i in range(size)])]
    ppermute x5, waiting for transfers between devices: 24.3 us -> 4.96 us  [step(): lax.ppermute(after(self.values, token), axis, [(i, i ^ bit) for i in rang...]
    all_gather x2, waiting for transfers between devices: 14.1 us -> 0.01 us  [the longest x1 0.01 us: shards(): all_rows = lax.all_gather(slot_rows, ('dp', 'tensor'))]
    ppermute x12, waiting for transfers between devices: 38.3 us -> 28.8 us  [hand_on(): lax.ppermute(part, 'tensor', [(i, (i + step) % n_t) for i in range(n_t)])]
    pallas_call x18 -> x12, Pallas kernels: 25.2 us -> 18.7 us  [the longest x11 18.7 us: call(): small_call(kernel, (1,), [spec for _, spec in operands], [whole(v.shape)...]
    pallas_call x3, Pallas kernels: 36.2 us -> 31.9 us  [attention_backward(): pl.pallas_call(functools.partial(attention_backward_kernel, quarters, las...]
    unnamed x159 -> x165, local copies, waits for them, and re-layouts: 24.1 us -> 27.8 us
    dot_general x5 -> x4, matrix products: 10.8 us -> 9.67 us  [dot(): lax.dot_general(left, right, (dims, ((), ())), preferred_element_type=F32)]
  transfers between devices with their start and end apart: 76 -> 76, of which waited for: 30 -> 32; matrix products, arithmetic and copies ran while one was open for 12% -> 11% of each run, Pallas kernels for 23% -> 24%
where the time goes in v3:
time: 350 us; the launch traced here: 348 us
  Pallas kernels  107 us (31%)
  waiting for transfers between devices  99.3 us (28%)
  starting transfers between devices  61 us (17%)
  local copies, waits for them, and re-layouts  42.8 us (12%)
  between operations  15 us (4%)
  other arithmetic  13.7 us (4%)
  matrix products  9.67 us (3%)
    ppermute x48, waiting for transfers between devices, swap(): return lax.ppermute(values, 'dp', [(i, i ^ bit) for i in range(size)])  60.7 us
    pallas_call x3, Pallas kernels, attention_backward(): pl.pallas_call(functools.partial(attention_backward_kernel, quarters, las...  31.9 us
    ppermute x48, starting transfers between devices, swap(): return lax.ppermute(values, 'dp', [(i, i ^ bit) for i in range(size)])  31.2 us
    ppermute x12, waiting for transfers between devices, hand_on(): lax.ppermute(part, 'tensor', [(i, (i + step) % n_t) for i in range(n_t)])  28.8 us
    unnamed x165, local copies, waits for them, and re-layouts  27.8 us
    pallas_call x2, Pallas kernels, attention_forward(): pl.pallas_call(functools.partial(attention_forward_kernel, layer, pieces....  19.2 us
    pallas_call x11, Pallas kernels, call(): small_call(kernel, (1,), [spec for _, spec in operands], [whole(v.shape)...  18.7 us
    ppermute x12, starting transfers between devices, hand_on(): lax.ppermute(part, 'tensor', [(i, (i + step) % n_t) for i in range(n_t)])  18.4 us
  transfers between devices with their start and end apart: 76, of which 32 were waited for; matrix products, arithmetic and copies ran while one was open for 11% of the time, Pallas kernels for 24%

profile of v3, /device:TPU:0, one launch (start us, length us, event | category | flops | bytes accessed | tf_op | source)
XLA Modules:
  0.0 348.0 jit_solution(1664847710673867863)
XLA Ops:
  10.0 3.1 collective-permute-start
  13.1 2.1 collective-permute-start.1
  16.0 2.0 select_add_fusion.x
  18.0 1.8 collective-permute-done.refs_0_
  21.0 2.4 copy.30
  23.5 3.3 collective-permute-done.4.refs_1_
  30.1 3.8 %collective-permute-start.3 = (bf16[192,768]{1,0:T(8,128)(2,1)S(1)}, bf16[192,768]{1,0:T(8,128)(2,1)S(1)}, u32[]{:S(2)}, u32[]{:S(2)}) collective-permute-start(bf16[192,768]{1,0:T(8,128)(2,1)S(1)} %pad_maximum_fusion.4), channel_id=1, source_target_pairs={{0,3},{1,0},{2,1},{3,2},{4,7},{5,4},{6,5},{7,6},{8,11},{9,8},{10,9... | collective-permute-start | bytes 884744 | tf_op jit(solution)/shard_map/ppermute | solution.py:884
  34.0 6.1 %collective-permute-done.2.refs_0_ = bf16[192,768]{1,0:T(8,128)(2,1)S(1)} collective-permute-done((bf16[192,768]{1,0:T(8,128)(2,1)S(1)}, bf16[192,768]{1,0:T(8,128)(2,1)S(1)}, u32[]{:S(2)}, u32[]{:S(2)}) %collective-permute-start.2) | collective-permute-done | bytes 294944 | tf_op jit(solution)/shard_map/ppermute | solution.py:884
  43.7 6.1 %collective-permute-done.11.rest_6_ = bf16[1,3,96,768]{3,2,1,0:T(8,128)(2,1)} collective-permute-done((bf16[1,3,96,768]{3,2,1,0:T(8,128)(2,1)}, bf16[1,3,96,768]{3,2,1,0:T(8,128)(2,1)}, u32[]{:S(2)}, u32[]{:S(2)}) %collective-permute-start.11) | collective-permute-done | bytes 442400 | tf_op jit(solution)/shard_map/ppermute | solution.py:596
  50.6 3.2 collective-permute-done.7.refs_1_
  53.8 3.9 %collective-permute-start.14 = (bf16[288,768]{1,0:T(8,128)(2,1)S(1)}, bf16[288,768]{1,0:T(8,128)(2,1)S(1)}, u32[]{:S(2)}, u32[]{:S(2)}) collective-permute-start(bf16[288,768]{1,0:T(8,128)(2,1)S(1)} %pad_maximum_fusion.3), channel_id=1, source_target_pairs={{0,3},{1,0},{2,1},{3,2},{4,7},{5,4},{6,5},{7,6},{8,11},{9,8},{10,9... | collective-permute-start | bytes 1327112 | tf_op jit(solution)/shard_map/ppermute | solution.py:884
  60.6 9.6 %attention_forward.2 = (f32[256,768]{1,0:T(8,128)}, bf16[256,768]{1,0:T(8,128)(2,1)}, bf16[4,256,576]{2,1,0:T(8,128)(2,1)}, f32[256,128]{1,0:T(8,128)}, bf16[4,256,256]{2,1,0:T(8,128)(2,1)}) custom-call(s32[1]{0:T(128)} %bitcast.spot_ref, f32[256,768]{1,0:T(8,128)} %select_add_fusion.x, f32[1,768]{1,0:T(1,128)} %get-tuple-element.462.gain.total_in, ...), custom_call_target="tpu_custom_call" | custom-call | flops 40000000000 | bytes 1000000 | tf_op jit(solution)/shard_map/attention_forward/pallas_call | solution.py:242
  70.2 4.5 %collective-permute-done.14.refs_2_ = bf16[288,768]{1,0:T(8,128)(2,1)S(1)} collective-permute-done((bf16[288,768]{1,0:T(8,128)(2,1)S(1)}, bf16[288,768]{1,0:T(8,128)(2,1)S(1)}, u32[]{:S(2)}, u32[]{:S(2)}) %collective-permute-start.14) | collective-permute-done | bytes 442400 | tf_op jit(solution)/shard_map/ppermute | solution.py:884
  75.6 2.3 collective-permute-done.17.rest_2_.rest_4_
  83.2 3.8 %collective-permute-done.15.refs_1_ = bf16[288,768]{1,0:T(8,128)(2,1)S(1)} collective-permute-done((bf16[288,768]{1,0:T(8,128)(2,1)S(1)}, bf16[288,768]{1,0:T(8,128)(2,1)S(1)}, u32[]{:S(2)}, u32[]{:S(2)}) %collective-permute-start.15) | collective-permute-done | bytes 442400 | tf_op jit(solution)/shard_map/ppermute | solution.py:884
  87.0 3.0 collective-permute-done.23.rest_8_.rest_10_
  96.7 8.0 %mlp_forward.2 = (f32[256,768]{1,0:T(8,128)}, bf16[256,768]{1,0:T(8,128)(2,1)}, f32[4,256,768]{2,1,0:T(8,128)}) custom-call(s32[1]{0:T(128)} %bitcast.spot_ref, f32[256,768]{1,0:T(8,128)} %get-tuple-element.230.x, f32[1,768]{1,0:T(1,128)} %get-tuple-element.463.gain.total_in, f32[1,768]{1,0:T(1,128)} %get-tuple-element.452.bias, ...), custom_call_target="tpu_custom_call" | custom-call | flops 40000000000 | bytes 1000000 | tf_op jit(solution)/shard_map/mlp_forward/pallas_call | solution.py:303
  109.0 9.4 %collective-permute-done.30.rest_6_ = bf16[1,3,96,768]{3,2,1,0:T(8,128)(2,1)S(1)} collective-permute-done((bf16[1,3,96,768]{3,2,1,0:T(8,128)(2,1)S(1)}, bf16[1,3,96,768]{3,2,1,0:T(8,128)(2,1)S(1)}, u32[]{:S(2)}, u32[]{:S(2)}) %collective-permute-start.30) | collective-permute-done | bytes 442400 | tf_op jit(solution)/shard_map/ppermute | solution.py:596
  120.4 9.6 %attention_forward.3 = (f32[256,768]{1,0:T(8,128)}, bf16[256,768]{1,0:T(8,128)(2,1)}, bf16[4,256,576]{2,1,0:T(8,128)(2,1)}, f32[256,128]{1,0:T(8,128)}, bf16[4,256,256]{2,1,0:T(8,128)(2,1)}) custom-call(s32[1]{0:T(128)} %bitcast.spot_ref, f32[256,768]{1,0:T(8,128)} %get-tuple-element.238.x, f32[1,768]{1,0:T(1,128)} %get-tuple-element.461.gain.total_in, ...), custom_call_target="tpu_custom_call" | custom-call | flops 1000000 | bytes 1000000 | tf_op jit(solution)/shard_map/attention_forward/pallas_call | solution.py:242
  130.0 6.4 %collective-permute-done.32.rest_2_ = bf16[2,3,96,768]{3,2,1,0:T(8,128)(2,1)} collective-permute-done((bf16[2,3,96,768]{3,2,1,0:T(8,128)(2,1)S(1)}, bf16[2,3,96,768]{3,2,1,0:T(8,128)(2,1)}, u32[]{:S(2)}, u32[]{:S(2)}) %collective-permute-start.32) | collective-permute-done | bytes 884768 | tf_op jit(solution)/shard_map/ppermute | solution.py:596
  142.3 7.8 %collective-permute-done.39.rest_8_ = bf16[3,96,768]{2,1,0:T(8,128)(2,1)S(1)} collective-permute-done((bf16[3,96,768]{2,1,0:T(8,128)(2,1)S(1)}, bf16[3,96,768]{2,1,0:T(8,128)(2,1)S(1)}, u32[]{:S(2)}, u32[]{:S(2)}) %collective-permute-start.39) | collective-permute-done | bytes 442400 | tf_op jit(solution)/shard_map/ppermute | solution.py:596
  154.8 7.9 %top_backward.1 = (f32[48,768]{1,0:T(8,128)}, f32[1,768]{1,0:T(1,128)}, f32[1,768]{1,0:T(1,128)}, bf16[32,768]{1,0:T(8,128)(2,1)}) custom-call(s32[1]{0:T(128)} %bitcast.spot_ref, f32[48,768]{1,0:T(8,128)} %fusion.22.incoming, f32[256,768]{1,0:T(8,128)} %get-tuple-element.249.x, f32[1,768]{1,0:T(1,128)} %get-tuple-element.464.gain, ...), custom_call_target="tpu_custom_call" | custom-call | flops 40000000000 | bytes 1000000 | tf_op jit(solution)/shard_map/top_backward/pallas_call | solution.py:436
  162.7 13.5 %attention_backward.3 = (f32[256,768]{1,0:T(8,128)}, f32[256,768]{1,0:T(8,128)}, f32[1,768]{1,0:T(1,128)}, f32[1,768]{1,0:T(1,128)}, f32[2,768]{1,0:T(2,128)}, /...) custom-call(s32[1]{0:T(128)} %bitcast.spot_ref, ...), custom_call_target="tpu_custom_call" | custom-call | flops 40000000000 | bytes 1000000 | tf_op jit(solution)/shard_map/attention_backward/pallas_call | solution.py:563
  176.8 7.4 %mlp_forward.3 = bf16[256,768]{1,0:T(8,128)(2,1)} custom-call(s32[1]{0:T(128)} %bitcast.spot_ref, f32[256,768]{1,0:T(8,128)} %get-tuple-element.249.x, f32[1,768]{1,0:T(1,128)} %get-tuple-element.464.gain, f32[1,768]{1,0:T(1,128)} %get-tuple-element.451.bias, bf16[2,768,768]{2,1,0:T(8,128)(2,1)} %rest_0_.1, bf16[2,768,768]{2,1,0:T(8,128)(2,1)} %rest_1_.1, ...), custom_call_target="tpu_custom_call" | custom-call | flops 40000000000 | bytes 1000000 | tf_op jit(solution)/shard_map/mlp_forward/pallas_call | solution.py:303
  184.2 3.8 %collective-permute-start.45 = (bf16[256,768]{1,0:T(8,128)(2,1)}, bf16[256,768]{1,0:T(8,128)(2,1)}, u32[]{:S(2)}, u32[]{:S(2)}) collective-permute-start(bf16[256,768]{1,0:T(8,128)(2,1)} %mlp_forward.3), channel_id=1, source_target_pairs={{0,3},{1,0},{2,1},{3,2},{4,7},{5,4},{6,5},{7,6},{8,11},{9,8},{10,9... | collective-permute-start | bytes 1179656 | tf_op jit(solution)/shard_map/ppermute | solution.py:884
  192.3 13.1 %mlp_backward.1 = (f32[256,768]{1,0:T(8,128)}, f32[256,768]{1,0:T(8,128)}, f32[1,768]{1,0:T(1,128)}, f32[1,768]{1,0:T(1,128)}, bf16[4,2,96,768]{3,2,1,0:T(8,128)...) custom-call(s32[1]{0:T(128)} %bitcast.spot_ref, ...), custom_call_target="tpu_custom_call" | custom-call | flops 40000000000 | bytes 1000000 | tf_op jit(solution)/shard_map/mlp_backward/pallas_call | solution.py:384
  206.3 2.0 far_sum.3
  210.0 8.4 %attention_backward.4 = (f32[256,768]{1,0:T(8,128)}, bf16[2,1,96,768]{3,2,1,0:T(8,128)(2,1)}, bf16[2,1,96,768]{3,2,1,0:T(8,128)(2,1)}, bf16[2,1,96,768]{3,2,1,0:...) custom-call(s32[1]{0:T(128)} %bitcast.spot_ref, ...), custom_call_target="tpu_custom_call" | custom-call | flops 40000000000 | bytes 1000000 | tf_op jit(solution)/shard_map/attention_backward/pallas_call | solution.py:563
  219.0 5.0 %collective-permute-done.49 = bf16[256,768]{1,0:T(8,128)(2,1)} collective-permute-done((bf16[256,768]{1,0:T(8,128)(2,1)}, bf16[256,768]{1,0:T(8,128)(2,1)}, u32[]{:S(2)}, u32[]{:S(2)}) %collective-permute-start.49) | collective-permute-done | bytes 393248 | tf_op jit(solution)/shard_map/ppermute | solution.py:884
  226.6 3.5 near_sum.4
  232.4 2.0 own_sum.3
  235.1 2.0 collective-permute-start.54
  237.2 10.0 %attention_backward.5 = (f32[256,768]{1,0:T(8,128)}, bf16[256,768]{1,0:T(8,128)(2,1)}, f32[1,768]{1,0:T(1,128)}, f32[1,768]{1,0:T(1,128)}, f32[2,768]{1,0:T(2,12...) custom-call(s32[1]{0:T(128)} %bitcast.spot_ref, ...), custom_call_target="tpu_custom_call" | custom-call | flops 40000000000 | bytes 1000000 | tf_op jit(solution)/shard_map/attention_backward/pallas_call | solution.py:563
  250.2 11.2 %collective-permute-done.50.refs_2_ = bf16[2,2,2,96,768]{4,3,2,1,0:T(8,128)(2,1)} collective-permute-done((bf16[2,2,2,96,768]{4,3,2,1,0:T(8,128)(2,1)}, bf16[2,2,2,96,768]{4,3,2,1,0:T(8,128)(2,1)}, u32[]{:S(2)}, u32[]{:S(2)}) %collective-permute-start.50) | collective-permute-done | bytes 1179680 | tf_op jit(solution)/shard_map/ppermute | solution.py:596
  263.4 2.9 far_sum.4
  279.1 3.7 %collective-permute-done.59.refs_3_ = bf16[2,2,96,768]{3,2,1,0:T(8,128)(2,1)} collective-permute-done((bf16[2,2,96,768]{3,2,1,0:T(8,128)(2,1)}, bf16[2,2,96,768]{3,2,1,0:T(8,128)(2,1)}, u32[]{:S(2)}, u32[]{:S(2)}) %collective-permute-start.59) | collective-permute-done | bytes 589856 | tf_op jit(solution)/shard_map/ppermute | solution.py:596
  284.0 2.9 own_sum.4
  287.4 4.7 %collective-permute-done.58 = f32[16,768]{1,0:T(8,128)S(1)} collective-permute-done((f32[16,768]{1,0:T(8,128)S(1)}, f32[16,768]{1,0:T(8,128)S(1)}, u32[]{:S(2)}, u32[]{:S(2)}) %collective-permute-start.58) | collective-permute-done | bytes 49184 | tf_op jit(solution)/shard_map/ppermute | solution.py:837
  292.7 2.4 collective-permute-done.62.refs_2_
  298.2 2.5 fusion.34
  300.7 1.9 fusion.7
  302.6 4.2 %fusion.6 = f32[96,768]{1,0:T(8,128)} fusion(f32[512,768]{1,0:T(8,128)} %fusion.7, bf16[512,768]{1,0:T(8,128)(2,1)} %bitcast.97, bf16[2,768,768]{2,1,0:T(8,128)(2,1)} %rest_1_.1, bf16[512,768]{1,0:T(8,128)(2,1)} %bitcast.100, s32[]{:T(128)S(6)} %select_n.79), kind=kOutput, calls=%fused_computation.9 | convolution fusion | flops 683409408 | bytes 3964932 | tf_op jit(solution)/shard_map/dot_general | solution.py:27
  306.8 2.7 fusion.14
  310.6 1.9 own_sum.5
  314.6 2.0 collective-permute-start.72
  324.2 2.0 collective-permute-done.68.second
  328.0 2.2 collective-permute-start.71
  331.7 3.4 convert_element_type.34
  (351 shorter events, 101.6 us)
Async XLA Ops:
  7.2 291.0 %all-gather.6.cloned.1.call-start = ((), (), s32[]{:S(2)}) async-start(), calls=%async_computation.1 | async-start | bytes 1622016 | tf_op jit(solution)/shard_map/all_gather | solution.py:982
  26.8 14.4 %collective-permute-start.5 = (bf16[1,3,96,768]{3,2,1,0:T(8,128)(2,1)S(1)}, bf16[1,3,96,768]{3,2,1,0:T(8,128)(2,1)}, u32[]{:S(2)}, u32[]{:S(2)}) collective-permute-start(bf16[1,3,96,768]{3,2,1,0:T(8,128)(2,1)S(1)} %pack.3.rest_0_), channel_id=1, source_target_pairs={{0,8},{4,12},{8,0},{12,4},{16,24},{20,28},{24,16},{28,20},{1,9},{5... | collective-permute-start | bytes 1327112 | tf_op jit(solution)/shard_map/ppermute | solution.py:596
  28.6 12.6 %collective-permute-start.6 = (bf16[1,3,96,768]{3,2,1,0:T(8,128)(2,1)S(1)}, bf16[1,3,96,768]{3,2,1,0:T(8,128)(2,1)}, u32[]{:S(2)}, u32[]{:S(2)}) collective-permute-start(bf16[1,3,96,768]{3,2,1,0:T(8,128)(2,1)S(1)} %pack.3.rest_0_), channel_id=1, source_target_pairs={{0,16},{4,20},{8,24},{12,28},{16,0},{20,4},{24,8},{28,12},{1,17},{... | collective-permute-start | bytes 1327112 | tf_op jit(solution)/shard_map/ppermute | solution.py:596
  30.1 11.1 %collective-permute-start.3 = (bf16[192,768]{1,0:T(8,128)(2,1)S(1)}, bf16[192,768]{1,0:T(8,128)(2,1)S(1)}, u32[]{:S(2)}, u32[]{:S(2)}) collective-permute-start(bf16[192,768]{1,0:T(8,128)(2,1)S(1)} %pad_maximum_fusion.4), channel_id=1, source_target_pairs={{0,3},{1,0},{2,1},{3,2},{4,7},{5,4},{6,5},{7,6},{8,11},{9,8},{10,9... | collective-permute-start | bytes 884744 | tf_op jit(solution)/shard_map/ppermute | solution.py:884
  42.4 11.5 %collective-permute-start.8 = (bf16[1,3,96,768]{3,2,1,0:T(8,128)(2,1)S(1)}, bf16[1,3,96,768]{3,2,1,0:T(8,128)(2,1)}, u32[]{:S(2)}, u32[]{:S(2)}) collective-permute-start(bf16[1,3,96,768]{3,2,1,0:T(8,128)(2,1)S(1)} %pack.3.rest_0_), channel_id=1, source_target_pairs={{0,4},{4,0},{8,12},{12,8},{16,20},{20,16},{24,28},{28,24},{1,5},{5... | collective-permute-start | bytes 1327112 | tf_op jit(solution)/shard_map/ppermute | solution.py:596
  42.5 16.1 %collective-permute-start.9 = (bf16[1,3,96,768]{3,2,1,0:T(8,128)(2,1)}, bf16[1,3,96,768]{3,2,1,0:T(8,128)(2,1)S(1)}, u32[]{:S(2)}, u32[]{:S(2)}) collective-permute-start(bf16[1,3,96,768]{3,2,1,0:T(8,128)(2,1)} %collective-permute-done.5.rest_2_), channel_id=1, source_target_pairs={{0,4},{4,0},{8,12},{12,8},{16,20},{20,16},{24,28},{28,24},{1,5},{5... | collective-permute-start | bytes 1327112 | tf_op jit(solution)/shard_map/ppermute | solution.py:596
  43.7 14.0 %collective-permute-start.10 = (bf16[1,3,96,768]{3,2,1,0:T(8,128)(2,1)}, bf16[1,3,96,768]{3,2,1,0:T(8,128)(2,1)S(1)}, u32[]{:S(2)}, u32[]{:S(2)}) collective-permute-start(bf16[1,3,96,768]{3,2,1,0:T(8,128)(2,1)} %collective-permute-done.6.rest_4_), channel_id=1, source_target_pairs={{0,4},{4,0},{8,12},{12,8},{16,20},{20,16},{24,28},{28,24},{1,5},{5... | collective-permute-start | bytes 1327112 | tf_op jit(solution)/shard_map/ppermute | solution.py:596
  53.7 16.4 %collective-permute-start.13 = (bf16[288,768]{1,0:T(8,128)(2,1)S(1)}, bf16[288,768]{1,0:T(8,128)(2,1)S(1)}, u32[]{:S(2)}, u32[]{:S(2)}) collective-permute-start(bf16[288,768]{1,0:T(8,128)(2,1)S(1)} %pad_maximum_fusion.3), channel_id=1, source_target_pairs={{0,1},{1,2},{2,3},{3,0},{4,5},{5,6},{6,7},{7,4},{8,9},{9,10},{10,1... | collective-permute-start | bytes 1327112 | tf_op jit(solution)/shard_map/ppermute | solution.py:884
  53.8 20.8 %collective-permute-start.14 = (bf16[288,768]{1,0:T(8,128)(2,1)S(1)}, bf16[288,768]{1,0:T(8,128)(2,1)S(1)}, u32[]{:S(2)}, u32[]{:S(2)}) collective-permute-start(bf16[288,768]{1,0:T(8,128)(2,1)S(1)} %pad_maximum_fusion.3), channel_id=1, source_target_pairs={{0,3},{1,0},{2,1},{3,2},{4,7},{5,4},{6,5},{7,6},{8,11},{9,8},{10,9... | collective-permute-start | bytes 1327112 | tf_op jit(solution)/shard_map/ppermute | solution.py:884
  57.7 20.2 %collective-permute-start.17 = (bf16[2,3,96,768]{3,2,1,0:T(8,128)(2,1)S(1)}, bf16[2,3,96,768]{3,2,1,0:T(8,128)(2,1)S(1)}, u32[]{:S(2)}, u32[]{:S(2)}) collective-permute-start(bf16[2,3,96,768]{3,2,1,0:T(8,128)(2,1)S(1)} %pack.4.rest_0_.rest_2_), channel_id=1, source_target_pairs={{0,8},{4,12},{8,0},{12,4},{16,24},{20,28},{24,16},{28,20},{1,9},{5... | collective-permute-start | bytes 2654216 | tf_op jit(solution)/shard_map/ppermute | solution.py:596
  58.5 20.3 %collective-permute-start.18 = (bf16[2,3,96,768]{3,2,1,0:T(8,128)(2,1)S(1)}, bf16[2,3,96,768]{3,2,1,0:T(8,128)(2,1)}, u32[]{:S(2)}, u32[]{:S(2)}) collective-permute-start(bf16[2,3,96,768]{3,2,1,0:T(8,128)(2,1)S(1)} %pack.4.rest_0_.rest_2_), channel_id=1, source_target_pairs={{0,16},{4,20},{8,24},{12,28},{16,0},{20,4},{24,8},{28,12},{1,17},{... | collective-permute-start | bytes 2654216 | tf_op jit(solution)/shard_map/ppermute | solution.py:596
  59.8 32.6 %collective-permute-start.16 = (bf16[2,3,96,768]{3,2,1,0:T(8,128)(2,1)S(1)}, bf16[2,3,96,768]{3,2,1,0:T(8,128)(2,1)}, u32[]{:S(2)}, u32[]{:S(2)}) collective-permute-start(bf16[2,3,96,768]{3,2,1,0:T(8,128)(2,1)S(1)} %pack.4.rest_0_.rest_2_), channel_id=1, source_target_pairs={{0,4},{4,0},{8,12},{12,8},{16,20},{20,16},{24,28},{28,24},{1,5},{5... | collective-permute-start | bytes 2654216 | tf_op jit(solution)/shard_map/ppermute | solution.py:596
  74.7 12.3 %collective-permute-start.15 = (bf16[288,768]{1,0:T(8,128)(2,1)S(1)}, bf16[288,768]{1,0:T(8,128)(2,1)S(1)}, u32[]{:S(2)}, u32[]{:S(2)}) collective-permute-start(bf16[288,768]{1,0:T(8,128)(2,1)S(1)} %collective-permute-done.13.refs_0_), channel_id=1, source_target_pairs={{0,1},{1,2},{2,3},{3,0},{4,5},{5,6},{6,7},{7,4},{8,9},{9,10},{10,1... | collective-permute-start | bytes 1327112 | tf_op jit(solution)/shard_map/ppermute | solution.py:884
  83.2 11.5 %collective-permute-start.19 = (bf16[2,3,96,768]{3,2,1,0:T(8,128)(2,1)S(1)}, bf16[2,3,96,768]{3,2,1,0:T(8,128)(2,1)S(1)}, u32[]{:S(2)}, u32[]{:S(2)}) collective-permute-start(bf16[2,3,96,768]{3,2,1,0:T(8,128)(2,1)S(1)} %copy-done.63), channel_id=1, source_target_pairs={{0,4},{4,0},{8,12},{12,8},{16,20},{20,16},{24,28},{28,24},{1,5},{5... | collective-permute-start | bytes 2654216 | tf_op jit(solution)/shard_map/ppermute | solution.py:596
  92.4 12.3 %collective-permute-start.25 = (bf16[1,3,96,768]{3,2,1,0:T(8,128)(2,1)S(1)}, bf16[1,3,96,768]{3,2,1,0:T(8,128)(2,1)S(1)}, u32[]{:S(2)}, u32[]{:S(2)}) collective-permute-start(bf16[1,3,96,768]{3,2,1,0:T(8,128)(2,1)S(1)} %get-tuple-element.229.rest_0_), channel_id=1, source_target_pairs={{0,8},{4,12},{8,0},{12,4},{16,24},{20,28},{24,16},{28,20},{1,9},{5... | collective-permute-start | bytes 1327112 | tf_op jit(solution)/shard_map/ppermute | solution.py:596
  93.6 11.7 %collective-permute-start.26 = (bf16[1,3,96,768]{3,2,1,0:T(8,128)(2,1)S(1)}, bf16[1,3,96,768]{3,2,1,0:T(8,128)(2,1)S(1)}, u32[]{:S(2)}, u32[]{:S(2)}) collective-permute-start(bf16[1,3,96,768]{3,2,1,0:T(8,128)(2,1)S(1)} %get-tuple-element.229.rest_0_), channel_id=1, source_target_pairs={{0,16},{4,20},{8,24},{12,28},{16,0},{20,4},{24,8},{28,12},{1,17},{... | collective-permute-start | bytes 1327112 | tf_op jit(solution)/shard_map/ppermute | solution.py:596
  94.7 13.8 %collective-permute-start.27 = (bf16[1,3,96,768]{3,2,1,0:T(8,128)(2,1)S(1)}, bf16[1,3,96,768]{3,2,1,0:T(8,128)(2,1)S(1)}, u32[]{:S(2)}, u32[]{:S(2)}) collective-permute-start(bf16[1,3,96,768]{3,2,1,0:T(8,128)(2,1)S(1)} %get-tuple-element.229.rest_0_), channel_id=1, source_target_pairs={{0,4},{4,0},{8,12},{12,8},{16,20},{20,16},{24,28},{28,24},{1,5},{5... | collective-permute-start | bytes 1327112 | tf_op jit(solution)/shard_map/ppermute | solution.py:596
  105.4 13.1 %collective-permute-start.30 = (bf16[1,3,96,768]{3,2,1,0:T(8,128)(2,1)S(1)}, bf16[1,3,96,768]{3,2,1,0:T(8,128)(2,1)S(1)}, u32[]{:S(2)}, u32[]{:S(2)}) collective-permute-start(bf16[1,3,96,768]{3,2,1,0:T(8,128)(2,1)S(1)} %collective-permute-done.26.rest_4_), channel_id=1, source_target_pairs={{0,8},{4,12},{8,0},{12,4},{16,24},{20,28},{24,16},{28,20},{1,9},{5... | collective-permute-start | bytes 1327112 | tf_op jit(solution)/shard_map/ppermute | solution.py:596
  106.2 30.2 %collective-permute-start.32 = (bf16[2,3,96,768]{3,2,1,0:T(8,128)(2,1)S(1)}, bf16[2,3,96,768]{3,2,1,0:T(8,128)(2,1)}, u32[]{:S(2)}, u32[]{:S(2)}) collective-permute-start(bf16[2,3,96,768]{3,2,1,0:T(8,128)(2,1)S(1)} %get-tuple-element.246.rest_0_), channel_id=1, source_target_pairs={{0,8},{4,12},{8,0},{12,4},{16,24},{20,28},{24,16},{28,20},{1,9},{5... | collective-permute-start | bytes 2654216 | tf_op jit(solution)/shard_map/ppermute | solution.py:596
  107.4 29.0 %collective-permute-start.33 = (bf16[2,3,96,768]{3,2,1,0:T(8,128)(2,1)S(1)}, bf16[2,3,96,768]{3,2,1,0:T(8,128)(2,1)}, u32[]{:S(2)}, u32[]{:S(2)}) collective-permute-start(bf16[2,3,96,768]{3,2,1,0:T(8,128)(2,1)S(1)} %get-tuple-element.246.rest_0_), channel_id=1, source_target_pairs={{0,16},{4,20},{8,24},{12,28},{16,0},{20,4},{24,8},{28,12},{1,17},{... | collective-permute-start | bytes 2654216 | tf_op jit(solution)/shard_map/ppermute | solution.py:596
  118.4 35.1 %collective-permute-start.34 = (bf16[2,3,96,768]{3,2,1,0:T(8,128)(2,1)S(1)}, bf16[2,3,96,768]{3,2,1,0:T(8,128)(2,1)}, u32[]{:S(2)}, u32[]{:S(2)}) collective-permute-start(bf16[2,3,96,768]{3,2,1,0:T(8,128)(2,1)S(1)} %get-tuple-element.246.rest_0_), channel_id=1, source_target_pairs={{0,4},{4,0},{8,12},{12,8},{16,20},{20,16},{24,28},{28,24},{1,5},{5... | collective-permute-start | bytes 2654216 | tf_op jit(solution)/shard_map/ppermute | solution.py:596
  136.4 17.3 %collective-permute-start.35 = (bf16[2,3,96,768]{3,2,1,0:T(8,128)(2,1)}, bf16[2,3,96,768]{3,2,1,0:T(8,128)(2,1)S(1)}, u32[]{:S(2)}, u32[]{:S(2)}) collective-permute-start(bf16[2,3,96,768]{3,2,1,0:T(8,128)(2,1)} %collective-permute-done.32.rest_2_), channel_id=1, source_target_pairs={{0,4},{4,0},{8,12},{12,8},{16,20},{20,16},{24,28},{28,24},{1,5},{5... | collective-permute-start | bytes 2654216 | tf_op jit(solution)/shard_map/ppermute | solution.py:596
  136.4 17.3 %collective-permute-start.36 = (bf16[2,3,96,768]{3,2,1,0:T(8,128)(2,1)}, bf16[2,3,96,768]{3,2,1,0:T(8,128)(2,1)}, u32[]{:S(2)}, u32[]{:S(2)}) collective-permute-start(bf16[2,3,96,768]{3,2,1,0:T(8,128)(2,1)} %collective-permute-done.33.rest_4_), channel_id=1, source_target_pairs={{0,4},{4,0},{8,12},{12,8},{16,20},{20,16},{24,28},{28,24},{1,5},{5... | collective-permute-start | bytes 2654216 | tf_op jit(solution)/shard_map/ppermute | solution.py:596
  138.0 12.1 %collective-permute-start.39 = (bf16[3,96,768]{2,1,0:T(8,128)(2,1)S(1)}, bf16[3,96,768]{2,1,0:T(8,128)(2,1)S(1)}, u32[]{:S(2)}, u32[]{:S(2)}) collective-permute-start(bf16[3,96,768]{2,1,0:T(8,128)(2,1)S(1)} %slice_bitcast_fusion), channel_id=1, source_target_pairs={{0,8},{4,12},{8,0},{12,4},{16,24},{20,28},{24,16},{28,20},{1,9},{5... | collective-permute-start | bytes 1327112 | tf_op jit(solution)/shard_map/ppermute | solution.py:596
  140.0 11.9 %collective-permute-start.37 = (bf16[3,96,768]{2,1,0:T(8,128)(2,1)S(1)}, bf16[3,96,768]{2,1,0:T(8,128)(2,1)S(1)}, u32[]{:S(2)}, u32[]{:S(2)}) collective-permute-start(bf16[3,96,768]{2,1,0:T(8,128)(2,1)S(1)} %slice_bitcast_fusion.1), channel_id=1, source_target_pairs={{0,16},{4,20},{8,24},{12,28},{16,0},{20,4},{24,8},{28,12},{1,17},{... | collective-permute-start | bytes 1327112 | tf_op jit(solution)/shard_map/ppermute | solution.py:596
  184.1 21.2 %collective-permute-start.44 = (bf16[256,768]{1,0:T(8,128)(2,1)}, bf16[256,768]{1,0:T(8,128)(2,1)}, u32[]{:S(2)}, u32[]{:S(2)}) collective-permute-start(bf16[256,768]{1,0:T(8,128)(2,1)} %mlp_forward.3), channel_id=1, source_target_pairs={{0,1},{1,2},{2,3},{3,0},{4,5},{5,6},{6,7},{7,4},{8,9},{9,10},{10,1... | collective-permute-start | bytes 1179656 | tf_op jit(solution)/shard_map/ppermute | solution.py:884
  184.2 21.2 %collective-permute-start.45 = (bf16[256,768]{1,0:T(8,128)(2,1)}, bf16[256,768]{1,0:T(8,128)(2,1)}, u32[]{:S(2)}, u32[]{:S(2)}) collective-permute-start(bf16[256,768]{1,0:T(8,128)(2,1)} %mlp_forward.3), channel_id=1, source_target_pairs={{0,3},{1,0},{2,1},{3,2},{4,7},{5,4},{6,5},{7,6},{8,11},{9,8},{10,9... | collective-permute-start | bytes 1179656 | tf_op jit(solution)/shard_map/ppermute | solution.py:884
  190.3 15.1 %collective-permute-start.42 = (bf16[2,2,1,96,768]{4,3,2,1,0:T(8,128)(2,1)}, bf16[2,2,1,96,768]{4,3,2,1,0:T(8,128)(2,1)}, u32[]{:S(2)}, u32[]{:S(2)}) collective-permute-start(bf16[2,2,1,96,768]{4,3,2,1,0:T(8,128)(2,1)} %get-tuple-element.265), channel_id=1, source_target_pairs={{0,8},{4,12},{8,0},{12,4},{16,24},{20,28},{24,16},{28,20},{1,9},{5... | collective-permute-start | bytes 1769480 | tf_op jit(solution)/shard_map/ppermute | solution.py:596
  191.4 14.9 %collective-permute-start.43 = (bf16[2,2,1,96,768]{4,3,2,1,0:T(8,128)(2,1)}, bf16[2,2,1,96,768]{4,3,2,1,0:T(8,128)(2,1)}, u32[]{:S(2)}, u32[]{:S(2)}) collective-permute-start(bf16[2,2,1,96,768]{4,3,2,1,0:T(8,128)(2,1)} %get-tuple-element.266), channel_id=1, source_target_pairs={{0,16},{4,20},{8,24},{12,28},{16,0},{20,4},{24,8},{28,12},{1,17},{... | collective-permute-start | bytes 1769480 | tf_op jit(solution)/shard_map/ppermute | solution.py:596
  206.2 17.8 %collective-permute-start.46 = (bf16[4,4,2,96,768]{4,3,2,1,0:T(8,128)(2,1)}, bf16[4,4,2,96,768]{4,3,2,1,0:T(8,128)(2,1)}, u32[]{:S(2)}, u32[]{:S(2)}) collective-permute-start(bf16[4,4,2,96,768]{4,3,2,1,0:T(8,128)(2,1)} %get-tuple-element.295), channel_id=1, source_target_pairs={{0,4},{4,0},{8,12},{12,8},{16,20},{20,16},{24,28},{28,24},{1,5},{5... | collective-permute-start | bytes 14155784 | tf_op jit(solution)/shard_map/ppermute | solution.py:596
  206.2 125.5 %all-gather.4.cloned.1.call-start = ((), (), s32[]{:S(2)}) async-start(), calls=%async_computation | async-start | bytes 1966080 | tf_op jit(solution)/shard_map/all_gather | solution.py:1026
  210.0 14.0 %collective-permute-start.49 = (bf16[256,768]{1,0:T(8,128)(2,1)}, bf16[256,768]{1,0:T(8,128)(2,1)}, u32[]{:S(2)}, u32[]{:S(2)}) collective-permute-start(bf16[256,768]{1,0:T(8,128)(2,1)} %collective-permute-done.44), channel_id=1, source_target_pairs={{0,1},{1,2},{2,3},{3,0},{4,5},{5,6},{6,7},{7,4},{8,9},{9,10},{10,1... | collective-permute-start | bytes 1179656 | tf_op jit(solution)/shard_map/ppermute | solution.py:884
  230.0 31.4 %collective-permute-start.50 = (bf16[2,2,2,96,768]{4,3,2,1,0:T(8,128)(2,1)}, bf16[2,2,2,96,768]{4,3,2,1,0:T(8,128)(2,1)}, u32[]{:S(2)}, u32[]{:S(2)}) collective-permute-start(bf16[2,2,2,96,768]{4,3,2,1,0:T(8,128)(2,1)} %get-tuple-element.315), channel_id=1, source_target_pairs={{0,8},{4,12},{8,0},{12,4},{16,24},{20,28},{24,16},{28,20},{1,9},{5... | collective-permute-start | bytes 3538952 | tf_op jit(solution)/shard_map/ppermute | solution.py:596
  231.2 30.4 %collective-permute-start.51 = (bf16[2,2,2,96,768]{4,3,2,1,0:T(8,128)(2,1)}, bf16[2,2,2,96,768]{4,3,2,1,0:T(8,128)(2,1)}, u32[]{:S(2)}, u32[]{:S(2)}) collective-permute-start(bf16[2,2,2,96,768]{4,3,2,1,0:T(8,128)(2,1)} %get-tuple-element.316), channel_id=1, source_target_pairs={{0,16},{4,20},{8,24},{12,28},{16,0},{20,4},{24,8},{28,12},{1,17},{... | collective-permute-start | bytes 3538952 | tf_op jit(solution)/shard_map/ppermute | solution.py:596
  235.1 12.0 %collective-permute-start.52 = (bf16[1,1,96,768]{3,2,1,0:T(8,128)(2,1)}, bf16[1,1,96,768]{3,2,1,0:T(8,128)(2,1)S(1)}, u32[]{:S(2)}, u32[]{:S(2)}) collective-permute-start(bf16[1,1,96,768]{3,2,1,0:T(8,128)(2,1)} %get-tuple-element.320), channel_id=1, source_target_pairs={{0,3},{1,0},{2,1},{3,2},{4,7},{5,4},{6,5},{7,6},{8,11},{9,8},{10,9... | collective-permute-start | bytes 442376 | tf_op jit(solution)/shard_map/ppermute | solution.py:782
  235.1 13.8 %collective-permute-start.53 = (bf16[1,1,96,768]{3,2,1,0:T(8,128)(2,1)}, bf16[1,1,96,768]{3,2,1,0:T(8,128)(2,1)S(1)}, u32[]{:S(2)}, u32[]{:S(2)}) collective-permute-start(bf16[1,1,96,768]{3,2,1,0:T(8,128)(2,1)} %get-tuple-element.321), channel_id=1, source_target_pairs={{0,2},{1,3},{2,0},{3,1},{4,6},{5,7},{6,4},{7,5},{8,10},{9,11},{10,... | collective-permute-start | bytes 442376 | tf_op jit(solution)/shard_map/ppermute | solution.py:782
  235.1 14.5 %collective-permute-start.54 = (bf16[1,1,96,768]{3,2,1,0:T(8,128)(2,1)}, bf16[1,1,96,768]{3,2,1,0:T(8,128)(2,1)S(1)}, u32[]{:S(2)}, u32[]{:S(2)}) collective-permute-start(bf16[1,1,96,768]{3,2,1,0:T(8,128)(2,1)} %get-tuple-element.322), channel_id=1, source_target_pairs={{0,1},{1,2},{2,3},{3,0},{4,5},{5,6},{6,7},{7,4},{8,9},{9,10},{10,1... | collective-permute-start | bytes 442376 | tf_op jit(solution)/shard_map/ppermute | solution.py:782
  266.3 16.5 %collective-permute-start.59 = (bf16[2,2,96,768]{3,2,1,0:T(8,128)(2,1)}, bf16[2,2,96,768]{3,2,1,0:T(8,128)(2,1)}, u32[]{:S(2)}, u32[]{:S(2)}) collective-permute-start(bf16[2,2,96,768]{3,2,1,0:T(8,128)(2,1)} %get-tuple-element.339), channel_id=1, source_target_pairs={{0,16},{4,20},{8,24},{12,28},{16,0},{20,4},{24,8},{28,12},{1,17},{... | collective-permute-start | bytes 1769480 | tf_op jit(solution)/shard_map/ppermute | solution.py:596
  267.3 16.6 %collective-permute-start.60 = (bf16[2,2,96,768]{3,2,1,0:T(8,128)(2,1)}, bf16[2,2,96,768]{3,2,1,0:T(8,128)(2,1)}, u32[]{:S(2)}, u32[]{:S(2)}) collective-permute-start(bf16[2,2,96,768]{3,2,1,0:T(8,128)(2,1)} %get-tuple-element.340), channel_id=1, source_target_pairs={{0,8},{4,12},{8,0},{12,4},{16,24},{20,28},{24,16},{28,20},{1,9},{5... | collective-permute-start | bytes 1769480 | tf_op jit(solution)/shard_map/ppermute | solution.py:596
  272.5 22.6 %collective-permute-start.62 = (bf16[2,2,1,96,768]{4,3,2,1,0:T(8,128)(2,1)S(1)}, bf16[2,2,1,96,768]{4,3,2,1,0:T(8,128)(2,1)S(1)}, u32[]{:S(2)}, u32[]{:S(2)}) collective-permute-start(bf16[2,2,1,96,768]{4,3,2,1,0:T(8,128)(2,1)S(1)} %get-tuple-element.346), channel_id=1, source_target_pairs={{0,8},{4,12},{8,0},{12,4},{16,24},{20,28},{24,16},{28,20},{1,9},{5... | collective-permute-start | bytes 1769480 | tf_op jit(solution)/shard_map/ppermute | solution.py:596
  273.6 21.5 %collective-permute-start.63 = (bf16[2,2,1,96,768]{4,3,2,1,0:T(8,128)(2,1)S(1)}, bf16[2,2,1,96,768]{4,3,2,1,0:T(8,128)(2,1)S(1)}, u32[]{:S(2)}, u32[]{:S(2)}) collective-permute-start(bf16[2,2,1,96,768]{4,3,2,1,0:T(8,128)(2,1)S(1)} %get-tuple-element.347), channel_id=1, source_target_pairs={{0,16},{4,20},{8,24},{12,28},{16,0},{20,4},{24,8},{28,12},{1,17},{... | collective-permute-start | bytes 1769480 | tf_op jit(solution)/shard_map/ppermute | solution.py:596
  286.9 22.6 %collective-permute-start.66 = (bf16[1,2,96,768]{3,2,1,0:T(8,128)(2,1)}, bf16[1,2,96,768]{3,2,1,0:T(8,128)(2,1)}, u32[]{:S(2)}, u32[]{:S(2)}) collective-permute-start(bf16[1,2,96,768]{3,2,1,0:T(8,128)(2,1)} %get-tuple-element.371), channel_id=1, source_target_pairs={{0,3},{1,0},{2,1},{3,2},{4,7},{5,4},{6,5},{7,6},{8,11},{9,8},{10,9... | collective-permute-start | bytes 884744 | tf_op jit(solution)/shard_map/ppermute | solution.py:782
  296.1 13.4 %collective-permute-start.64 = (bf16[2,1,96,768]{3,2,1,0:T(8,128)(2,1)}, bf16[2,1,96,768]{3,2,1,0:T(8,128)(2,1)}, u32[]{:S(2)}, u32[]{:S(2)}) collective-permute-start(bf16[2,1,96,768]{3,2,1,0:T(8,128)(2,1)} %get-tuple-element.381), channel_id=1, source_target_pairs={{0,16},{4,20},{8,24},{12,28},{16,0},{20,4},{24,8},{28,12},{1,17},{... | collective-permute-start | bytes 884744 | tf_op jit(solution)/shard_map/ppermute | solution.py:596
  297.1 12.4 %collective-permute-start.65 = (bf16[2,1,96,768]{3,2,1,0:T(8,128)(2,1)}, bf16[2,1,96,768]{3,2,1,0:T(8,128)(2,1)}, u32[]{:S(2)}, u32[]{:S(2)}) collective-permute-start(bf16[2,1,96,768]{3,2,1,0:T(8,128)(2,1)} %get-tuple-element.382), channel_id=1, source_target_pairs={{0,8},{4,12},{8,0},{12,4},{16,24},{20,28},{24,16},{28,20},{1,9},{5... | collective-permute-start | bytes 884744 | tf_op jit(solution)/shard_map/ppermute | solution.py:596
  314.6 11.6 %collective-permute-start.68 = (bf16[1,1,96,768]{3,2,1,0:T(8,128)(2,1)}, bf16[1,1,96,768]{3,2,1,0:T(8,128)(2,1)S(1)}, u32[]{:S(2)}, u32[]{:S(2)}) collective-permute-start(bf16[1,1,96,768]{3,2,1,0:T(8,128)(2,1)} %get-tuple-element.392), channel_id=1, source_target_pairs={{0,3},{1,0},{2,1},{3,2},{4,7},{5,4},{6,5},{7,6},{8,11},{9,8},{10,9... | collective-permute-start | bytes 442376 | tf_op jit(solution)/shard_map/ppermute | solution.py:782
  314.6 20.5 %collective-permute-start.72 = (bf16[1,2,96,768]{3,2,1,0:T(8,128)(2,1)}, bf16[1,2,96,768]{3,2,1,0:T(8,128)(2,1)S(1)}, u32[]{:S(2)}, u32[]{:S(2)}) collective-permute-start(bf16[1,2,96,768]{3,2,1,0:T(8,128)(2,1)} %copy-done.27), channel_id=1, source_target_pairs={{0,1},{1,2},{2,3},{3,0},{4,5},{5,6},{6,7},{7,4},{8,9},{9,10},{10,1... | collective-permute-start | bytes 884744 | tf_op jit(solution)/shard_map/ppermute | solution.py:782
  316.6 19.0 %collective-permute-start.73 = (bf16[1,2,96,768]{3,2,1,0:T(8,128)(2,1)}, bf16[1,2,96,768]{3,2,1,0:T(8,128)(2,1)S(1)}, u32[]{:S(2)}, u32[]{:S(2)}) collective-permute-start(bf16[1,2,96,768]{3,2,1,0:T(8,128)(2,1)} %copy-done.30), channel_id=1, source_target_pairs={{0,3},{1,0},{2,1},{3,2},{4,7},{5,4},{6,5},{7,6},{8,11},{9,8},{10,9... | collective-permute-start | bytes 884744 | tf_op jit(solution)/shard_map/ppermute | solution.py:782
  318.4 19.3 %collective-permute-start.70 = (bf16[1,1,96,768]{3,2,1,0:T(8,128)(2,1)}, bf16[1,1,96,768]{3,2,1,0:T(8,128)(2,1)S(1)}, u32[]{:S(2)}, u32[]{:S(2)}) collective-permute-start(bf16[1,1,96,768]{3,2,1,0:T(8,128)(2,1)} %copy-done.39), channel_id=1, source_target_pairs={{0,1},{1,2},{2,3},{3,0},{4,5},{5,6},{6,7},{7,4},{8,9},{9,10},{10,1... | collective-permute-start | bytes 442376 | tf_op jit(solution)/shard_map/ppermute | solution.py:782
  (109 other events, 749.2 us)
Sparse Core Ops, SparseCore 0:
  206.4 61.8 all-gather.5
  270.4 43.8 all-gather.3

commit v4 on v3

--- a/solution.py
+++ b/solution.py
@@ -102,7 +102,7 @@
                 pltpu.make_async_copy(own[m].at[layer], scratch.at[0], sems.at[0]).start()
         for m, at_k, s, which, lead, row in plan:
             if at_k == k:
-                source = sources[which].at[lead]
+                source = sources[which] if lead is None else sources[which].at[lead]
                 at = pl.multiple_of((spot ^ s) * rows, rows)
                 pltpu.make_async_copy(
                     source.at[pl.ds(row, rows)],
@@ -868,13 +868,15 @@
     own_mlp = (w_up, w_down)
 
     def attn_part(l):
-        left = lax.dynamic_slice(w_qkv, (l, spot * rows, 0, 0), (1, rows, 3, inner)).reshape(rows, 3 * inner)
-        right = lax.dynamic_slice(w_out, (l, 0, spot * rows), (1, inner, rows))[0].T
+        at = spot * rows
+        left = lax.dynamic_slice(w_qkv, (l, at, 0, 0), (1, rows, 3, inner)).reshape(rows, 3 * inner)
+        right = lax.dynamic_slice(w_out, (l, 0, at), (1, inner, rows))[0].T
         return jnp.concatenate([left, right], 1)
 
-    def mlp_part(l):
+    def mlp_part(l, s=0):
+        at = (spot ^ s) * rows
         return jnp.concatenate(
-            [lax.dynamic_slice(w, (l, spot * rows, 0), (1, rows, w.shape[2]))[0] for w in (w_up, w_down)], 0
+            [lax.dynamic_slice(w, (l, at, 0), (1, rows, w.shape[2]))[0] for w in (w_up, w_down)], 0
         )
 
     assert layers == 2
@@ -894,7 +896,15 @@
         return held[1:]
 
     def slices_of(matrices):
-        return Pieces([[[(v, lead + (k,), 0) for v, lead in slices] for k in range(n_t - 1)] for slices in matrices])
+        return Pieces(
+            [
+                [
+                    [(v[k], None, at) if isinstance(v, list) else (v, at + (k,), 0) for v, at in slices]
+                    for k in range(n_t - 1)
+                ]
+                for slices in matrices
+            ]
+        )
 
     def core_swap(v):
         return swap(v, 1, n_dp)
@@ -912,6 +922,14 @@
         ends = [(first, core_swap(first)), (second, core_swap(second))]
         return slices_of(
             [[(v, (m,)) for v in sides] + [(v, ()) for v in ends[m]] for m in range(2)]
+        )
+
+    def two_with_corners(own, x_piece, y_piece, last):
+        own_c, x_c, y_c = core_swap(own), core_swap(x_piece), core_swap(y_piece)
+        last_c = [core_swap(v) for v in last]
+        sides = [own, own_c, x_piece, x_c, y_piece, y_c]
+        return slices_of(
+            [[(v, (m,)) for v in sides] + [(last, m * rows), (last_c, m * rows)] for m in range(2)]
         )
 
     def sides_of(own):
@@ -944,16 +962,16 @@
     mlp_pieces = [two_matrices(own_m, x_m, y_m, first[0])]
     hops_l = passed_on(held_l)
     own_a, own_m = pack(hops_l, 1, 2)
+    held_c = to_neighbours(after(mlp_part(1, 6), hops_l))
     x_a, y_a = sides_of(own_a)
     x_m, y_m = sides_of(own_m)
     second = run_feed_forward(0, after(first[0], own_a), mlp_pieces[0], True, F32)
-    second, ((x_a, y_a),) = gate(second, (x_a, y_a))
+    second, ((x_a, y_a), held_c) = gate(second, (x_a, y_a), held_c)
     attn_pieces.append(one_matrix(own_a, x_a, y_a, True))
+    hops_c = passed_on(held_c)
     third = run_attention(1, second[0], attn_pieces[1], 1_000_000)
-    if SIDES_FIRST:
-        x_m, y_m = after((x_m, y_m), third[0])
-        third, ((x_m, y_m),) = gate(third, (x_m, y_m))
-    mlp_pieces.append(two_matrices(own_m, x_m, y_m, third[0]))
+    third, ((x_m, y_m), hops_c) = gate(third, (x_m, y_m), hops_c)
+    mlp_pieces.append(two_with_corners(own_m, x_m, y_m, hops_c))
     saved = [(stream, *first[1:], first[0], *second[1:]), (second[0], *third[1:], third[0])]
 
     def put_pairs(held):

time: 350 us -> 342 us (0.977)
  waiting for transfers between devices: 99.3 us -> 86.4 us
  starting transfers between devices: 61 us -> 66 us
    ppermute x48 -> x47, waiting for transfers between devices: 60.7 us -> 43.2 us  [swap(): return lax.ppermute(values, 'dp', [(i, i ^ bit) for i in range(size)])]
    ppermute x12 -> x15, starting transfers between devices: 18.4 us -> 25.1 us  [hand_on(): lax.ppermute(part, 'tensor', [(i, (i + step) % n_t) for i in range(n_t)])]
    ppermute x12 -> x15, waiting for transfers between devices: 28.8 us -> 33.3 us  [hand_on(): lax.ppermute(part, 'tensor', [(i, (i + step) % n_t) for i in range(n_t)])]
    unnamed x165 -> x171, local copies, waits for them, and re-layouts: 27.8 us -> 30.8 us
    ppermute x48 -> x47, starting transfers between devices: 31.2 us -> 29.5 us  [swap(): return lax.ppermute(values, 'dp', [(i, i ^ bit) for i in range(size)])]
  transfers between devices with their start and end apart: 76 -> 78, of which waited for: 32 -> 31; matrix products, arithmetic and copies ran while one was open for 11% -> 11% of each run, Pallas kernels for 24% -> 25%
where the time goes in v4:
time: 342 us; the launch traced here: 341 us
  Pallas kernels  106 us (31%)
  waiting for transfers between devices  86.4 us (25%)
  starting transfers between devices  66 us (19%)
  local copies, waits for them, and re-layouts  43.7 us (13%)
  between operations  15 us (4%)
  other arithmetic  13.6 us (4%)
  matrix products  9.69 us (3%)
    ppermute x47, waiting for transfers between devices, swap(): return lax.ppermute(values, 'dp', [(i, i ^ bit) for i in range(size)])  43.2 us
    ppermute x15, waiting for transfers between devices, hand_on(): lax.ppermute(part, 'tensor', [(i, (i + step) % n_t) for i in range(n_t)])  33.3 us
    pallas_call x3, Pallas kernels, attention_backward(): pl.pallas_call(functools.partial(attention_backward_kernel, quarters, las...  31.8 us
    unnamed x171, local copies, waits for them, and re-layouts  30.8 us
    ppermute x47, starting transfers between devices, swap(): return lax.ppermute(values, 'dp', [(i, i ^ bit) for i in range(size)])  29.5 us
    ppermute x15, starting transfers between devices, hand_on(): lax.ppermute(part, 'tensor', [(i, (i + step) % n_t) for i in range(n_t)])  25.1 us
    pallas_call x2, Pallas kernels, attention_forward(): pl.pallas_call(functools.partial(attention_forward_kernel, layer, pieces....  19.2 us
    pallas_call x11, Pallas kernels, call(): small_call(kernel, (1,), [spec for _, spec in operands], [whole(v.shape)...  18.5 us
  transfers between devices with their start and end apart: 78, of which 31 were waited for; matrix products, arithmetic and copies ran while one was open for 11% of the time, Pallas kernels for 25%

profile of v4, /device:TPU:0, one launch (start us, length us, event | category | flops | bytes accessed | tf_op | source)
XLA Modules:
  0.0 340.6 jit_solution(6238931619798242272)
XLA Ops:
  9.9 3.1 collective-permute-start
  13.0 2.1 collective-permute-start.1
  15.8 2.0 select_add_fusion.x
  17.9 1.8 collective-permute-done.refs_0_
  21.0 4.0 %copy.30 = bf16[2,768,3,192]{3,1,2,0:T(8,128)(2,1)} copy(bf16[2,768,3,192]{1,3,2,0:T(8,128)(2,1)} %param.14) | data formatting | bytes 3538944 | tf_op args[4]
  30.6 3.2 collective-permute-start.3
  33.8 6.1 %collective-permute-done.2.refs_0_ = bf16[192,768]{1,0:T(8,128)(2,1)S(1)} collective-permute-done((bf16[192,768]{1,0:T(8,128)(2,1)S(1)}, bf16[192,768]{1,0:T(8,128)(2,1)S(1)}, u32[]{:S(2)}, u32[]{:S(2)}) %collective-permute-start.2) | collective-permute-done | bytes 294944 | tf_op jit(solution)/shard_map/ppermute | solution.py:886
  43.1 2.0 collective-permute-start.7
  45.1 4.9 %collective-permute-done.11.rest_6_ = bf16[1,3,96,768]{3,2,1,0:T(8,128)(2,1)} collective-permute-done((bf16[1,3,96,768]{3,2,1,0:T(8,128)(2,1)}, bf16[1,3,96,768]{3,2,1,0:T(8,128)(2,1)}, u32[]{:S(2)}, u32[]{:S(2)}) %collective-permute-start.11) | collective-permute-done | bytes 442400 | tf_op jit(solution)/shard_map/ppermute | solution.py:596
  50.7 3.2 collective-permute-done.7.refs_1_
  54.4 3.4 %collective-permute-start.14 = (bf16[288,768]{1,0:T(8,128)(2,1)S(1)}, bf16[288,768]{1,0:T(8,128)(2,1)S(1)}, u32[]{:S(2)}, u32[]{:S(2)}) collective-permute-start(bf16[288,768]{1,0:T(8,128)(2,1)S(1)} %pad_maximum_fusion.3), channel_id=1, source_target_pairs={{0,3},{1,0},{2,1},{3,2},{4,7},{5,4},{6,5},{7,6},{8,11},{9,8},{10,9... | collective-permute-start | bytes 1327112 | tf_op jit(solution)/shard_map/ppermute | solution.py:886
  60.7 9.6 %attention_forward.2 = (f32[256,768]{1,0:T(8,128)}, bf16[256,768]{1,0:T(8,128)(2,1)}, bf16[4,256,576]{2,1,0:T(8,128)(2,1)}, f32[256,128]{1,0:T(8,128)}, bf16[4,256,256]{2,1,0:T(8,128)(2,1)}) custom-call(s32[1]{0:T(128)} %bitcast.spot_ref, f32[256,768]{1,0:T(8,128)} %select_add_fusion.x, f32[1,768]{1,0:T(1,128)} %get-tuple-element.469.gain.total_in, ...), custom_call_target="tpu_custom_call" | custom-call | flops 40000000000 | bytes 1000000 | tf_op jit(solution)/shard_map/attention_forward/pallas_call | solution.py:242
  70.3 6.0 %collective-permute-done.14.refs_2_ = bf16[288,768]{1,0:T(8,128)(2,1)S(1)} collective-permute-done((bf16[288,768]{1,0:T(8,128)(2,1)S(1)}, bf16[288,768]{1,0:T(8,128)(2,1)S(1)}, u32[]{:S(2)}, u32[]{:S(2)}) %collective-permute-start.14) | collective-permute-done | bytes 442400 | tf_op jit(solution)/shard_map/ppermute | solution.py:886
  83.4 6.6 %collective-permute-done.15.refs_1_ = bf16[288,768]{1,0:T(8,128)(2,1)S(1)} collective-permute-done((bf16[288,768]{1,0:T(8,128)(2,1)S(1)}, bf16[288,768]{1,0:T(8,128)(2,1)S(1)}, u32[]{:S(2)}, u32[]{:S(2)}) %collective-permute-start.15) | collective-permute-done | bytes 442400 | tf_op jit(solution)/shard_map/ppermute | solution.py:886
  90.5 2.0 collective-permute-done.21.rest_6_.rest_8_
  94.2 2.9 collective-permute-start.28
  100.0 8.0 %mlp_forward.2 = (f32[256,768]{1,0:T(8,128)}, bf16[256,768]{1,0:T(8,128)(2,1)}, f32[4,256,768]{2,1,0:T(8,128)}) custom-call(s32[1]{0:T(128)} %bitcast.spot_ref, f32[256,768]{1,0:T(8,128)} %get-tuple-element.232.x, f32[1,768]{1,0:T(1,128)} %get-tuple-element.470.gain.total_in, f32[1,768]{1,0:T(1,128)} %get-tuple-element.458.bias, ...), custom_call_target="tpu_custom_call" | custom-call | flops 40000000000 | bytes 1000000 | tf_op jit(solution)/shard_map/mlp_forward/pallas_call | solution.py:303
  112.9 9.4 %collective-permute-done.32.rest_6_ = bf16[1,3,96,768]{3,2,1,0:T(8,128)(2,1)S(1)} collective-permute-done((bf16[1,3,96,768]{3,2,1,0:T(8,128)(2,1)S(1)}, bf16[1,3,96,768]{3,2,1,0:T(8,128)(2,1)S(1)}, u32[]{:S(2)}, u32[]{:S(2)}) %collective-permute-start.32) | collective-permute-done | bytes 442400 | tf_op jit(solution)/shard_map/ppermute | solution.py:596
  125.4 9.7 %attention_forward.3 = (f32[256,768]{1,0:T(8,128)}, bf16[256,768]{1,0:T(8,128)(2,1)}, bf16[4,256,576]{2,1,0:T(8,128)(2,1)}, f32[256,128]{1,0:T(8,128)}, bf16[4,256,256]{2,1,0:T(8,128)(2,1)}) custom-call(s32[1]{0:T(128)} %bitcast.spot_ref, f32[256,768]{1,0:T(8,128)} %get-tuple-element.241.x, f32[1,768]{1,0:T(1,128)} %get-tuple-element.468.gain.total_in, ...), custom_call_target="tpu_custom_call" | custom-call | flops 1000000 | bytes 1000000 | tf_op jit(solution)/shard_map/attention_forward/pallas_call | solution.py:242
  135.0 4.8 %collective-permute-done.34.rest_2_ = bf16[2,3,96,768]{3,2,1,0:T(8,128)(2,1)} collective-permute-done((bf16[2,3,96,768]{3,2,1,0:T(8,128)(2,1)S(1)}, bf16[2,3,96,768]{3,2,1,0:T(8,128)(2,1)}, u32[]{:S(2)}, u32[]{:S(2)}) %collective-permute-start.34) | collective-permute-done | bytes 884768 | tf_op jit(solution)/shard_map/ppermute | solution.py:596
  147.0 7.9 %top_backward.1 = (f32[48,768]{1,0:T(8,128)}, f32[1,768]{1,0:T(1,128)}, f32[1,768]{1,0:T(1,128)}, bf16[32,768]{1,0:T(8,128)(2,1)}) custom-call(s32[1]{0:T(128)} %bitcast.spot_ref, f32[48,768]{1,0:T(8,128)} %fusion.22.incoming, f32[256,768]{1,0:T(8,128)} %get-tuple-element.252.x, f32[1,768]{1,0:T(1,128)} %get-tuple-element.471.gain, ...), custom_call_target="tpu_custom_call" | custom-call | flops 40000000000 | bytes 1000000 | tf_op jit(solution)/shard_map/top_backward/pallas_call | solution.py:436
  155.0 13.4 %attention_backward.3 = (f32[256,768]{1,0:T(8,128)}, f32[256,768]{1,0:T(8,128)}, f32[1,768]{1,0:T(1,128)}, f32[1,768]{1,0:T(1,128)}, f32[2,768]{1,0:T(2,128)}, /...) custom-call(s32[1]{0:T(128)} %bitcast.spot_ref, ...), custom_call_target="tpu_custom_call" | custom-call | flops 40000000000 | bytes 1000000 | tf_op jit(solution)/shard_map/attention_backward/pallas_call | solution.py:563
  168.6 7.5 %mlp_forward.3 = bf16[256,768]{1,0:T(8,128)(2,1)} custom-call(s32[1]{0:T(128)} %bitcast.spot_ref, f32[256,768]{1,0:T(8,128)} %get-tuple-element.252.x, f32[1,768]{1,0:T(1,128)} %get-tuple-element.471.gain, f32[1,768]{1,0:T(1,128)} %get-tuple-element.457.bias, bf16[2,768,768]{2,1,0:T(8,128)(2,1)} %rest_0_.1, bf16[2,768,768]{2,1,0:T(8,128)(2,1)} %rest_1_.1, ...), custom_call_target="tpu_custom_call" | custom-call | flops 40000000000 | bytes 1000000 | tf_op jit(solution)/shard_map/mlp_forward/pallas_call | solution.py:303
  176.1 2.3 collective-permute-start.46
  184.4 13.0 %mlp_backward.1 = (f32[256,768]{1,0:T(8,128)}, f32[256,768]{1,0:T(8,128)}, f32[1,768]{1,0:T(1,128)}, f32[1,768]{1,0:T(1,128)}, bf16[4,2,96,768]{3,2,1,0:T(8,128)...) custom-call(s32[1]{0:T(128)} %bitcast.spot_ref, ...), custom_call_target="tpu_custom_call" | custom-call | flops 40000000000 | bytes 1000000 | tf_op jit(solution)/shard_map/mlp_backward/pallas_call | solution.py:384
  198.5 2.0 far_sum.3
  202.9 8.4 %attention_backward.4 = (f32[256,768]{1,0:T(8,128)}, bf16[2,1,96,768]{3,2,1,0:T(8,128)(2,1)}, bf16[2,1,96,768]{3,2,1,0:T(8,128)(2,1)}, bf16[2,1,96,768]{3,2,1,0:...) custom-call(s32[1]{0:T(128)} %bitcast.spot_ref, ...), custom_call_target="tpu_custom_call" | custom-call | flops 40000000000 | bytes 1000000 | tf_op jit(solution)/shard_map/attention_backward/pallas_call | solution.py:563
  211.3 4.9 %collective-permute-done.51 = bf16[256,768]{1,0:T(8,128)(2,1)} collective-permute-done((bf16[256,768]{1,0:T(8,128)(2,1)}, bf16[256,768]{1,0:T(8,128)(2,1)}, u32[]{:S(2)}, u32[]{:S(2)}) %collective-permute-start.51) | collective-permute-done | bytes 393248 | tf_op jit(solution)/shard_map/ppermute | solution.py:886
  218.7 3.4 near_sum.4
  224.3 2.0 own_sum.3
  227.1 2.0 collective-permute-start.56
  229.1 10.0 %attention_backward.5 = (f32[256,768]{1,0:T(8,128)}, bf16[256,768]{1,0:T(8,128)(2,1)}, f32[1,768]{1,0:T(1,128)}, f32[1,768]{1,0:T(1,128)}, f32[2,768]{1,0:T(2,12...) custom-call(s32[1]{0:T(128)} %bitcast.spot_ref, ...), custom_call_target="tpu_custom_call" | custom-call | flops 40000000000 | bytes 1000000 | tf_op jit(solution)/shard_map/attention_backward/pallas_call | solution.py:563
  242.4 11.1 %collective-permute-done.52.refs_2_ = bf16[2,2,2,96,768]{4,3,2,1,0:T(8,128)(2,1)} collective-permute-done((bf16[2,2,2,96,768]{4,3,2,1,0:T(8,128)(2,1)}, bf16[2,2,2,96,768]{4,3,2,1,0:T(8,128)(2,1)}, u32[]{:S(2)}, u32[]{:S(2)}) %collective-permute-start.52) | collective-permute-done | bytes 1179680 | tf_op jit(solution)/shard_map/ppermute | solution.py:596
  255.4 2.8 far_sum.4
  271.1 3.7 %collective-permute-done.61.refs_3_ = bf16[2,2,96,768]{3,2,1,0:T(8,128)(2,1)} collective-permute-done((bf16[2,2,96,768]{3,2,1,0:T(8,128)(2,1)}, bf16[2,2,96,768]{3,2,1,0:T(8,128)(2,1)}, u32[]{:S(2)}, u32[]{:S(2)}) %collective-permute-start.61) | collective-permute-done | bytes 589856 | tf_op jit(solution)/shard_map/ppermute | solution.py:596
  276.1 2.9 own_sum.4
  279.5 4.4 %collective-permute-done.60 = f32[16,768]{1,0:T(8,128)S(1)} collective-permute-done((f32[16,768]{1,0:T(8,128)S(1)}, f32[16,768]{1,0:T(8,128)S(1)}, u32[]{:S(2)}, u32[]{:S(2)}) %collective-permute-start.60) | collective-permute-done | bytes 49184 | tf_op jit(solution)/shard_map/ppermute | solution.py:837
  284.6 2.7 collective-permute-done.64.refs_2_
  290.2 2.5 fusion.34
  292.7 1.9 fusion.7
  294.6 4.2 %fusion.6 = f32[96,768]{1,0:T(8,128)} fusion(f32[512,768]{1,0:T(8,128)} %fusion.7, bf16[512,768]{1,0:T(8,128)(2,1)} %bitcast.97, bf16[2,768,768]{2,1,0:T(8,128)(2,1)} %rest_1_.1, bf16[512,768]{1,0:T(8,128)(2,1)} %bitcast.100, s32[]{:T(128)S(6)} %select_n.84), kind=kOutput, calls=%fused_computation.9 | convolution fusion | flops 683409408 | bytes 3964932 | tf_op jit(solution)/shard_map/dot_general | solution.py:27
  298.8 2.7 fusion.14
  303.3 1.8 own_sum.5
  307.2 2.0 collective-permute-start.74
  309.2 1.8 collective-permute-start.75
  316.8 2.3 collective-permute-done.70.second
  320.6 2.2 collective-permute-start.73
  324.6 3.4 convert_element_type.34
  (360 shorter events, 101.7 us)
Async XLA Ops:
  7.2 283.0 %all-gather.6.cloned.1.call-start = ((), (), s32[]{:S(2)}) async-start(), calls=%async_computation.1 | async-start | bytes 1622016 | tf_op jit(solution)/shard_map/all_gather | solution.py:1000
  13.0 12.1 %collective-permute-start.1 = (bf16[96,768]{1,0:T(8,128)(2,1)S(1)}, bf16[96,768]{1,0:T(8,128)(2,1)S(1)}, u32[]{:S(2)}, u32[]{:S(2)}) collective-permute-start(bf16[96,768]{1,0:T(8,128)(2,1)S(1)} %pad_maximum_fusion.7), channel_id=1, source_target_pairs={{0,3},{1,0},{2,1},{3,2},{4,7},{5,4},{6,5},{7,6},{8,11},{9,8},{10,9... | collective-permute-start | bytes 442376 | tf_op jit(solution)/shard_map/ppermute | solution.py:886
  26.7 14.6 %collective-permute-start.5 = (bf16[1,3,96,768]{3,2,1,0:T(8,128)(2,1)S(1)}, bf16[1,3,96,768]{3,2,1,0:T(8,128)(2,1)}, u32[]{:S(2)}, u32[]{:S(2)}) collective-permute-start(bf16[1,3,96,768]{3,2,1,0:T(8,128)(2,1)S(1)} %pack.3.rest_0_), channel_id=1, source_target_pairs={{0,8},{4,12},{8,0},{12,4},{16,24},{20,28},{24,16},{28,20},{1,9},{5... | collective-permute-start | bytes 1327112 | tf_op jit(solution)/shard_map/ppermute | solution.py:596
  28.5 12.8 %collective-permute-start.6 = (bf16[1,3,96,768]{3,2,1,0:T(8,128)(2,1)S(1)}, bf16[1,3,96,768]{3,2,1,0:T(8,128)(2,1)}, u32[]{:S(2)}, u32[]{:S(2)}) collective-permute-start(bf16[1,3,96,768]{3,2,1,0:T(8,128)(2,1)S(1)} %pack.3.rest_0_), channel_id=1, source_target_pairs={{0,16},{4,20},{8,24},{12,28},{16,0},{20,4},{24,8},{28,12},{1,17},{... | collective-permute-start | bytes 1327112 | tf_op jit(solution)/shard_map/ppermute | solution.py:596
  42.5 11.9 %collective-permute-start.8 = (bf16[1,3,96,768]{3,2,1,0:T(8,128)(2,1)S(1)}, bf16[1,3,96,768]{3,2,1,0:T(8,128)(2,1)S(1)}, u32[]{:S(2)}, u32[]{:S(2)}) collective-permute-start(bf16[1,3,96,768]{3,2,1,0:T(8,128)(2,1)S(1)} %pack.3.rest_0_), channel_id=1, source_target_pairs={{0,4},{4,0},{8,12},{12,8},{16,20},{20,16},{24,28},{28,24},{1,5},{5... | collective-permute-start | bytes 1327112 | tf_op jit(solution)/shard_map/ppermute | solution.py:596
  42.6 15.8 %collective-permute-start.9 = (bf16[1,3,96,768]{3,2,1,0:T(8,128)(2,1)}, bf16[1,3,96,768]{3,2,1,0:T(8,128)(2,1)S(1)}, u32[]{:S(2)}, u32[]{:S(2)}) collective-permute-start(bf16[1,3,96,768]{3,2,1,0:T(8,128)(2,1)} %collective-permute-done.5.rest_2_), channel_id=1, source_target_pairs={{0,4},{4,0},{8,12},{12,8},{16,20},{20,16},{24,28},{28,24},{1,5},{5... | collective-permute-start | bytes 1327112 | tf_op jit(solution)/shard_map/ppermute | solution.py:596
  45.1 12.8 %collective-permute-start.10 = (bf16[1,3,96,768]{3,2,1,0:T(8,128)(2,1)}, bf16[1,3,96,768]{3,2,1,0:T(8,128)(2,1)S(1)}, u32[]{:S(2)}, u32[]{:S(2)}) collective-permute-start(bf16[1,3,96,768]{3,2,1,0:T(8,128)(2,1)} %collective-permute-done.6.rest_4_), channel_id=1, source_target_pairs={{0,4},{4,0},{8,12},{12,8},{16,20},{20,16},{24,28},{28,24},{1,5},{5... | collective-permute-start | bytes 1327112 | tf_op jit(solution)/shard_map/ppermute | solution.py:596
  53.8 16.4 %collective-permute-start.13 = (bf16[288,768]{1,0:T(8,128)(2,1)S(1)}, bf16[288,768]{1,0:T(8,128)(2,1)S(1)}, u32[]{:S(2)}, u32[]{:S(2)}) collective-permute-start(bf16[288,768]{1,0:T(8,128)(2,1)S(1)} %pad_maximum_fusion.3), channel_id=1, source_target_pairs={{0,1},{1,2},{2,3},{3,0},{4,5},{5,6},{6,7},{7,4},{8,9},{9,10},{10,1... | collective-permute-start | bytes 1327112 | tf_op jit(solution)/shard_map/ppermute | solution.py:886
  54.4 21.8 %collective-permute-start.14 = (bf16[288,768]{1,0:T(8,128)(2,1)S(1)}, bf16[288,768]{1,0:T(8,128)(2,1)S(1)}, u32[]{:S(2)}, u32[]{:S(2)}) collective-permute-start(bf16[288,768]{1,0:T(8,128)(2,1)S(1)} %pad_maximum_fusion.3), channel_id=1, source_target_pairs={{0,3},{1,0},{2,1},{3,2},{4,7},{5,4},{6,5},{7,6},{8,11},{9,8},{10,9... | collective-permute-start | bytes 1327112 | tf_op jit(solution)/shard_map/ppermute | solution.py:886
  57.8 20.2 %collective-permute-start.17 = (bf16[2,3,96,768]{3,2,1,0:T(8,128)(2,1)S(1)}, bf16[2,3,96,768]{3,2,1,0:T(8,128)(2,1)S(1)}, u32[]{:S(2)}, u32[]{:S(2)}) collective-permute-start(bf16[2,3,96,768]{3,2,1,0:T(8,128)(2,1)S(1)} %pack.4.rest_0_.rest_2_), channel_id=1, source_target_pairs={{0,8},{4,12},{8,0},{12,4},{16,24},{20,28},{24,16},{28,20},{1,9},{5... | collective-permute-start | bytes 2654216 | tf_op jit(solution)/shard_map/ppermute | solution.py:596
  58.4 20.6 %collective-permute-start.18 = (bf16[2,3,96,768]{3,2,1,0:T(8,128)(2,1)S(1)}, bf16[2,3,96,768]{3,2,1,0:T(8,128)(2,1)}, u32[]{:S(2)}, u32[]{:S(2)}) collective-permute-start(bf16[2,3,96,768]{3,2,1,0:T(8,128)(2,1)S(1)} %pack.4.rest_0_.rest_2_), channel_id=1, source_target_pairs={{0,16},{4,20},{8,24},{12,28},{16,0},{20,4},{24,8},{28,12},{1,17},{... | collective-permute-start | bytes 2654216 | tf_op jit(solution)/shard_map/ppermute | solution.py:596
  59.9 33.4 %collective-permute-start.16 = (bf16[2,3,96,768]{3,2,1,0:T(8,128)(2,1)S(1)}, bf16[2,3,96,768]{3,2,1,0:T(8,128)(2,1)}, u32[]{:S(2)}, u32[]{:S(2)}) collective-permute-start(bf16[2,3,96,768]{3,2,1,0:T(8,128)(2,1)S(1)} %pack.4.rest_0_.rest_2_), channel_id=1, source_target_pairs={{0,4},{4,0},{8,12},{12,8},{16,20},{20,16},{24,28},{28,24},{1,5},{5... | collective-permute-start | bytes 2654216 | tf_op jit(solution)/shard_map/ppermute | solution.py:596
  76.2 13.7 %collective-permute-start.15 = (bf16[288,768]{1,0:T(8,128)(2,1)S(1)}, bf16[288,768]{1,0:T(8,128)(2,1)S(1)}, u32[]{:S(2)}, u32[]{:S(2)}) collective-permute-start(bf16[288,768]{1,0:T(8,128)(2,1)S(1)} %collective-permute-done.13.refs_0_), channel_id=1, source_target_pairs={{0,1},{1,2},{2,3},{3,0},{4,5},{5,6},{6,7},{7,4},{8,9},{9,10},{10,1... | collective-permute-start | bytes 1327112 | tf_op jit(solution)/shard_map/ppermute | solution.py:886
  83.4 14.5 %collective-permute-start.19 = (bf16[2,3,96,768]{3,2,1,0:T(8,128)(2,1)S(1)}, bf16[2,3,96,768]{3,2,1,0:T(8,128)(2,1)S(1)}, u32[]{:S(2)}, u32[]{:S(2)}) collective-permute-start(bf16[2,3,96,768]{3,2,1,0:T(8,128)(2,1)S(1)} %copy-done.63), channel_id=1, source_target_pairs={{0,4},{4,0},{8,12},{12,8},{16,20},{20,16},{24,28},{28,24},{1,5},{5... | collective-permute-start | bytes 2654216 | tf_op jit(solution)/shard_map/ppermute | solution.py:596
  93.3 14.8 %collective-permute-start.27 = (bf16[192,768]{1,0:T(8,128)(2,1)S(1)}, bf16[192,768]{1,0:T(8,128)(2,1)}, u32[]{:S(2)}, u32[]{:S(2)}) collective-permute-start(bf16[192,768]{1,0:T(8,128)(2,1)S(1)} %pad_maximum_fusion.5), channel_id=1, source_target_pairs={{0,1},{1,2},{2,3},{3,0},{4,5},{5,6},{6,7},{7,4},{8,9},{9,10},{10,1... | collective-permute-start | bytes 884744 | tf_op jit(solution)/shard_map/ppermute | solution.py:886
  94.2 14.9 %collective-permute-start.28 = (bf16[192,768]{1,0:T(8,128)(2,1)S(1)}, bf16[192,768]{1,0:T(8,128)(2,1)S(1)}, u32[]{:S(2)}, u32[]{:S(2)}) collective-permute-start(bf16[192,768]{1,0:T(8,128)(2,1)S(1)} %pad_maximum_fusion.5), channel_id=1, source_target_pairs={{0,3},{1,0},{2,1},{3,2},{4,7},{5,4},{6,5},{7,6},{8,11},{9,8},{10,9... | collective-permute-start | bytes 884744 | tf_op jit(solution)/shard_map/ppermute | solution.py:886
  97.1 12.0 %collective-permute-start.25 = (bf16[1,3,96,768]{3,2,1,0:T(8,128)(2,1)S(1)}, bf16[1,3,96,768]{3,2,1,0:T(8,128)(2,1)S(1)}, u32[]{:S(2)}, u32[]{:S(2)}) collective-permute-start(bf16[1,3,96,768]{3,2,1,0:T(8,128)(2,1)S(1)} %get-tuple-element.231.rest_0_), channel_id=1, source_target_pairs={{0,8},{4,12},{8,0},{12,4},{16,24},{20,28},{24,16},{28,20},{1,9},{5... | collective-permute-start | bytes 1327112 | tf_op jit(solution)/shard_map/ppermute | solution.py:596
  97.8 11.3 %collective-permute-start.26 = (bf16[1,3,96,768]{3,2,1,0:T(8,128)(2,1)S(1)}, bf16[1,3,96,768]{3,2,1,0:T(8,128)(2,1)S(1)}, u32[]{:S(2)}, u32[]{:S(2)}) collective-permute-start(bf16[1,3,96,768]{3,2,1,0:T(8,128)(2,1)S(1)} %get-tuple-element.231.rest_0_), channel_id=1, source_target_pairs={{0,16},{4,20},{8,24},{12,28},{16,0},{20,4},{24,8},{28,12},{1,17},{... | collective-permute-start | bytes 1327112 | tf_op jit(solution)/shard_map/ppermute | solution.py:596
  100.0 12.3 %collective-permute-start.29 = (bf16[1,3,96,768]{3,2,1,0:T(8,128)(2,1)S(1)}, bf16[1,3,96,768]{3,2,1,0:T(8,128)(2,1)S(1)}, u32[]{:S(2)}, u32[]{:S(2)}) collective-permute-start(bf16[1,3,96,768]{3,2,1,0:T(8,128)(2,1)S(1)} %get-tuple-element.231.rest_0_), channel_id=1, source_target_pairs={{0,4},{4,0},{8,12},{12,8},{16,20},{20,16},{24,28},{28,24},{1,5},{5... | collective-permute-start | bytes 1327112 | tf_op jit(solution)/shard_map/ppermute | solution.py:596
  109.1 13.2 %collective-permute-start.32 = (bf16[1,3,96,768]{3,2,1,0:T(8,128)(2,1)S(1)}, bf16[1,3,96,768]{3,2,1,0:T(8,128)(2,1)S(1)}, u32[]{:S(2)}, u32[]{:S(2)}) collective-permute-start(bf16[1,3,96,768]{3,2,1,0:T(8,128)(2,1)S(1)} %collective-permute-done.26.rest_4_), channel_id=1, source_target_pairs={{0,8},{4,12},{8,0},{12,4},{16,24},{20,28},{24,16},{28,20},{1,9},{5... | collective-permute-start | bytes 1327112 | tf_op jit(solution)/shard_map/ppermute | solution.py:596
  110.3 29.5 %collective-permute-start.34 = (bf16[2,3,96,768]{3,2,1,0:T(8,128)(2,1)S(1)}, bf16[2,3,96,768]{3,2,1,0:T(8,128)(2,1)}, u32[]{:S(2)}, u32[]{:S(2)}) collective-permute-start(bf16[2,3,96,768]{3,2,1,0:T(8,128)(2,1)S(1)} %get-tuple-element.249.rest_0_), channel_id=1, source_target_pairs={{0,8},{4,12},{8,0},{12,4},{16,24},{20,28},{24,16},{28,20},{1,9},{5... | collective-permute-start | bytes 2654216 | tf_op jit(solution)/shard_map/ppermute | solution.py:596
  111.2 28.6 %collective-permute-start.35 = (bf16[2,3,96,768]{3,2,1,0:T(8,128)(2,1)S(1)}, bf16[2,3,96,768]{3,2,1,0:T(8,128)(2,1)}, u32[]{:S(2)}, u32[]{:S(2)}) collective-permute-start(bf16[2,3,96,768]{3,2,1,0:T(8,128)(2,1)S(1)} %get-tuple-element.249.rest_0_), channel_id=1, source_target_pairs={{0,16},{4,20},{8,24},{12,28},{16,0},{20,4},{24,8},{28,12},{1,17},{... | collective-permute-start | bytes 2654216 | tf_op jit(solution)/shard_map/ppermute | solution.py:596
  122.3 20.1 %collective-permute-start.37 = (bf16[2,3,96,768]{3,2,1,0:T(8,128)(2,1)S(1)}, bf16[2,3,96,768]{3,2,1,0:T(8,128)(2,1)}, u32[]{:S(2)}, u32[]{:S(2)}) collective-permute-start(bf16[2,3,96,768]{3,2,1,0:T(8,128)(2,1)S(1)} %get-tuple-element.249.rest_0_), channel_id=1, source_target_pairs={{0,4},{4,0},{8,12},{12,8},{16,20},{20,16},{24,28},{28,24},{1,5},{5... | collective-permute-start | bytes 2654216 | tf_op jit(solution)/shard_map/ppermute | solution.py:596
  123.7 16.1 %collective-permute-start.36 = (bf16[192,768]{1,0:T(8,128)(2,1)}, bf16[192,768]{1,0:T(8,128)(2,1)S(1)}, u32[]{:S(2)}, u32[]{:S(2)}) collective-permute-start(bf16[192,768]{1,0:T(8,128)(2,1)} %collective-permute-done.27.rest_6_), channel_id=1, source_target_pairs={{0,1},{1,2},{2,3},{3,0},{4,5},{5,6},{6,7},{7,4},{8,9},{9,10},{10,1... | collective-permute-start | bytes 884744 | tf_op jit(solution)/shard_map/ppermute | solution.py:886
  176.1 21.3 %collective-permute-start.46 = (bf16[256,768]{1,0:T(8,128)(2,1)}, bf16[256,768]{1,0:T(8,128)(2,1)}, u32[]{:S(2)}, u32[]{:S(2)}) collective-permute-start(bf16[256,768]{1,0:T(8,128)(2,1)} %mlp_forward.3), channel_id=1, source_target_pairs={{0,1},{1,2},{2,3},{3,0},{4,5},{5,6},{6,7},{7,4},{8,9},{9,10},{10,1... | collective-permute-start | bytes 1179656 | tf_op jit(solution)/shard_map/ppermute | solution.py:886
  178.4 19.7 %collective-permute-start.47 = (bf16[256,768]{1,0:T(8,128)(2,1)}, bf16[256,768]{1,0:T(8,128)(2,1)}, u32[]{:S(2)}, u32[]{:S(2)}) collective-permute-start(bf16[256,768]{1,0:T(8,128)(2,1)} %mlp_forward.3), channel_id=1, source_target_pairs={{0,3},{1,0},{2,1},{3,2},{4,7},{5,4},{6,5},{7,6},{8,11},{9,8},{10,9... | collective-permute-start | bytes 1179656 | tf_op jit(solution)/shard_map/ppermute | solution.py:886
  182.2 15.8 %collective-permute-start.44 = (bf16[2,2,1,96,768]{4,3,2,1,0:T(8,128)(2,1)}, bf16[2,2,1,96,768]{4,3,2,1,0:T(8,128)(2,1)}, u32[]{:S(2)}, u32[]{:S(2)}) collective-permute-start(bf16[2,2,1,96,768]{4,3,2,1,0:T(8,128)(2,1)} %get-tuple-element.269), channel_id=1, source_target_pairs={{0,8},{4,12},{8,0},{12,4},{16,24},{20,28},{24,16},{28,20},{1,9},{5... | collective-permute-start | bytes 1769480 | tf_op jit(solution)/shard_map/ppermute | solution.py:596
  183.4 15.0 %collective-permute-start.45 = (bf16[2,2,1,96,768]{4,3,2,1,0:T(8,128)(2,1)}, bf16[2,2,1,96,768]{4,3,2,1,0:T(8,128)(2,1)}, u32[]{:S(2)}, u32[]{:S(2)}) collective-permute-start(bf16[2,2,1,96,768]{4,3,2,1,0:T(8,128)(2,1)} %get-tuple-element.270), channel_id=1, source_target_pairs={{0,16},{4,20},{8,24},{12,28},{16,0},{20,4},{24,8},{28,12},{1,17},{... | collective-permute-start | bytes 1769480 | tf_op jit(solution)/shard_map/ppermute | solution.py:596
  198.4 17.8 %collective-permute-start.48 = (bf16[4,4,2,96,768]{4,3,2,1,0:T(8,128)(2,1)}, bf16[4,4,2,96,768]{4,3,2,1,0:T(8,128)(2,1)}, u32[]{:S(2)}, u32[]{:S(2)}) collective-permute-start(bf16[4,4,2,96,768]{4,3,2,1,0:T(8,128)(2,1)} %get-tuple-element.299), channel_id=1, source_target_pairs={{0,4},{4,0},{8,12},{12,8},{16,20},{20,16},{24,28},{28,24},{1,5},{5... | collective-permute-start | bytes 14155784 | tf_op jit(solution)/shard_map/ppermute | solution.py:596
  198.4 126.2 %all-gather.4.cloned.1.call-start = ((), (), s32[]{:S(2)}) async-start(), calls=%async_computation | async-start | bytes 1966080 | tf_op jit(solution)/shard_map/all_gather | solution.py:1044
  202.3 13.9 %collective-permute-start.51 = (bf16[256,768]{1,0:T(8,128)(2,1)}, bf16[256,768]{1,0:T(8,128)(2,1)}, u32[]{:S(2)}, u32[]{:S(2)}) collective-permute-start(bf16[256,768]{1,0:T(8,128)(2,1)} %collective-permute-done.46), channel_id=1, source_target_pairs={{0,1},{1,2},{2,3},{3,0},{4,5},{5,6},{6,7},{7,4},{8,9},{9,10},{10,1... | collective-permute-start | bytes 1179656 | tf_op jit(solution)/shard_map/ppermute | solution.py:886
  222.1 31.3 %collective-permute-start.52 = (bf16[2,2,2,96,768]{4,3,2,1,0:T(8,128)(2,1)}, bf16[2,2,2,96,768]{4,3,2,1,0:T(8,128)(2,1)}, u32[]{:S(2)}, u32[]{:S(2)}) collective-permute-start(bf16[2,2,2,96,768]{4,3,2,1,0:T(8,128)(2,1)} %get-tuple-element.319), channel_id=1, source_target_pairs={{0,8},{4,12},{8,0},{12,4},{16,24},{20,28},{24,16},{28,20},{1,9},{5... | collective-permute-start | bytes 3538952 | tf_op jit(solution)/shard_map/ppermute | solution.py:596
  223.3 30.4 %collective-permute-start.53 = (bf16[2,2,2,96,768]{4,3,2,1,0:T(8,128)(2,1)}, bf16[2,2,2,96,768]{4,3,2,1,0:T(8,128)(2,1)}, u32[]{:S(2)}, u32[]{:S(2)}) collective-permute-start(bf16[2,2,2,96,768]{4,3,2,1,0:T(8,128)(2,1)} %get-tuple-element.320), channel_id=1, source_target_pairs={{0,16},{4,20},{8,24},{12,28},{16,0},{20,4},{24,8},{28,12},{1,17},{... | collective-permute-start | bytes 3538952 | tf_op jit(solution)/shard_map/ppermute | solution.py:596
  227.1 12.0 %collective-permute-start.54 = (bf16[1,1,96,768]{3,2,1,0:T(8,128)(2,1)}, bf16[1,1,96,768]{3,2,1,0:T(8,128)(2,1)S(1)}, u32[]{:S(2)}, u32[]{:S(2)}) collective-permute-start(bf16[1,1,96,768]{3,2,1,0:T(8,128)(2,1)} %get-tuple-element.324), channel_id=1, source_target_pairs={{0,3},{1,0},{2,1},{3,2},{4,7},{5,4},{6,5},{7,6},{8,11},{9,8},{10,9... | collective-permute-start | bytes 442376 | tf_op jit(solution)/shard_map/ppermute | solution.py:782
  227.1 14.0 %collective-permute-start.55 = (bf16[1,1,96,768]{3,2,1,0:T(8,128)(2,1)}, bf16[1,1,96,768]{3,2,1,0:T(8,128)(2,1)S(1)}, u32[]{:S(2)}, u32[]{:S(2)}) collective-permute-start(bf16[1,1,96,768]{3,2,1,0:T(8,128)(2,1)} %get-tuple-element.325), channel_id=1, source_target_pairs={{0,2},{1,3},{2,0},{3,1},{4,6},{5,7},{6,4},{7,5},{8,10},{9,11},{10,... | collective-permute-start | bytes 442376 | tf_op jit(solution)/shard_map/ppermute | solution.py:782
  227.1 14.7 %collective-permute-start.56 = (bf16[1,1,96,768]{3,2,1,0:T(8,128)(2,1)}, bf16[1,1,96,768]{3,2,1,0:T(8,128)(2,1)S(1)}, u32[]{:S(2)}, u32[]{:S(2)}) collective-permute-start(bf16[1,1,96,768]{3,2,1,0:T(8,128)(2,1)} %get-tuple-element.326), channel_id=1, source_target_pairs={{0,1},{1,2},{2,3},{3,0},{4,5},{5,6},{6,7},{7,4},{8,9},{9,10},{10,1... | collective-permute-start | bytes 442376 | tf_op jit(solution)/shard_map/ppermute | solution.py:782
  258.2 16.5 %collective-permute-start.61 = (bf16[2,2,96,768]{3,2,1,0:T(8,128)(2,1)}, bf16[2,2,96,768]{3,2,1,0:T(8,128)(2,1)}, u32[]{:S(2)}, u32[]{:S(2)}) collective-permute-start(bf16[2,2,96,768]{3,2,1,0:T(8,128)(2,1)} %get-tuple-element.343), channel_id=1, source_target_pairs={{0,16},{4,20},{8,24},{12,28},{16,0},{20,4},{24,8},{28,12},{1,17},{... | collective-permute-start | bytes 1769480 | tf_op jit(solution)/shard_map/ppermute | solution.py:596
  259.4 16.5 %collective-permute-start.62 = (bf16[2,2,96,768]{3,2,1,0:T(8,128)(2,1)}, bf16[2,2,96,768]{3,2,1,0:T(8,128)(2,1)}, u32[]{:S(2)}, u32[]{:S(2)}) collective-permute-start(bf16[2,2,96,768]{3,2,1,0:T(8,128)(2,1)} %get-tuple-element.344), channel_id=1, source_target_pairs={{0,8},{4,12},{8,0},{12,4},{16,24},{20,28},{24,16},{28,20},{1,9},{5... | collective-permute-start | bytes 1769480 | tf_op jit(solution)/shard_map/ppermute | solution.py:596
  264.6 22.6 %collective-permute-start.64 = (bf16[2,2,1,96,768]{4,3,2,1,0:T(8,128)(2,1)S(1)}, bf16[2,2,1,96,768]{4,3,2,1,0:T(8,128)(2,1)S(1)}, u32[]{:S(2)}, u32[]{:S(2)}) collective-permute-start(bf16[2,2,1,96,768]{4,3,2,1,0:T(8,128)(2,1)S(1)} %get-tuple-element.350), channel_id=1, source_target_pairs={{0,8},{4,12},{8,0},{12,4},{16,24},{20,28},{24,16},{28,20},{1,9},{5... | collective-permute-start | bytes 1769480 | tf_op jit(solution)/shard_map/ppermute | solution.py:596
  265.7 21.6 %collective-permute-start.65 = (bf16[2,2,1,96,768]{4,3,2,1,0:T(8,128)(2,1)S(1)}, bf16[2,2,1,96,768]{4,3,2,1,0:T(8,128)(2,1)S(1)}, u32[]{:S(2)}, u32[]{:S(2)}) collective-permute-start(bf16[2,2,1,96,768]{4,3,2,1,0:T(8,128)(2,1)S(1)} %get-tuple-element.351), channel_id=1, source_target_pairs={{0,16},{4,20},{8,24},{12,28},{16,0},{20,4},{24,8},{28,12},{1,17},{... | collective-permute-start | bytes 1769480 | tf_op jit(solution)/shard_map/ppermute | solution.py:596
  279.0 22.5 %collective-permute-start.68 = (bf16[1,2,96,768]{3,2,1,0:T(8,128)(2,1)}, bf16[1,2,96,768]{3,2,1,0:T(8,128)(2,1)}, u32[]{:S(2)}, u32[]{:S(2)}) collective-permute-start(bf16[1,2,96,768]{3,2,1,0:T(8,128)(2,1)} %get-tuple-element.375), channel_id=1, source_target_pairs={{0,3},{1,0},{2,1},{3,2},{4,7},{5,4},{6,5},{7,6},{8,11},{9,8},{10,9... | collective-permute-start | bytes 884744 | tf_op jit(solution)/shard_map/ppermute | solution.py:782
  288.2 13.3 %collective-permute-start.66 = (bf16[2,1,96,768]{3,2,1,0:T(8,128)(2,1)}, bf16[2,1,96,768]{3,2,1,0:T(8,128)(2,1)}, u32[]{:S(2)}, u32[]{:S(2)}) collective-permute-start(bf16[2,1,96,768]{3,2,1,0:T(8,128)(2,1)} %get-tuple-element.385), channel_id=1, source_target_pairs={{0,16},{4,20},{8,24},{12,28},{16,0},{20,4},{24,8},{28,12},{1,17},{... | collective-permute-start | bytes 884744 | tf_op jit(solution)/shard_map/ppermute | solution.py:596
  289.1 12.4 %collective-permute-start.67 = (bf16[2,1,96,768]{3,2,1,0:T(8,128)(2,1)}, bf16[2,1,96,768]{3,2,1,0:T(8,128)(2,1)}, u32[]{:S(2)}, u32[]{:S(2)}) collective-permute-start(bf16[2,1,96,768]{3,2,1,0:T(8,128)(2,1)} %get-tuple-element.386), channel_id=1, source_target_pairs={{0,8},{4,12},{8,0},{12,4},{16,24},{20,28},{24,16},{28,20},{1,9},{5... | collective-permute-start | bytes 884744 | tf_op jit(solution)/shard_map/ppermute | solution.py:596
  307.1 11.9 %collective-permute-start.70 = (bf16[1,1,96,768]{3,2,1,0:T(8,128)(2,1)}, bf16[1,1,96,768]{3,2,1,0:T(8,128)(2,1)S(1)}, u32[]{:S(2)}, u32[]{:S(2)}) collective-permute-start(bf16[1,1,96,768]{3,2,1,0:T(8,128)(2,1)} %get-tuple-element.396), channel_id=1, source_target_pairs={{0,3},{1,0},{2,1},{3,2},{4,7},{5,4},{6,5},{7,6},{8,11},{9,8},{10,9... | collective-permute-start | bytes 442376 | tf_op jit(solution)/shard_map/ppermute | solution.py:782
  307.2 20.8 %collective-permute-start.74 = (bf16[1,2,96,768]{3,2,1,0:T(8,128)(2,1)}, bf16[1,2,96,768]{3,2,1,0:T(8,128)(2,1)S(1)}, u32[]{:S(2)}, u32[]{:S(2)}) collective-permute-start(bf16[1,2,96,768]{3,2,1,0:T(8,128)(2,1)} %copy-done.27), channel_id=1, source_target_pairs={{0,1},{1,2},{2,3},{3,0},{4,5},{5,6},{6,7},{7,4},{8,9},{9,10},{10,1... | collective-permute-start | bytes 884744 | tf_op jit(solution)/shard_map/ppermute | solution.py:782
  309.2 19.4 %collective-permute-start.75 = (bf16[1,2,96,768]{3,2,1,0:T(8,128)(2,1)}, bf16[1,2,96,768]{3,2,1,0:T(8,128)(2,1)S(1)}, u32[]{:S(2)}, u32[]{:S(2)}) collective-permute-start(bf16[1,2,96,768]{3,2,1,0:T(8,128)(2,1)} %copy-done.30), channel_id=1, source_target_pairs={{0,3},{1,0},{2,1},{3,2},{4,7},{5,4},{6,5},{7,6},{8,11},{9,8},{10,9... | collective-permute-start | bytes 884744 | tf_op jit(solution)/shard_map/ppermute | solution.py:782
  311.0 19.7 %collective-permute-start.72 = (bf16[1,1,96,768]{3,2,1,0:T(8,128)(2,1)}, bf16[1,1,96,768]{3,2,1,0:T(8,128)(2,1)S(1)}, u32[]{:S(2)}, u32[]{:S(2)}) collective-permute-start(bf16[1,1,96,768]{3,2,1,0:T(8,128)(2,1)} %copy-done.39), channel_id=1, source_target_pairs={{0,1},{1,2},{2,3},{3,0},{4,5},{5,6},{6,7},{7,4},{8,9},{9,10},{10,1... | collective-permute-start | bytes 442376 | tf_op jit(solution)/shard_map/ppermute | solution.py:782
  320.6 10.8 %collective-permute-start.73 = (bf16[1,1,96,768]{3,2,1,0:T(8,128)(2,1)S(1)}, bf16[1,1,96,768]{3,2,1,0:T(8,128)(2,1)S(1)}, u32[]{:S(2)}, u32[]{:S(2)}) collective-permute-start(bf16[1,1,96,768]{3,2,1,0:T(8,128)(2,1)S(1)} %relay_sum.3), channel_id=1, source_target_pairs={{0,3},{1,0},{2,1},{3,2},{4,7},{5,4},{6,5},{7,6},{8,11},{9,8},{10,9... | collective-permute-start | bytes 442376 | tf_op jit(solution)/shard_map/ppermute | solution.py:782
  (114 other events, 775.5 us)
Sparse Core Ops, SparseCore 0:
  198.5 61.2 all-gather.5
  262.0 43.6 all-gather.3
